TPU v7x, 32 devices: a whole 2x2x4 slice. The times are simulated.
32 devices in a mesh: group: 2 (over y), tensor: 16 (over z, x, core).
Axes of the slice: x: 2, y: 2, z: 4, core: 2. Of those that a mesh axis runs over, the one named last changes fastest.
Arguments:
- x_coded: bfloat16 [256, 16384], P('group', 'tensor'), parts along dimension 0, may hold values from -1 to 1
- x_scales: bfloat16 [128, 256], P('tensor', 'group'), parts along dimension 1, may hold values from 0.29882812 to 3
- signs: int32 [16384], replicated, may hold values from 0 to 1
- block_order: int32 [32], P('group'), parts along dimension 0, may hold values from 0 to 15, each once
- norm_gain: bfloat16 [16384], replicated, may hold values from 0.099609375 to 1.8984375
- w_query: bfloat16 [16384, 2048], P(None, 'tensor'), may hold values from -0.046875 to 0.046875
- w_key: bfloat16 [16384, 1024], P('tensor'), may hold values from -0.046875 to 0.046875
- w_value: bfloat16 [16384, 1024], P('tensor'), may hold values from -0.046875 to 0.046875
- w_out: bfloat16 [2048, 16384], P('tensor'), may hold values from -0.125 to 0.125
Outputs:
- out_coded: bfloat16 [256, 16384], P('group', 'tensor'), parts along dimension 0
- out_scales: bfloat16 [128, 256], P('tensor', 'group'), parts along dimension 1
There are 2 independent parts, one for each index of `group`. A program takes and returns all parts, laid end to end along the dimension named above; an argument that names none is the same for every part. Nothing has to cross between parts.
Inputs may be any that keep to these rules, and one draw needn't show every extreme that they name: `block_order`: each number 0 to 15 appears once.
All inputs are finite; a program needn't handle non-finite values. Where the computation divides by a largest or mean magnitude, that divisor is 1e-20 or more.
Results may differ from a plain program's by a relative error of at most 0.011.
Values may be sent and summed in bfloat16 or wider, within the bound.
No kernel may reach another device: no remote copies, remote signals or barrier semaphores. Data moves between devices by JAX's collectives and lax.ppermute only.
A program may use at most 128 MiB of HBM per device.

v0:
```python
import functools
import math

import jax
import jax.numpy as jnp
from jax import lax
from jax.experimental import pallas as pl
from jax.experimental.pallas import tpu as pltpu
from jax.sharding import PartitionSpec as P

HD = 128
KVH = 8
BLK = 128
NBLOCK = 16


HIGH = lax.Precision.HIGHEST


def hadamard(width):
    idx = jnp.arange(width)
    parity = jnp.zeros((width, width), jnp.int32)
    bit = 1
    while bit < width:
        parity = parity + idx[:, None] // bit % 2 * (idx[None, :] // bit % 2)
        bit = bit * 2
    return jnp.where(parity % 2 == 0, 1.0, -1.0).astype(jnp.float32) / jnp.sqrt(jnp.float32(width))


def rotate_rows(value, sgn, mat):
    rows = value.shape[0]
    blocks = (value * sgn).reshape(rows, -1, mat.shape[0])
    return jnp.einsum("tnb,bc->tnc", blocks, mat, precision=HIGH).reshape(rows, -1)


def unrotate_rows(value, sgn, mat):
    rows = value.shape[0]
    blocks = value.reshape(rows, -1, mat.shape[0])
    return jnp.einsum("tnb,bc->tnc", blocks, mat, precision=HIGH).reshape(rows, -1) * sgn


def rope(value, positions, heads):
    rows = value.shape[0]
    half = HD // 2
    freqs = 500000.0 ** (-(jnp.arange(half).astype(jnp.float32) * 2.0) / HD)
    angle = positions.astype(jnp.float32)[:, None] * freqs[None, :]
    cosine = jnp.cos(angle)[:, None, :]
    sine = jnp.sin(angle)[:, None, :]
    parts = value.reshape(rows, heads, HD)
    first = parts[:, :, :half]
    second = parts[:, :, half:]
    out = jnp.concatenate([first * cosine - second * sine, second * cosine + first * sine], axis=2)
    return out.reshape(rows, heads * HD)


def encode_pairs(joined, positions):
    width = KVH * HD
    keys = rope(joined[:, :width], positions, KVH)
    return jnp.concatenate([keys, joined[:, width:]], axis=1).astype(jnp.bfloat16)


def attend(query_head, key_head, value_head, allowed):
    score = jnp.einsum(
        "qd,kd->qk", query_head, key_head, preferred_element_type=jnp.float32
    ) / jnp.sqrt(jnp.float32(HD))
    score = jnp.where(allowed, score, -1e30)
    probs = jax.nn.softmax(score, axis=1).astype(jnp.bfloat16)
    return jnp.dot(probs, value_head, preferred_element_type=jnp.float32).astype(jnp.bfloat16)


def general(x_coded, x_scales, signs, block_order, norm_gain, w_query, w_key, w_value, w_out):
    count = lax.axis_size("tensor")
    index = lax.axis_index("tensor")
    mat = hadamard(BLK)
    sgn = (2 * signs - 1).astype(jnp.float32)
    coded_all, scales_all = (
        lax.all_gather(x_coded, "tensor", axis=1, tiled=True),
        lax.all_gather(x_scales, "tensor", axis=0, tiled=True),
    )
    tokens = coded_all.shape[0]
    nblocks = scales_all.shape[0]
    deq = (
        coded_all.astype(jnp.float32).reshape(tokens, nblocks, BLK)
        * scales_all.astype(jnp.float32).T[:, :, None]
    )
    resid = unrotate_rows(deq.reshape(tokens, -1), sgn, mat)
    inv = lax.rsqrt(jnp.mean(resid * resid, axis=1, keepdims=True) + 1e-05)
    normed = (resid * norm_gain.astype(jnp.float32) * inv).astype(jnp.bfloat16)
    rows = jnp.arange(tokens)
    blen = tokens // NBLOCK
    positions = block_order[rows // blen] * blen + rows % blen
    heads_here = w_query.shape[1] // HD
    query = rope(
        jnp.dot(normed, w_query, preferred_element_type=jnp.float32), positions, heads_here
    ).astype(jnp.bfloat16)
    width = w_key.shape[0]
    mine = lax.dynamic_slice_in_dim(normed, index * width, width, 1)
    joined_w = jnp.concatenate([w_key, w_value], axis=1)
    kv_part = jnp.dot(mine, joined_w, preferred_element_type=jnp.float32)
    share = lax.psum_scatter(kv_part, "tensor", scatter_dimension=0, tiled=True)
    share_rows = share.shape[0]
    share_pos = lax.dynamic_slice_in_dim(positions, index * share_rows, share_rows, 0)
    keyval = lax.all_gather(encode_pairs(share, share_pos), "tensor", axis=0, tiled=True)
    allowed = positions[None, :] <= positions[:, None]
    per_kv = heads_here * count // KVH
    head = index * heads_here + 0
    group = head // per_kv
    key_head = lax.dynamic_slice_in_dim(keyval, group * HD, HD, 1)
    value_head = lax.dynamic_slice_in_dim(keyval, KVH * HD + group * HD, HD, 1)
    outputs = attend(query, key_head, value_head, allowed)
    rotated_w = rotate_rows(w_out.astype(jnp.float32), sgn, mat)
    rotated = jnp.dot(outputs.astype(jnp.float32), rotated_w, precision=HIGH)
    blocks = rotated.reshape(tokens, nblocks, BLK)
    scale = (jnp.max(jnp.abs(blocks), axis=2) + 1e-06).astype(jnp.bfloat16)
    coded = (blocks / scale.astype(jnp.float32)[:, :, None]).astype(jnp.bfloat16)
    send_vals = coded.reshape(tokens, count, width)
    send_scale = scale.reshape(tokens, count, nblocks // count)
    got_vals, got_scale = (
        lax.all_to_all(send_vals, "tensor", split_axis=1, concat_axis=1, tiled=True),
        lax.all_to_all(send_scale, "tensor", split_axis=1, concat_axis=1, tiled=True),
    )
    back = (
        got_vals.astype(jnp.float32).reshape(tokens, count, width // BLK, BLK)
        * got_scale.astype(jnp.float32)[:, :, :, None]
    )
    summed = jnp.sum(back, axis=1).reshape(tokens, width)
    sgn_mine = lax.dynamic_slice_in_dim(sgn, index * width, width, 0)
    resid_mine = lax.dynamic_slice_in_dim(resid, index * width, width, 1)
    newres = resid_mine + unrotate_rows(summed, sgn_mine, mat)
    final = rotate_rows(newres, sgn_mine, mat).reshape(tokens, width // BLK, BLK)
    out_scale = (jnp.max(jnp.abs(final), axis=2) + 1e-06).astype(jnp.bfloat16)
    out_coded = (final / out_scale.astype(jnp.float32)[:, :, None]).astype(jnp.bfloat16)
    return (out_coded.reshape(tokens, width), out_scale.T)


def spin(rows, cols):
    i = lax.broadcasted_iota(jnp.int32, (rows, cols), 0)
    j = lax.broadcasted_iota(jnp.int32, (rows, cols), 1)
    v = i & j
    v = v ^ (v >> 4)
    v = v ^ (v >> 2)
    v = v ^ (v >> 1)
    return (1 - 2 * (v & 1)).astype(jnp.float32).astype(jnp.bfloat16)


def dot(a, b):
    return jnp.dot(a, b, preferred_element_type=jnp.float32)


VMEM = pl.BlockSpec(memory_space=pltpu.VMEM)
SMEM = pl.BlockSpec(memory_space=pltpu.SMEM)
HBM = pl.BlockSpec(memory_space=pltpu.HBM)
ANY = pl.BlockSpec(memory_space=pl.ANY)


def call(kernel, outs, args, specs, scratch=(), micros=1):
    many = isinstance(outs, tuple)
    args = [pltpu.with_memory_space_constraint(a, pltpu.HBM) if spec is HBM else a for a, spec in zip(args, specs)]
    return pl.pallas_call(
        kernel,
        out_shape=outs,
        in_specs=specs,
        out_specs=(VMEM,) * len(outs) if many else VMEM,
        scratch_shapes=scratch,
        compiler_params=pltpu.CompilerParams(vmem_limit_bytes=32 * 2**20),
        cost_estimate=pl.CostEstimate(flops=micros * 10**9, bytes_accessed=10**6, transcendentals=0),
    )(*args)


def fetch(pairs, sems):
    copies = [pltpu.make_async_copy(src, dst, sems.at[k]) for k, (src, dst) in enumerate(pairs)]
    for copy in copies:
        copy.start()
    return copies


def unrotate_kernel(
    me, x_hbm, s_hbm, sign_hbm, gain_hbm, u_ref, x, s, sign, gain, held, sems
):
    per = sign.shape[0]
    at = pl.multiple_of(me[0] * per, per)
    copies = fetch(
        ((gain_hbm, gain), (sign_hbm.at[pl.ds(at, per), :], sign), (s_hbm, s), (x_hbm, x)),
        sems,
    )

    had = spin(BLK, BLK)
    copies[0].wait()
    held[...] = gain[...].astype(jnp.float32)
    copies[1].wait()
    sg = held[pl.ds(at, per), :] * ((2 * sign[...] - 1).astype(jnp.float32) / math.sqrt(BLK))
    copies[2].wait()
    scale = s[...].astype(jnp.float32).T
    copies[3].wait()
    for b in range(per):
        cols = slice(b * BLK, (b + 1) * BLK)
        part = dot(x[:, cols], had) * scale[:, b : b + 1]
        u_ref[:, cols] = (part * sg[b : b + 1, :]).astype(jnp.bfloat16)


def token_kernel(*refs):
    refs[-1][...] = jnp.zeros_like(refs[-1])


def keyval_kernel(me, u_ref, wk_hbm, wv_hbm, kv_ref, first, second, sems):
    copies = fetch(((wk_hbm, first), (wv_hbm, second)), sems)
    core, chip = me[0] & 1, me[0] >> 1
    for kind, weights in enumerate((first, second)):
        copies[kind].wait()
        part = dot(u_ref[...], weights[...]).astype(jnp.bfloat16)
        for p in range(KVH):
            kv_ref[(chip ^ p) & 1, 1 - (core ^ kind), p >> 1] = part[:, p * HD : (p + 1) * HD]


def joint(me, w_hbm, x_hbm, rel, into):
    width = into.shape[0]
    at = pl.ds(pl.multiple_of((me[0] ^ rel) * width, width), width)
    return [(w_hbm.at[at, :], into.at[:, pl.ds(0, HD)]), (x_hbm.at[at, :], into.at[:, pl.ds(HD, HD)])]


def products(me, rel, u, weights, held):
    per = u.shape[1] // BLK
    inverse = held[pl.ds(pl.multiple_of((me[0] ^ rel) * per, per), per), :]
    square = 0.0
    for b in range(per):
        r = u[:, b * BLK : (b + 1) * BLK].astype(jnp.float32) * inverse[b : b + 1, :]
        square = square + r * r
    return dot(u, weights), square


def query_kernel(rels, me, token, gain_ref, w_hbm, x_hbm, *refs):
    n = len(rels)
    us, (pay_ref, ws, held, sems) = refs[:n], refs[n:]
    pairs = []
    for k, rel in enumerate(rels):
        pairs += joint(me, w_hbm, x_hbm, rel, ws.at[k])
    copies = fetch(pairs, sems)
    held[...] = 1.0 / gain_ref[...].astype(jnp.float32)
    pay, square = 0.0, 0.0
    for k, rel in enumerate(rels):
        copies[2 * k].wait()
        copies[2 * k + 1].wait()
        part, squares = products(me, rel, us[k][...], ws[k], held)
        pay, square = pay + part, square + squares
    pay_ref[:, : 2 * HD] = pay
    pay_ref[:, 2 * HD :] = square


def more_kernel(rels, ahead, me, done, gain_ref, w_hbm, x_hbm, before_ref, *refs):
    n = len(rels)
    us, (pay_ref, ahead_ref, ws, held, sems) = refs[:n], refs[n:]
    pairs = []
    for k, rel in enumerate(rels):
        pairs += joint(me, w_hbm, x_hbm, rel, ws.at[k])
    for k, rel in enumerate(ahead):
        pairs += joint(me, w_hbm, x_hbm, rel, ahead_ref.at[k])
    copies = fetch(pairs, sems)
    held[...] = 1.0 / gain_ref[...].astype(jnp.float32)
    pay, square = before_ref[:, : 2 * HD], before_ref[:, 2 * HD :]
    for k, rel in enumerate(rels):
        copies[2 * k].wait()
        copies[2 * k + 1].wait()
        part, squares = products(me, rel, us[k][...], ws[k], held)
        pay, square = pay + part, square + squares
    for copy in copies[2 * n :]:
        copy.wait()
    pay_ref[:, : 2 * HD] = pay
    pay_ref[:, 2 * HD :] = square


def last_kernel(rels, me, done, gain_ref, w_ref, before_ref, *refs):
    us, (pay_ref, held) = refs[:-2], refs[-2:]
    held[...] = 1.0 / gain_ref[...].astype(jnp.float32)
    pay, square = before_ref[:, : 2 * HD], before_ref[:, 2 * HD :]
    for k, rel in enumerate(rels):
        part, squares = products(me, rel, us[k][...], w_ref[k], held)
        pay, square = pay + part, square + squares
    pay_ref[:, : 2 * HD] = pay
    pay_ref[:, 2 * HD :] = square


def turn(value, cosine, sine):
    half = HD // 2
    swapped = jnp.concatenate([value[:, half:], value[:, :half]], axis=1)
    return (value * cosine + swapped * sine).astype(jnp.bfloat16)


def columns(me, rel, width):
    return pl.ds(pl.multiple_of((me[0] ^ rel) * width, width), width)


def attend_kernel(total, rels, me, pay_ref, got_ref, kv_ref, kvx_ref, cos_ref, sin_ref, row_ref, col_ref, w_hbm, x_hbm, *refs):
    att_ref, outs, (ws, xs, sems) = refs[0], refs[1:-3], refs[-3:]
    width = ws.shape[2]
    copies = fetch(
        [(src.at[:, columns(me, rel, width)], dst.at[k]) for k, rel in enumerate(rels) for src, dst in ((w_hbm, ws), (x_hbm, xs))],
        sems,
    )
    square = jnp.sum(pay_ref[:, 2 * HD :] + got_ref[:, 2 * HD :], axis=1, keepdims=True)
    inv = lax.rsqrt(square / total + 1e-05)
    cosine, sine = cos_ref[...], sin_ref[...]
    core = me[0] & 1
    mine, theirs = kv_ref[...].astype(jnp.float32), kvx_ref[...].astype(jnp.float32)
    key = turn(jnp.where(core == 0, mine, theirs) * inv, cosine, sine)
    value = (jnp.where(core == 0, theirs, mine) * inv).astype(jnp.bfloat16)
    allowed = row_ref[...] <= col_ref[...]
    heads = []
    for at in range(2):
        query = pay_ref[:, at * HD : (at + 1) * HD] + got_ref[:, (1 - at) * HD : (2 - at) * HD]
        query = turn(query * inv, cosine, sine)
        score = lax.dot_general(query, key, (((1,), (1,)), ((), ())), preferred_element_type=jnp.float32)
        score = jnp.where(allowed, score / math.sqrt(HD), -1e30)
        weight = jnp.exp(score - jnp.max(score, axis=1, keepdims=True))
        probs = (weight / jnp.sum(weight, axis=1, keepdims=True)).astype(jnp.bfloat16)
        head = dot(probs, value).astype(jnp.bfloat16)
        att_ref[:, at * HD : (at + 1) * HD] = head
        heads.append(head)
    for k, out in enumerate(outs):
        copies[2 * k].wait()
        copies[2 * k + 1].wait()
        out[...] = (dot(heads[0], ws[k]) + dot(heads[1], xs[k])).astype(out.dtype)


def term_kernel(rels, added, me, done, att_ref, w_hbm, x_hbm, *refs):
    adds, outs, (ws, xs, sems) = refs[:added], refs[added:-3], refs[-3:]
    width = ws.shape[2]
    copies = fetch(
        [(src.at[:, columns(me, rel, width)], dst.at[k]) for k, rel in enumerate(rels) for src, dst in ((w_hbm, ws), (x_hbm, xs))],
        sems,
    )
    for k, out in enumerate(outs):
        copies[2 * k].wait()
        copies[2 * k + 1].wait()
        term = dot(att_ref[:, :HD], ws[k]) + dot(att_ref[:, HD:], xs[k])
        if k < added:
            term = term + adds[k][...].astype(jnp.float32)
        out[...] = term.astype(out.dtype)


def final_kernel(n, me, done, x_ref, s_ref, sign_ref, *refs):
    had = spin(BLK, BLK)
    scale = s_ref[...].astype(jnp.float32).T
    per = s_ref.shape[0]
    sign = (2 * sign_ref[pl.ds(pl.multiple_of(me[0] * per, per), per), :] - 1).astype(jnp.float32) / math.sqrt(BLK)
    parts, (coded_ref, scales_ref) = refs[:n], refs[n:]
    tops = []
    for b in range(per):
        at = slice(b * BLK, (b + 1) * BLK)
        part = parts[0][:, at].astype(jnp.float32)
        for ref in parts[1:]:
            part = part + ref[:, at].astype(jnp.float32)
        part = part * sign[b : b + 1, :]
        high = part.astype(jnp.bfloat16)
        part = part - high.astype(jnp.float32)
        mid = part.astype(jnp.bfloat16)
        low = (part - mid.astype(jnp.float32)).astype(jnp.bfloat16)
        new = dot(high, had) + (dot(mid, had) + dot(low, had))
        new = new + x_ref[:, at].astype(jnp.float32) * scale[:, b : b + 1]
        top = (jnp.max(jnp.abs(new), axis=1, keepdims=True) + 1e-06).astype(jnp.bfloat16).astype(jnp.float32)
        coded_ref[:, at] = (new / top).astype(jnp.bfloat16)
        tops.append(top)
    scales_ref[...] = jnp.concatenate(tops, axis=1).T.astype(jnp.bfloat16)


def swap(value, rel):
    count = lax.axis_size("tensor")
    return lax.ppermute(value, "tensor", [(i, i ^ rel) for i in range(count)])


CORE, ACROSS, NEAR, FAR = 1, 2, 4, 8


def paired(x_coded, x_scales, signs, block_order, norm_gain, w_query, w_key, w_value, w_out):
    count = lax.axis_size("tensor")
    index = lax.axis_index("tensor")
    me = jnp.reshape(index, (1,)).astype(jnp.int32)
    tokens, width = x_coded.shape
    bf16, f32 = jnp.bfloat16, jnp.float32
    block = jax.ShapeDtypeStruct((tokens, width), bf16)
    wide = jax.ShapeDtypeStruct((tokens, width), f32)
    dma = pltpu.SemaphoreType.DMA
    together = lax.optimization_barrier
    sign2 = signs.reshape(-1, BLK)
    gain2 = norm_gain.reshape(-1, BLK)
    u = call(
        unrotate_kernel,
        block,
        (me, x_coded, x_scales, sign2, gain2),
        [SMEM] + [HBM] * 4,
        [
            pltpu.VMEM(x_coded.shape, bf16),
            pltpu.VMEM(x_scales.shape, bf16),
            pltpu.VMEM((width // BLK, BLK), jnp.int32),
            pltpu.VMEM(gain2.shape, bf16),
            pltpu.VMEM(gain2.shape, f32),
            dma((4,)),
        ],
    )
    wq_other = swap(w_query, CORE)
    chunk = {0: u, FAR: swap(u, FAR)}
    kv = call(
        keyval_kernel,
        jax.ShapeDtypeStruct((2, 2, KVH // 2, tokens, HD), bf16),
        (me, u, w_key, w_value),
        [SMEM, VMEM, HBM, HBM],
        [pltpu.VMEM(w_key.shape, bf16), pltpu.VMEM(w_key.shape, bf16), dma((2,))],
        micros=20,
    )

    def plus(*parts):
        return sum(p.astype(f32) for p in parts).astype(bf16)

    def after(*arrays):
        return call(token_kernel, jax.ShapeDtypeStruct((8, BLK), f32), arrays, [ANY] * len(arrays), micros=3)

    chunk[ACROSS] = swap(u, ACROSS)
    chunk[NEAR] = swap(u, NEAR)
    kvx = swap(kv[1], ACROSS)
    done = after(chunk[8], chunk[2], chunk[4])
    done, chunk[8], chunk[2], chunk[4], kvx, wq_other = together((done, chunk[8], chunk[2], chunk[4], kvx, wq_other))
    kv = plus(kv[0], kvx)
    chunk[12] = swap(chunk[8], NEAR)
    chunk[10] = swap(chunk[8], ACROSS)

    partial = jax.ShapeDtypeStruct((tokens, 3 * HD), f32)

    early, more, late = (0, 2, 4), (8, 10, 12), (6, 14)
    pay = call(
        functools.partial(query_kernel, early),
        partial,
        (me, done, gain2, w_query, wq_other) + tuple(chunk[r] for r in early),
        [SMEM, ANY, VMEM, HBM, HBM] + [VMEM] * len(early),
        [
            pltpu.VMEM((len(early), width, 2 * HD), bf16),
            pltpu.VMEM(gain2.shape, f32),
            dma((2 * len(early),)),
        ],
        micros=3,
    )
    kv = plus(kv[1], swap(kv[0], CORE))
    kv, w_out_now = together((kv, w_out))
    wo_other = swap(w_out_now, CORE)
    kv, pay = together((kv, pay))
    alike = [[4 * z + low for z in range(count // 4)] for low in range(4)]
    kv = lax.all_to_all(kv, "tensor", 0, 0, axis_index_groups=alike, tiled=True)
    done = after(chunk[12], chunk[10])
    done, chunk[2], chunk[12], chunk[10], pay = together((done, chunk[2], chunk[12], chunk[10], pay))
    chunk[14] = swap(chunk[12], ACROSS)
    chunk[6] = swap(chunk[2], NEAR)
    pay, ahead = call(
        functools.partial(more_kernel, more, late),
        (partial, jax.ShapeDtypeStruct((len(late), width, 2 * HD), bf16)),
        (me, done, gain2, w_query, wq_other, pay) + tuple(chunk[r] for r in more),
        [SMEM, ANY, VMEM, HBM, HBM, VMEM] + [VMEM] * len(more),
        [
            pltpu.VMEM((len(more), width, 2 * HD), bf16),
            pltpu.VMEM(gain2.shape, f32),
            dma((2 * len(more + late),)),
        ],
        micros=3,
    )
    kv = jnp.sum(kv.astype(f32), axis=0).astype(bf16)
    kv_other = swap(kv, CORE)
    pay = call(
        functools.partial(last_kernel, late),
        partial,
        (me, after(chunk[14], chunk[6]), gain2, ahead, pay) + tuple(chunk[r] for r in late),
        [SMEM, ANY] + [VMEM] * (3 + len(late)),
        [pltpu.VMEM(gain2.shape, f32)],
    )
    got = swap(pay, CORE)

    blen = tokens // NBLOCK
    positions = (block_order[:, None] * blen + jnp.arange(blen)[None, :]).reshape(-1)
    half = HD // 2
    freqs = 500000.0 ** (-(jnp.arange(half).astype(f32) * 2.0) / HD)
    angle = positions.astype(f32)[:, None] * freqs[None, :]
    cosine, sine = jnp.cos(angle), jnp.sin(angle)
    cosine = jnp.concatenate([cosine, cosine], axis=1)
    sine = jnp.concatenate([-sine, sine], axis=1)

    def buffers(n):
        return [pltpu.VMEM((n, HD, width), bf16), pltpu.VMEM((n, HD, width), bf16), dma((2 * n,))]

    args = (me, pay, got, kv, kv_other, cosine, sine, positions[None, :], positions[:, None], w_out, wo_other)
    att, t14, t6 = call(
        functools.partial(attend_kernel, count * width, (14, 6)),
        (jax.ShapeDtypeStruct((tokens, 2 * HD), bf16), block, block),
        args,
        [SMEM] + [VMEM] * 8 + [HBM] * 2,
        buffers(2),
    )

    a14 = swap(t14, ACROSS)
    n6 = swap(t6, NEAR)

    def terms(rels, kinds, done, adds=()):
        return call(
            functools.partial(term_kernel, rels, len(adds)),
            kinds,
            (me, done, att, w_out, wo_other) + adds,
            [SMEM, ANY, VMEM, HBM, HBM] + [VMEM] * len(adds),
            buffers(len(rels)),
            micros=20,
        )

    t10, t4, t12, t8, t0 = terms((10, 4, 12, 8, 0), (block, block, wide, wide, wide), me)
    done, a14, n6, t10 = together((after(a14), a14, n6, t10))
    n12 = swap(plus(t12, a14), NEAR)
    a10 = swap(t10, ACROSS)
    n12, a10, n6, t4 = together((n12, a10, n6, t4))
    n8 = swap(plus(t8, a10, n12), FAR)
    n4 = swap(t4, NEAR)
    (t2,) = terms((2,), (block,), done, (n6,))
    a2 = swap(t2, ACROSS)
    parts = (t0, a2, n4, n8)
    return call(
        functools.partial(final_kernel, len(parts)),
        (block, jax.ShapeDtypeStruct(x_scales.shape, bf16)),
        (me, after(n8), x_coded, x_scales, sign2) + parts,
        [SMEM, ANY] + [VMEM] * (3 + len(parts)),
    )


def per_device(*args):
    if lax.axis_size("tensor") == 16:
        return paired(*args)
    return general(*args)


def solution(mesh):
    in_specs = (
        P("group", "tensor"),
        P("tensor", "group"),
        P(),
        P("group"),
        P(),
        P(None, "tensor"),
        P("tensor", None),
        P("tensor", None),
        P("tensor", None),
    )
    out_specs = (P("group", "tensor"), P("tensor", "group"))
    return jax.shard_map(
        per_device, mesh=mesh, in_specs=in_specs, out_specs=out_specs, check_vma=False
    )
```

profile of v0, /device:TPU:0, one launch (start us, length us, event | category | flops | bytes accessed | tf_op | source)
XLA Modules:
  0.0 79.6 jit_solution(4619841187051041507)
XLA Ops:
  0.6 0.5 collective-permute-start.4
  1.1 1.3 %shard_map.104.u_ref.refs_0_ = bf16[128,1024]{1,0:T(8,128)(2,1)S(1)} custom-call(s32[1]{0:T(128)} %bitcast.me.done, bf16[128,1024]{1,0:T(8,128)(2,1)} %x_ref.1, bf16[8,128]{1,0:T(8,128)(2,1)} %s_ref.1, s32[128,128]{1,0:T(8,128)} %bitcast.17, bf16[128,128]{1,0:T(8,128)(2,1)} %bitcast.19), custom_call_target="tpu_custom_call" | custom-call | flops 1000000000 | bytes 1000000 | tf_op jit(solution)/shard_map/pallas_call | solution.py:159
  2.4 2.7 %collective-permute-start.2 = (bf16[128,1024]{1,0:T(8,128)(2,1)S(1)}, bf16[128,1024]{1,0:T(8,128)(2,1)S(1)}, u32[]{:S(2)}, u32[]{:S(2)}) collective-permute-start(bf16[128,1024]{1,0:T(8,128)(2,1)S(1)} %shard_map.104.u_ref.refs_0_), channel_id=1, source_target_pairs={{0,4},{1,5},{2,6},{3,7},{4,0},{5,1},{6,2},{7,3},{8,12},{9,13},{10,... | collective-permute-start | bytes 786440 | tf_op jit(solution)/shard_map/ppermute | solution.py:367
  5.1 1.5 %collective-permute-start.1 = (bf16[128,1024]{1,0:T(8,128)(2,1)S(1)}, bf16[128,1024]{1,0:T(8,128)(2,1)S(1)}, u32[]{:S(2)}, u32[]{:S(2)}) collective-permute-start(bf16[128,1024]{1,0:T(8,128)(2,1)S(1)} %shard_map.104.u_ref.refs_0_), channel_id=1, source_target_pairs={{0,2},{1,3},{2,0},{3,1},{4,6},{5,7},{6,4},{7,5},{8,10},{9,11},{10,... | collective-permute-start | bytes 786440 | tf_op jit(solution)/shard_map/ppermute | solution.py:367
  6.6 2.6 %collective-permute-start = (bf16[128,1024]{1,0:T(8,128)(2,1)S(1)}, bf16[128,1024]{1,0:T(8,128)(2,1)S(1)}, u32[]{:S(2)}, u32[]{:S(2)}) collective-permute-start(bf16[128,1024]{1,0:T(8,128)(2,1)S(1)} %shard_map.104.u_ref.refs_0_), channel_id=1, source_target_pairs={{0,8},{1,9},{2,10},{3,11},{4,12},{5,13},{6,14},{7,15},{8,0},{9,1},... | collective-permute-start | bytes 786440 | tf_op jit(solution)/shard_map/ppermute | solution.py:367
  9.2 2.7 %shard_map.106 = bf16[2,2,4,128,128]{4,3,2,1,0:T(8,128)(2,1)S(1)} custom-call(s32[1]{0:T(128)} %bitcast.me.done, bf16[128,1024]{1,0:T(8,128)(2,1)S(1)} %shard_map.104.u_ref.refs_0_, bf16[1024,1024]{1,0:T(8,128)(2,1)} %wk_hbm.1, bf16[1024,1024]{1,0:T(8,128)(2,1)} %wv_hbm.1), custom_call_target="tpu_custom_call" | custom-call | flops 20000000000 | bytes 1000000 | tf_op jit(solution)/shard_map/pallas_call | solution.py:159
  11.9 0.0 copy-start.4
  11.9 0.0 copy-start.2
  11.9 0.6 collective-permute-start.3
  12.5 3.8 %collective-permute-done.2.refs_2_ = bf16[128,1024]{1,0:T(8,128)(2,1)S(1)} collective-permute-done((bf16[128,1024]{1,0:T(8,128)(2,1)S(1)}, bf16[128,1024]{1,0:T(8,128)(2,1)S(1)}, u32[]{:S(2)}, u32[]{:S(2)}) %collective-permute-start.2) | collective-permute-done | bytes 262176 | tf_op jit(solution)/shard_map/ppermute | solution.py:367
  16.3 0.0 collective-permute-done.1.refs_1_
  16.3 4.9 %collective-permute-done.refs_0_ = bf16[128,1024]{1,0:T(8,128)(2,1)S(1)} collective-permute-done((bf16[128,1024]{1,0:T(8,128)(2,1)S(1)}, bf16[128,1024]{1,0:T(8,128)(2,1)S(1)}, u32[]{:S(2)}, u32[]{:S(2)}) %collective-permute-start) | collective-permute-done | bytes 262176 | tf_op jit(solution)/shard_map/ppermute | solution.py:367
  21.3 0.0 collective-permute-done.3
  21.3 0.0 collective-permute-done.4.x_hbm
  21.3 0.1 fusion
  21.4 0.1 collective-permute-start.7
  21.5 1.3 %collective-permute-done.7 = bf16[4,128,128]{2,1,0:T(8,128)(2,1)S(1)} collective-permute-done((bf16[4,128,128]{2,1,0:T(8,128)(2,1)S(1)}, bf16[4,128,128]{2,1,0:T(8,128)(2,1)S(1)}, u32[]{:S(2)}, u32[]{:S(2)}) %collective-permute-start.7) | collective-permute-done | bytes 131104 | tf_op jit(solution)/shard_map/ppermute | solution.py:367
  22.8 0.7 fusion.1
  23.5 0.1 collective-permute-start.12
  23.7 0.1 iota_add_fusion
  23.7 0.1 convert_element_type.67
  23.8 0.6 collective-permute-start.6
  24.5 0.2 collective-permute-start.5
  24.6 1.9 %shard_map.108.before_ref = f32[128,384]{1,0:T(8,128)S(1)} custom-call(s32[1]{0:T(128)} %bitcast.me.done, f32[8,128]{1,0:T(8,128)S(1)} %shard_map.105.token, bf16[128,128]{1,0:T(8,128)(2,1)S(1)} %bitcast.20, bf16[16384,128]{1,0:T(8,128)(2,1)} %w_hbm.6, bf16[16384,128]{1,0:T(8,128)(2,1)} %collective-permute-done.4.x_hbm, ...), custom_call_target="tpu_custom_call" | custom-call | flops 3000000000 | bytes 1000000 | tf_op jit(solution)/shard_map/pallas_call | solution.py:159
  26.5 4.1 %all-to-all-start = ((bf16[4,128,128]{2,1,0:T(8,128)(2,1)}), bf16[4,128,128]{2,1,0:T(8,128)(2,1)S(1)}, u32[]{:S(2)}, u32[]{:S(2)}) async-start(bf16[4,128,128]{2,1,0:T(8,128)(2,1)} %fusion.1), calls=%async_computation | async-start | bytes 262144 | tf_op jit(solution)/shard_map/all_to_all | solution.py:445
  30.7 1.8 %collective-permute-done.6.refs_1_ = bf16[128,1024]{1,0:T(8,128)(2,1)S(1)} collective-permute-done((bf16[128,1024]{1,0:T(8,128)(2,1)S(1)}, bf16[128,1024]{1,0:T(8,128)(2,1)S(1)}, u32[]{:S(2)}, u32[]{:S(2)}) %collective-permute-start.6) | collective-permute-done | bytes 262176 | tf_op jit(solution)/shard_map/ppermute | solution.py:367
  32.5 0.3 collective-permute-done.5.refs_0_.refs_2_
  32.7 0.3 collective-permute-start.9
  33.0 1.5 %collective-permute-start.8 = (bf16[128,1024]{1,0:T(8,128)(2,1)S(1)}, bf16[128,1024]{1,0:T(8,128)(2,1)S(1)}, u32[]{:S(2)}, u32[]{:S(2)}) collective-permute-start(bf16[128,1024]{1,0:T(8,128)(2,1)S(1)} %collective-permute-done.5.refs_0_.refs_2_), channel_id=1, source_target_pairs={{0,2},{1,3},{2,0},{3,1},{4,6},{5,7},{6,4},{7,5},{8,10},{9,11},{10,... | collective-permute-start | bytes 786440 | tf_op jit(solution)/shard_map/ppermute | solution.py:367
  34.5 1.8 %shard_map.110 = (f32[128,384]{1,0:T(8,128)S(1)}, bf16[2,1024,256]{2,1,0:T(8,128)(2,1)S(1)}) custom-call(s32[1]{0:T(128)} %bitcast.me.done, f32[8,128]{1,0:T(8,128)S(1)} %shard_map.107.done, bf16[128,128]{1,0:T(8,128)(2,1)S(1)} %bitcast.21, bf16[16384,128]{1,0:T(8,128)(2,1)} %w_hbm.6, bf16[16384,128]{1,0:T(8,128)(2,1)} %collective-permute-done.4.x_hbm, ...), custom_call_target="tpu_custom_call" | custom-call | flops 3000000000 | bytes 1000000 | tf_op jit(solution)/shard_map/pallas_call | solution.py:159
  36.3 5.3 %collective-permute-done.9.refs_1_.refs_0_ = bf16[128,1024]{1,0:T(8,128)(2,1)S(1)} collective-permute-done((bf16[128,1024]{1,0:T(8,128)(2,1)S(1)}, bf16[128,1024]{1,0:T(8,128)(2,1)S(1)}, u32[]{:S(2)}, u32[]{:S(2)}) %collective-permute-start.9) | collective-permute-done | bytes 262176 | tf_op jit(solution)/shard_map/ppermute | solution.py:367
  41.6 0.0 collective-permute-done.8.refs_0_.refs_1_
  41.6 0.3 shard_map.111.pay_ref
  42.0 0.1 collective-permute-start.10
  42.0 0.3 fusion.2
  42.3 0.0 all-to-all-done
  42.4 0.6 collective-permute-start.11
  42.9 0.1 pad_maximum_fusion
  43.1 0.1 add.58.row_ref
  43.1 0.1 add.63.col_ref
  43.2 0.6 collective-permute-done.11.kvx_ref
  43.8 0.0 collective-permute-done.12.x_hbm
  43.8 2.2 %shard_map.112 = (bf16[128,256]{1,0:T(8,128)(2,1)S(1)}, bf16[128,1024]{1,0:T(8,128)(2,1)S(1)}, bf16[128,1024]{1,0:T(8,128)(2,1)S(1)}) custom-call(s32[1]{0:T(128)} %bitcast.me.done, f32[128,384]{1,0:T(8,128)S(1)} %shard_map.111.pay_ref, f32[128,384]{1,0:T(8,128)S(1)} %collective-permute-done.10.got_ref, bf16[128,128]{1,0:T(8,128)(2,1)S(1)} %reduce_sum.12.kv_ref, ...), custom_call_target="tpu_custom_call" | custom-call | flops 1000000000 | bytes 1000000 | tf_op jit(solution)/shard_map/pallas_call | solution.py:159
  46.0 1.6 %collective-permute-start.13 = (bf16[128,1024]{1,0:T(8,128)(2,1)S(1)}, bf16[128,1024]{1,0:T(8,128)(2,1)S(1)}, u32[]{:S(2)}, u32[]{:S(2)}) collective-permute-start(bf16[128,1024]{1,0:T(8,128)(2,1)S(1)} %get-tuple-element.55), channel_id=1, source_target_pairs={{0,2},{1,3},{2,0},{3,1},{4,6},{5,7},{6,4},{7,5},{8,10},{9,11},{10,... | collective-permute-start | bytes 786440 | tf_op jit(solution)/shard_map/ppermute | solution.py:367
  47.6 0.3 collective-permute-start.14
  47.9 2.6 %shard_map.113 = (bf16[128,1024]{1,0:T(8,128)(2,1)S(1)}, bf16[128,1024]{1,0:T(8,128)(2,1)S(1)}, f32[128,1024]{1,0:T(8,128)S(1)}, f32[128,1024]{1,0:T(8,128)S(1)}, f32[128,1024]{1,0:T(8,128)S(1)}) custom-call(s32[1]{0:T(128)} %bitcast.me.done, s32[1]{0:T(128)} %bitcast.me.done, bf16[128,256]{1,0:T(8,128)(2,1)S(1)} %get-tuple-element.52.att_ref, ...), custom_call_target="tpu_custom_call" | custom-call | flops 20000000000 | bytes 1000000 | tf_op jit(solution)/shard_map/pallas_call | solution.py:159
  50.4 4.2 %collective-permute-done.13.refs_0_ = bf16[128,1024]{1,0:T(8,128)(2,1)S(1)} collective-permute-done((bf16[128,1024]{1,0:T(8,128)(2,1)S(1)}, bf16[128,1024]{1,0:T(8,128)(2,1)S(1)}, u32[]{:S(2)}, u32[]{:S(2)}) %collective-permute-start.13) | collective-permute-done | bytes 262176 | tf_op jit(solution)/shard_map/ppermute | solution.py:367
  54.6 1.2 %collective-permute-done.14.refs_0_ = bf16[128,1024]{1,0:T(8,128)(2,1)S(1)} collective-permute-done((bf16[128,1024]{1,0:T(8,128)(2,1)S(1)}, bf16[128,1024]{1,0:T(8,128)(2,1)S(1)}, u32[]{:S(2)}, u32[]{:S(2)}) %collective-permute-start.14) | collective-permute-done | bytes 262176 | tf_op jit(solution)/shard_map/ppermute | solution.py:367
  55.8 0.1 add_convert_fusion.1
  55.9 0.4 collective-permute-start.15
  56.3 0.6 collective-permute-start.16
  56.9 6.5 %collective-permute-done.15 = bf16[128,1024]{1,0:T(8,128)(2,1)S(1)} collective-permute-done((bf16[128,1024]{1,0:T(8,128)(2,1)S(1)}, bf16[128,1024]{1,0:T(8,128)(2,1)S(1)}, u32[]{:S(2)}, u32[]{:S(2)}) %collective-permute-start.15) | collective-permute-done | bytes 262176 | tf_op jit(solution)/shard_map/ppermute | solution.py:367
  63.4 0.1 collective-permute-done.16
  63.5 0.1 add_convert_fusion
  63.6 2.1 %collective-permute-start.17 = (bf16[128,1024]{1,0:T(8,128)(2,1)S(1)}, bf16[128,1024]{1,0:T(8,128)(2,1)S(1)}, u32[]{:S(2)}, u32[]{:S(2)}) collective-permute-start(bf16[128,1024]{1,0:T(8,128)(2,1)S(1)} %add_convert_fusion), channel_id=1, source_target_pairs={{0,8},{1,9},{2,10},{3,11},{4,12},{5,13},{6,14},{7,15},{8,0},{9,1},... | collective-permute-start | bytes 786440 | tf_op jit(solution)/shard_map/ppermute | solution.py:367
  65.7 1.3 %shard_map.116 = bf16[128,1024]{1,0:T(8,128)(2,1)S(1)} custom-call(s32[1]{0:T(128)} %bitcast.me.done, f32[8,128]{1,0:T(8,128)S(1)} %shard_map.114.done, bf16[128,256]{1,0:T(8,128)(2,1)S(1)} %get-tuple-element.52.att_ref, bf16[128,16384]{1,0:T(8,128)(2,1)} %w_hbm.9, bf16[128,16384]{1,0:T(8,128)(2,1)} %collective-permute-done.12.x_hbm, ...), custom_call_target="tpu_custom_call" | custom-call | flops 20000000000 | bytes 1000000 | tf_op jit(solution)/shard_map/pallas_call | solution.py:159
  67.0 0.0 copy-start
  67.0 0.0 copy-start.1
  67.0 0.0 copy-start.3
  67.0 0.7 collective-permute-start.18
  67.7 1.1 %collective-permute-start.19 = (bf16[128,1024]{1,0:T(8,128)(2,1)S(1)}, bf16[128,1024]{1,0:T(8,128)(2,1)S(1)}, u32[]{:S(2)}, u32[]{:S(2)}) collective-permute-start(bf16[128,1024]{1,0:T(8,128)(2,1)S(1)} %get-tuple-element.67), channel_id=1, source_target_pairs={{0,4},{1,5},{2,6},{3,7},{4,0},{5,1},{6,2},{7,3},{8,12},{9,13},{10,... | collective-permute-start | bytes 786440 | tf_op jit(solution)/shard_map/ppermute | solution.py:367
  68.8 7.8 %collective-permute-done.17.refs_0_.refs_3_ = bf16[128,1024]{1,0:T(8,128)(2,1)S(1)} collective-permute-done((bf16[128,1024]{1,0:T(8,128)(2,1)S(1)}, bf16[128,1024]{1,0:T(8,128)(2,1)S(1)}, u32[]{:S(2)}, u32[]{:S(2)}) %collective-permute-start.17) | collective-permute-done | bytes 262176 | tf_op jit(solution)/shard_map/ppermute | solution.py:367
  76.7 1.4 %collective-permute-done.19.refs_2_ = bf16[128,1024]{1,0:T(8,128)(2,1)S(1)} collective-permute-done((bf16[128,1024]{1,0:T(8,128)(2,1)S(1)}, bf16[128,1024]{1,0:T(8,128)(2,1)S(1)}, u32[]{:S(2)}, u32[]{:S(2)}) %collective-permute-start.19) | collective-permute-done | bytes 262176 | tf_op jit(solution)/shard_map/ppermute | solution.py:367
  78.1 1.5 %shard_map.117 = (bf16[128,1024]{1,0:T(8,128)(2,1)}, bf16[8,128]{1,0:T(8,128)(2,1)}) custom-call(s32[1]{0:T(128)} %bitcast.me.done, f32[8,128]{1,0:T(8,128)S(1)} %shard_map.115.done, bf16[128,1024]{1,0:T(8,128)(2,1)S(1)} %copy-done, bf16[8,128]{1,0:T(8,128)(2,1)S(1)} %copy-done.3, s32[128,128]{1,0:T(8,128)S(1)} %bitcast.18, ...), custom_call_target="tpu_custom_call" | custom-call | flops 1000000000 | bytes 1000000 | tf_op jit(solution)/shard_map/pallas_call | solution.py:159
  (17 shorter events, 0.1 us)
Async XLA Ops:
  0.6 20.7 %collective-permute-start.4 = (bf16[16384,128]{1,0:T(8,128)(2,1)}, bf16[16384,128]{1,0:T(8,128)(2,1)}, u32[]{:S(2)}, u32[]{:S(2)}) collective-permute-start(bf16[16384,128]{1,0:T(8,128)(2,1)} %w_hbm.6), channel_id=1, source_target_pairs={{0,1},{1,0},{2,3},{3,2},{4,5},{5,4},{6,7},{7,6},{8,9},{9,8},{10,11... | collective-permute-start | bytes 12582920 | tf_op jit(solution)/shard_map/ppermute | solution.py:367
  2.4 13.9 %collective-permute-start.2 = (bf16[128,1024]{1,0:T(8,128)(2,1)S(1)}, bf16[128,1024]{1,0:T(8,128)(2,1)S(1)}, u32[]{:S(2)}, u32[]{:S(2)}) collective-permute-start(bf16[128,1024]{1,0:T(8,128)(2,1)S(1)} %shard_map.104.u_ref.refs_0_), channel_id=1, source_target_pairs={{0,4},{1,5},{2,6},{3,7},{4,0},{5,1},{6,2},{7,3},{8,12},{9,13},{10,... | collective-permute-start | bytes 786440 | tf_op jit(solution)/shard_map/ppermute | solution.py:367
  5.1 11.3 %collective-permute-start.1 = (bf16[128,1024]{1,0:T(8,128)(2,1)S(1)}, bf16[128,1024]{1,0:T(8,128)(2,1)S(1)}, u32[]{:S(2)}, u32[]{:S(2)}) collective-permute-start(bf16[128,1024]{1,0:T(8,128)(2,1)S(1)} %shard_map.104.u_ref.refs_0_), channel_id=1, source_target_pairs={{0,2},{1,3},{2,0},{3,1},{4,6},{5,7},{6,4},{7,5},{8,10},{9,11},{10,... | collective-permute-start | bytes 786440 | tf_op jit(solution)/shard_map/ppermute | solution.py:367
  6.6 14.7 %collective-permute-start = (bf16[128,1024]{1,0:T(8,128)(2,1)S(1)}, bf16[128,1024]{1,0:T(8,128)(2,1)S(1)}, u32[]{:S(2)}, u32[]{:S(2)}) collective-permute-start(bf16[128,1024]{1,0:T(8,128)(2,1)S(1)} %shard_map.104.u_ref.refs_0_), channel_id=1, source_target_pairs={{0,8},{1,9},{2,10},{3,11},{4,12},{5,13},{6,14},{7,15},{8,0},{9,1},... | collective-permute-start | bytes 786440 | tf_op jit(solution)/shard_map/ppermute | solution.py:367
  11.9 11.8 %copy-start.4 = (s32[16]{0:T(128)S(1)}, s32[16]{0:T(128)}, u32[]{:S(2)}) copy-start(s32[16]{0:T(128)} %param.12) | copy-start | bytes 196
  11.9 12.7 %copy-start.2 = (bf16[16384]{0:T(1024)(128)(2,1)S(1)}, bf16[16384]{0:T(1024)(128)(2,1)}, u32[]{:S(2)}) copy-start(bf16[16384]{0:T(1024)(128)(2,1)} %param.13) | copy-start | bytes 98308
  11.9 9.4 %collective-permute-start.3 = (bf16[2,4,128,128]{3,2,1,0:T(8,128)(2,1)S(1)}, bf16[2,4,128,128]{3,2,1,0:T(8,128)(2,1)S(1)}, u32[]{:S(2)}, u32[]{:S(2)}) collective-permute-start(bf16[2,4,128,128]{3,2,1,0:T(8,128)(2,1)S(1)} %slice_bitcast_fusion.1), channel_id=1, source_target_pairs={{0,2},{1,3},{2,0},{3,1},{4,6},{5,7},{6,4},{7,5},{8,10},{9,11},{10,... | collective-permute-start | bytes 786440 | tf_op jit(solution)/shard_map/ppermute | solution.py:367
  21.4 1.4 %collective-permute-start.7 = (bf16[4,128,128]{2,1,0:T(8,128)(2,1)S(1)}, bf16[4,128,128]{2,1,0:T(8,128)(2,1)S(1)}, u32[]{:S(2)}, u32[]{:S(2)}) collective-permute-start(bf16[4,128,128]{2,1,0:T(8,128)(2,1)S(1)} %slice_bitcast_fusion.2), channel_id=1, source_target_pairs={{0,1},{1,0},{2,3},{3,2},{4,5},{5,4},{6,7},{7,6},{8,9},{9,8},{10,11... | collective-permute-start | bytes 393224 | tf_op jit(solution)/shard_map/ppermute | solution.py:367
  23.5 20.3 %collective-permute-start.12 = (bf16[128,16384]{1,0:T(8,128)(2,1)}, bf16[128,16384]{1,0:T(8,128)(2,1)}, u32[]{:S(2)}, u32[]{:S(2)}) collective-permute-start(bf16[128,16384]{1,0:T(8,128)(2,1)} %w_hbm.9), channel_id=1, source_target_pairs={{0,1},{1,0},{2,3},{3,2},{4,5},{5,4},{6,7},{7,6},{8,9},{9,8},{10,11... | collective-permute-start | bytes 12582920 | tf_op jit(solution)/shard_map/ppermute | solution.py:367
  23.8 8.6 %collective-permute-start.6 = (bf16[128,1024]{1,0:T(8,128)(2,1)S(1)}, bf16[128,1024]{1,0:T(8,128)(2,1)S(1)}, u32[]{:S(2)}, u32[]{:S(2)}) collective-permute-start(bf16[128,1024]{1,0:T(8,128)(2,1)S(1)} %collective-permute-done.refs_0_), channel_id=1, source_target_pairs={{0,2},{1,3},{2,0},{3,1},{4,6},{5,7},{6,4},{7,5},{8,10},{9,11},{10,... | collective-permute-start | bytes 786440 | tf_op jit(solution)/shard_map/ppermute | solution.py:367
  24.5 8.3 %collective-permute-start.5 = (bf16[128,1024]{1,0:T(8,128)(2,1)S(1)}, bf16[128,1024]{1,0:T(8,128)(2,1)S(1)}, u32[]{:S(2)}, u32[]{:S(2)}) collective-permute-start(bf16[128,1024]{1,0:T(8,128)(2,1)S(1)} %collective-permute-done.refs_0_), channel_id=1, source_target_pairs={{0,4},{1,5},{2,6},{3,7},{4,0},{5,1},{6,2},{7,3},{8,12},{9,13},{10,... | collective-permute-start | bytes 786440 | tf_op jit(solution)/shard_map/ppermute | solution.py:367
  26.5 15.8 %all-to-all-start = ((bf16[4,128,128]{2,1,0:T(8,128)(2,1)}), bf16[4,128,128]{2,1,0:T(8,128)(2,1)S(1)}, u32[]{:S(2)}, u32[]{:S(2)}) async-start(bf16[4,128,128]{2,1,0:T(8,128)(2,1)} %fusion.1), calls=%async_computation | async-start | bytes 262144 | tf_op jit(solution)/shard_map/all_to_all | solution.py:445
  32.7 8.9 %collective-permute-start.9 = (bf16[128,1024]{1,0:T(8,128)(2,1)S(1)}, bf16[128,1024]{1,0:T(8,128)(2,1)S(1)}, u32[]{:S(2)}, u32[]{:S(2)}) collective-permute-start(bf16[128,1024]{1,0:T(8,128)(2,1)S(1)} %collective-permute-done.1.refs_1_), channel_id=1, source_target_pairs={{0,4},{1,5},{2,6},{3,7},{4,0},{5,1},{6,2},{7,3},{8,12},{9,13},{10,... | collective-permute-start | bytes 786440 | tf_op jit(solution)/shard_map/ppermute | solution.py:367
  33.0 8.6 %collective-permute-start.8 = (bf16[128,1024]{1,0:T(8,128)(2,1)S(1)}, bf16[128,1024]{1,0:T(8,128)(2,1)S(1)}, u32[]{:S(2)}, u32[]{:S(2)}) collective-permute-start(bf16[128,1024]{1,0:T(8,128)(2,1)S(1)} %collective-permute-done.5.refs_0_.refs_2_), channel_id=1, source_target_pairs={{0,2},{1,3},{2,0},{3,1},{4,6},{5,7},{6,4},{7,5},{8,10},{9,11},{10,... | collective-permute-start | bytes 786440 | tf_op jit(solution)/shard_map/ppermute | solution.py:367
  42.0 1.9 %collective-permute-start.10 = (f32[128,384]{1,0:T(8,128)S(1)}, f32[128,384]{1,0:T(8,128)S(1)}, u32[]{:S(2)}, u32[]{:S(2)}) collective-permute-start(f32[128,384]{1,0:T(8,128)S(1)} %shard_map.111.pay_ref), channel_id=1, source_target_pairs={{0,1},{1,0},{2,3},{3,2},{4,5},{5,4},{6,7},{7,6},{8,9},{9,8},{10,11... | collective-permute-start | bytes 589832 | tf_op jit(solution)/shard_map/ppermute | solution.py:367
  42.4 1.4 %collective-permute-start.11 = (bf16[128,128]{1,0:T(8,128)(2,1)S(1)}, bf16[128,128]{1,0:T(8,128)(2,1)S(1)}, u32[]{:S(2)}, u32[]{:S(2)}) collective-permute-start(bf16[128,128]{1,0:T(8,128)(2,1)S(1)} %reduce_sum.12.kv_ref), channel_id=1, source_target_pairs={{0,1},{1,0},{2,3},{3,2},{4,5},{5,4},{6,7},{7,6},{8,9},{9,8},{10,11... | collective-permute-start | bytes 98312 | tf_op jit(solution)/shard_map/ppermute | solution.py:367
  46.0 8.6 %collective-permute-start.13 = (bf16[128,1024]{1,0:T(8,128)(2,1)S(1)}, bf16[128,1024]{1,0:T(8,128)(2,1)S(1)}, u32[]{:S(2)}, u32[]{:S(2)}) collective-permute-start(bf16[128,1024]{1,0:T(8,128)(2,1)S(1)} %get-tuple-element.55), channel_id=1, source_target_pairs={{0,2},{1,3},{2,0},{3,1},{4,6},{5,7},{6,4},{7,5},{8,10},{9,11},{10,... | collective-permute-start | bytes 786440 | tf_op jit(solution)/shard_map/ppermute | solution.py:367
  47.6 8.3 %collective-permute-start.14 = (bf16[128,1024]{1,0:T(8,128)(2,1)S(1)}, bf16[128,1024]{1,0:T(8,128)(2,1)S(1)}, u32[]{:S(2)}, u32[]{:S(2)}) collective-permute-start(bf16[128,1024]{1,0:T(8,128)(2,1)S(1)} %get-tuple-element.56), channel_id=1, source_target_pairs={{0,4},{1,5},{2,6},{3,7},{4,0},{5,1},{6,2},{7,3},{8,12},{9,13},{10,... | collective-permute-start | bytes 786440 | tf_op jit(solution)/shard_map/ppermute | solution.py:367
  55.9 7.5 %collective-permute-start.15 = (bf16[128,1024]{1,0:T(8,128)(2,1)S(1)}, bf16[128,1024]{1,0:T(8,128)(2,1)S(1)}, u32[]{:S(2)}, u32[]{:S(2)}) collective-permute-start(bf16[128,1024]{1,0:T(8,128)(2,1)S(1)} %add_convert_fusion.1), channel_id=1, source_target_pairs={{0,4},{1,5},{2,6},{3,7},{4,0},{5,1},{6,2},{7,3},{8,12},{9,13},{10,... | collective-permute-start | bytes 786440 | tf_op jit(solution)/shard_map/ppermute | solution.py:367
  56.3 7.2 %collective-permute-start.16 = (bf16[128,1024]{1,0:T(8,128)(2,1)S(1)}, bf16[128,1024]{1,0:T(8,128)(2,1)S(1)}, u32[]{:S(2)}, u32[]{:S(2)}) collective-permute-start(bf16[128,1024]{1,0:T(8,128)(2,1)S(1)} %get-tuple-element.59), channel_id=1, source_target_pairs={{0,2},{1,3},{2,0},{3,1},{4,6},{5,7},{6,4},{7,5},{8,10},{9,11},{10,... | collective-permute-start | bytes 786440 | tf_op jit(solution)/shard_map/ppermute | solution.py:367
  63.6 13.1 %collective-permute-start.17 = (bf16[128,1024]{1,0:T(8,128)(2,1)S(1)}, bf16[128,1024]{1,0:T(8,128)(2,1)S(1)}, u32[]{:S(2)}, u32[]{:S(2)}) collective-permute-start(bf16[128,1024]{1,0:T(8,128)(2,1)S(1)} %add_convert_fusion), channel_id=1, source_target_pairs={{0,8},{1,9},{2,10},{3,11},{4,12},{5,13},{6,14},{7,15},{8,0},{9,1},... | collective-permute-start | bytes 786440 | tf_op jit(solution)/shard_map/ppermute | solution.py:367
  67.0 11.1 %copy-start = (bf16[128,1024]{1,0:T(8,128)(2,1)S(1)}, bf16[128,1024]{1,0:T(8,128)(2,1)}, u32[]{:S(2)}) copy-start(bf16[128,1024]{1,0:T(8,128)(2,1)} %x_ref.1) | copy-start | bytes 786436
  67.0 11.1 %copy-start.1 = (s32[16384]{0:T(1024)S(1)}, s32[16384]{0:T(1024)}, u32[]{:S(2)}) copy-start(s32[16384]{0:T(1024)} %param.11) | copy-start | bytes 196612
  67.0 11.1 %copy-start.3 = (bf16[8,128]{1,0:T(8,128)(2,1)S(1)}, bf16[8,128]{1,0:T(8,128)(2,1)}, u32[]{:S(2)}) copy-start(bf16[8,128]{1,0:T(8,128)(2,1)} %s_ref.1) | copy-start | bytes 6148
  67.0 9.6 %collective-permute-start.18 = (bf16[128,1024]{1,0:T(8,128)(2,1)S(1)}, bf16[128,1024]{1,0:T(8,128)(2,1)S(1)}, u32[]{:S(2)}, u32[]{:S(2)}) collective-permute-start(bf16[128,1024]{1,0:T(8,128)(2,1)S(1)} %shard_map.116), channel_id=1, source_target_pairs={{0,2},{1,3},{2,0},{3,1},{4,6},{5,7},{6,4},{7,5},{8,10},{9,11},{10,... | collective-permute-start | bytes 786440 | tf_op jit(solution)/shard_map/ppermute | solution.py:367
  67.7 10.4 %collective-permute-start.19 = (bf16[128,1024]{1,0:T(8,128)(2,1)S(1)}, bf16[128,1024]{1,0:T(8,128)(2,1)S(1)}, u32[]{:S(2)}, u32[]{:S(2)}) collective-permute-start(bf16[128,1024]{1,0:T(8,128)(2,1)S(1)} %get-tuple-element.67), channel_id=1, source_target_pairs={{0,4},{1,5},{2,6},{3,7},{4,0},{5,1},{6,2},{7,3},{8,12},{9,13},{10,... | collective-permute-start | bytes 786440 | tf_op jit(solution)/shard_map/ppermute | solution.py:367
where the time goes:
time: 79.9 us; the launch traced here: 79.6 us
  waiting for transfers between devices  39.2 us (49%)
  starting transfers between devices  22.1 us (28%)
  Pallas kernels  15.6 us (20%)
  other arithmetic  1.44 us (2%)
  between operations  0.86 us (1%)
    ppermute x20, waiting for transfers between devices, swap(): return lax.ppermute(value, 'tensor', [(i, i ^ rel) for i in range(count)])  39.2 us
    ppermute x20, starting transfers between devices, swap(): return lax.ppermute(value, 'tensor', [(i, i ^ rel) for i in range(count)])  18 us
    pallas_call x14, Pallas kernels, call(): pl.pallas_call(kernel, out_shape=outs, in_specs=specs, out_specs=(VMEM,)...  15.6 us
    all_to_all x1, starting transfers between devices, paired(): kv = lax.all_to_all(kv, 'tensor', 0, 0, axis_index_groups=alike, tiled=True)  4.12 us
  transfers between devices with their start and end apart: 21, of which 13 were waited for; matrix products, arithmetic and copies ran while one was open for 1% of the time, Pallas kernels for 15%

commit v1 on v0

--- a/solution.py
+++ b/solution.py
@@ -192,10 +192,12 @@
     copies[2].wait()
     scale = s[...].astype(jnp.float32).T
     copies[3].wait()
+    tokens = x.shape[0]
+    stacked = jnp.concatenate([x[:, b * BLK : (b + 1) * BLK] for b in range(per)], axis=0)
+    turned = dot(stacked, had)
     for b in range(per):
-        cols = slice(b * BLK, (b + 1) * BLK)
-        part = dot(x[:, cols], had) * scale[:, b : b + 1]
-        u_ref[:, cols] = (part * sg[b : b + 1, :]).astype(jnp.bfloat16)
+        part = turned[b * tokens : (b + 1) * tokens] * scale[:, b : b + 1]
+        u_ref[:, b * BLK : (b + 1) * BLK] = (part * sg[b : b + 1, :]).astype(jnp.bfloat16)
 
 
 def token_kernel(*refs):
@@ -209,7 +211,7 @@
         copies[kind].wait()
         part = dot(u_ref[...], weights[...]).astype(jnp.bfloat16)
         for p in range(KVH):
-            kv_ref[(chip ^ p) & 1, 1 - (core ^ kind), p >> 1] = part[:, p * HD : (p + 1) * HD]
+            kv_ref[1 - (core ^ kind), (chip ^ p) & 1, p >> 1] = part[:, p * HD : (p + 1) * HD]
 
 
 def joint(me, w_hbm, x_hbm, rel, into):
@@ -289,6 +291,15 @@
     return pl.ds(pl.multiple_of((me[0] ^ rel) * width, width), width)
 
 
+def put(outs, value):
+    at = 0
+    while at < value.shape[0]:
+        rows = outs[0].shape[0]
+        outs[0][...] = value[at : at + rows].astype(outs[0].dtype)
+        at, outs = at + rows, outs[1:]
+    return outs
+
+
 def attend_kernel(total, rels, me, pay_ref, got_ref, kv_ref, kvx_ref, cos_ref, sin_ref, row_ref, col_ref, w_hbm, x_hbm, *refs):
     att_ref, outs, (ws, xs, sems) = refs[0], refs[1:-3], refs[-3:]
     width = ws.shape[2]
@@ -315,26 +326,23 @@
         head = dot(probs, value).astype(jnp.bfloat16)
         att_ref[:, at * HD : (at + 1) * HD] = head
         heads.append(head)
-    for k, out in enumerate(outs):
+    for k in range(len(rels)):
         copies[2 * k].wait()
         copies[2 * k + 1].wait()
-        out[...] = (dot(heads[0], ws[k]) + dot(heads[1], xs[k])).astype(out.dtype)
-
-
-def term_kernel(rels, added, me, done, att_ref, w_hbm, x_hbm, *refs):
-    adds, outs, (ws, xs, sems) = refs[:added], refs[added:-3], refs[-3:]
+        outs = put(outs, dot(heads[0], ws[k]) + dot(heads[1], xs[k]))
+
+
+def term_kernel(rels, me, att_ref, w_hbm, x_hbm, *refs):
+    outs, (ws, xs, sems) = refs[:-3], refs[-3:]
     width = ws.shape[2]
     copies = fetch(
         [(src.at[:, columns(me, rel, width)], dst.at[k]) for k, rel in enumerate(rels) for src, dst in ((w_hbm, ws), (x_hbm, xs))],
         sems,
     )
-    for k, out in enumerate(outs):
+    for k in range(len(rels)):
         copies[2 * k].wait()
         copies[2 * k + 1].wait()
-        term = dot(att_ref[:, :HD], ws[k]) + dot(att_ref[:, HD:], xs[k])
-        if k < added:
-            term = term + adds[k][...].astype(jnp.float32)
-        out[...] = term.astype(out.dtype)
+        outs = put(outs, dot(att_ref[:, :HD], ws[k]) + dot(att_ref[:, HD:], xs[k]))
 
 
 def final_kernel(n, me, done, x_ref, s_ref, sign_ref, *refs):
@@ -343,19 +351,26 @@
     per = s_ref.shape[0]
     sign = (2 * sign_ref[pl.ds(pl.multiple_of(me[0] * per, per), per), :] - 1).astype(jnp.float32) / math.sqrt(BLK)
     parts, (coded_ref, scales_ref) = refs[:n], refs[n:]
+    tokens = x_ref.shape[0]
+
+    def piece(at):
+        held, total = [], 0.0
+        for ref in parts:
+            held.append(ref[:, at].astype(jnp.float32))
+            if sum(h.shape[0] for h in held) == tokens:
+                total, held = total + jnp.concatenate(held, axis=0), []
+        return total
+
+    sums = jnp.concatenate([piece(slice(b * BLK, (b + 1) * BLK)) * sign[b : b + 1, :] for b in range(per)], axis=0)
+    high = sums.astype(jnp.bfloat16)
+    rest = sums - high.astype(jnp.float32)
+    mid = rest.astype(jnp.bfloat16)
+    low = (rest - mid.astype(jnp.float32)).astype(jnp.bfloat16)
+    turned = dot(high, had) + (dot(mid, had) + dot(low, had))
     tops = []
     for b in range(per):
         at = slice(b * BLK, (b + 1) * BLK)
-        part = parts[0][:, at].astype(jnp.float32)
-        for ref in parts[1:]:
-            part = part + ref[:, at].astype(jnp.float32)
-        part = part * sign[b : b + 1, :]
-        high = part.astype(jnp.bfloat16)
-        part = part - high.astype(jnp.float32)
-        mid = part.astype(jnp.bfloat16)
-        low = (part - mid.astype(jnp.float32)).astype(jnp.bfloat16)
-        new = dot(high, had) + (dot(mid, had) + dot(low, had))
-        new = new + x_ref[:, at].astype(jnp.float32) * scale[:, b : b + 1]
+        new = turned[b * tokens : (b + 1) * tokens] + x_ref[:, at].astype(jnp.float32) * scale[:, b : b + 1]
         top = (jnp.max(jnp.abs(new), axis=1, keepdims=True) + 1e-06).astype(jnp.bfloat16).astype(jnp.float32)
         coded_ref[:, at] = (new / top).astype(jnp.bfloat16)
         tops.append(top)
@@ -378,10 +393,20 @@
     bf16, f32 = jnp.bfloat16, jnp.float32
     block = jax.ShapeDtypeStruct((tokens, width), bf16)
     wide = jax.ShapeDtypeStruct((tokens, width), f32)
+    half_block = jax.ShapeDtypeStruct((tokens // 2, width), bf16)
+    half_wide = jax.ShapeDtypeStruct((tokens // 2, width), f32)
+    partial = jax.ShapeDtypeStruct((tokens, 3 * HD), f32)
     dma = pltpu.SemaphoreType.DMA
     together = lax.optimization_barrier
     sign2 = signs.reshape(-1, BLK)
     gain2 = norm_gain.reshape(-1, BLK)
+
+    def plus(*parts):
+        return sum(p.astype(f32) for p in parts).astype(bf16)
+
+    def after(*arrays, micros=3):
+        return call(token_kernel, jax.ShapeDtypeStruct((8, BLK), f32), arrays, [ANY] * len(arrays), micros=micros)
+
     u = call(
         unrotate_kernel,
         block,
@@ -396,8 +421,9 @@
             dma((4,)),
         ],
     )
-    wq_other = swap(w_query, CORE)
-    chunk = {0: u, FAR: swap(u, FAR)}
+
+    _, w_query_now = together((u, w_query))
+    wq_other = swap(w_query_now, CORE)
     kv = call(
         keyval_kernel,
         jax.ShapeDtypeStruct((2, 2, KVH // 2, tokens, HD), bf16),
@@ -406,65 +432,61 @@
         [pltpu.VMEM(w_key.shape, bf16), pltpu.VMEM(w_key.shape, bf16), dma((2,))],
         micros=20,
     )
-
-    def plus(*parts):
-        return sum(p.astype(f32) for p in parts).astype(bf16)
-
-    def after(*arrays):
-        return call(token_kernel, jax.ShapeDtypeStruct((8, BLK), f32), arrays, [ANY] * len(arrays), micros=3)
-
-    chunk[ACROSS] = swap(u, ACROSS)
-    chunk[NEAR] = swap(u, NEAR)
-    kvx = swap(kv[1], ACROSS)
-    done = after(chunk[8], chunk[2], chunk[4])
-    done, chunk[8], chunk[2], chunk[4], kvx, wq_other = together((done, chunk[8], chunk[2], chunk[4], kvx, wq_other))
-    kv = plus(kv[0], kvx)
-    chunk[12] = swap(chunk[8], NEAR)
-    chunk[10] = swap(chunk[8], ACROSS)
-
-    partial = jax.ShapeDtypeStruct((tokens, 3 * HD), f32)
+    kv = plus(kv[1], swap(kv[0], CORE))
+    kv_across = swap(kv[1], ACROSS)
+    far = swap(u, FAR)
+    across = swap(u, ACROSS)
+    near = swap(u, NEAR)
+    w_out_now = w_out
+    done = after(after(across, near, micros=10), far, micros=30)
+    near, kv_across, across, wq_other, far, w_out_now, done = together(
+        (near, kv_across, across, wq_other, far, w_out_now, done)
+    )
+    chunk = {0: u, 2: across, 4: near, 8: far}
+    kv = plus(kv[0], kv_across)
 
     early, more, late = (0, 2, 4), (8, 10, 12), (6, 14)
     pay = call(
         functools.partial(query_kernel, early),
         partial,
-        (me, done, gain2, w_query, wq_other) + tuple(chunk[r] for r in early),
+        (me, done, gain2, w_query, wq_other) + tuple(chunk[rel] for rel in early),
         [SMEM, ANY, VMEM, HBM, HBM] + [VMEM] * len(early),
         [
             pltpu.VMEM((len(early), width, 2 * HD), bf16),
             pltpu.VMEM(gain2.shape, f32),
             dma((2 * len(early),)),
         ],
-        micros=3,
-    )
-    kv = plus(kv[1], swap(kv[0], CORE))
-    kv, w_out_now = together((kv, w_out))
+        micros=10,
+    )
     wo_other = swap(w_out_now, CORE)
-    kv, pay = together((kv, pay))
+    chunk[12] = swap(chunk[8], NEAR)
+    chunk[10] = swap(chunk[8], ACROSS)
+    pay, kv = together((pay, kv))
     alike = [[4 * z + low for z in range(count // 4)] for low in range(4)]
     kv = lax.all_to_all(kv, "tensor", 0, 0, axis_index_groups=alike, tiled=True)
     done = after(chunk[12], chunk[10])
-    done, chunk[2], chunk[12], chunk[10], pay = together((done, chunk[2], chunk[12], chunk[10], pay))
+    done, chunk[2], chunk[12], chunk[10], pay, _ = together((done, chunk[2], chunk[12], chunk[10], pay, w_out_now))
+
     chunk[14] = swap(chunk[12], ACROSS)
     chunk[6] = swap(chunk[2], NEAR)
     pay, ahead = call(
         functools.partial(more_kernel, more, late),
         (partial, jax.ShapeDtypeStruct((len(late), width, 2 * HD), bf16)),
-        (me, done, gain2, w_query, wq_other, pay) + tuple(chunk[r] for r in more),
+        (me, done, gain2, w_query, wq_other, pay) + tuple(chunk[rel] for rel in more),
         [SMEM, ANY, VMEM, HBM, HBM, VMEM] + [VMEM] * len(more),
         [
             pltpu.VMEM((len(more), width, 2 * HD), bf16),
             pltpu.VMEM(gain2.shape, f32),
             dma((2 * len(more + late),)),
         ],
-        micros=3,
+        micros=20,
     )
     kv = jnp.sum(kv.astype(f32), axis=0).astype(bf16)
     kv_other = swap(kv, CORE)
     pay = call(
         functools.partial(last_kernel, late),
         partial,
-        (me, after(chunk[14], chunk[6]), gain2, ahead, pay) + tuple(chunk[r] for r in late),
+        (me, after(chunk[14], chunk[6], micros=10), gain2, ahead, pay) + tuple(chunk[rel] for rel in late),
         [SMEM, ANY] + [VMEM] * (3 + len(late)),
         [pltpu.VMEM(gain2.shape, f32)],
     )
@@ -483,41 +505,46 @@
         return [pltpu.VMEM((n, HD, width), bf16), pltpu.VMEM((n, HD, width), bf16), dma((2 * n,))]
 
     args = (me, pay, got, kv, kv_other, cosine, sine, positions[None, :], positions[:, None], w_out, wo_other)
-    att, t14, t6 = call(
-        functools.partial(attend_kernel, count * width, (14, 6)),
-        (jax.ShapeDtypeStruct((tokens, 2 * HD), bf16), block, block),
+    att, t14a, t14b = call(
+        functools.partial(attend_kernel, count * width, (14,)),
+        (jax.ShapeDtypeStruct((tokens, 2 * HD), bf16), half_block, half_block),
         args,
         [SMEM] + [VMEM] * 8 + [HBM] * 2,
-        buffers(2),
-    )
-
-    a14 = swap(t14, ACROSS)
-    n6 = swap(t6, NEAR)
-
-    def terms(rels, kinds, done, adds=()):
-        return call(
-            functools.partial(term_kernel, rels, len(adds)),
-            kinds,
-            (me, done, att, w_out, wo_other) + adds,
-            [SMEM, ANY, VMEM, HBM, HBM] + [VMEM] * len(adds),
-            buffers(len(rels)),
-            micros=20,
-        )
-
-    t10, t4, t12, t8, t0 = terms((10, 4, 12, 8, 0), (block, block, wide, wide, wide), me)
-    done, a14, n6, t10 = together((after(a14), a14, n6, t10))
-    n12 = swap(plus(t12, a14), NEAR)
-    a10 = swap(t10, ACROSS)
-    n12, a10, n6, t4 = together((n12, a10, n6, t4))
-    n8 = swap(plus(t8, a10, n12), FAR)
-    n4 = swap(t4, NEAR)
-    (t2,) = terms((2,), (block,), done, (n6,))
-    a2 = swap(t2, ACROSS)
-    parts = (t0, a2, n4, n8)
+        buffers(1),
+    )
+
+    x14a = swap(t14a, ACROSS)
+    rels = (10, 6, 2, 12, 8, 4, 0)
+    t10a, t10b, t6a, t6b, t2, t12a, t12b, t8a, t8b, t4a, t4b, t0 = call(
+        functools.partial(term_kernel, rels),
+        (half_block,) * 4 + (block,) + (half_wide,) * 6 + (wide,),
+        (me, att, w_out, wo_other),
+        [SMEM, VMEM, HBM, HBM],
+        buffers(len(rels)),
+        micros=20,
+    )
+    x14b = swap(t14b, ACROSS)
+    x14a, t10a = together((x14a, t10a))
+    n12a = swap(plus(t12a, x14a), NEAR)
+    x10a = swap(t10a, ACROSS)
+    x14b, t10b = together((x14b, t10b))
+    n12b = swap(plus(t12b, x14b), NEAR)
+    x10b = swap(t10b, ACROSS)
+    n12a, x10a, t6a = together((n12a, x10a, t6a))
+    n8a = swap(plus(t8a, x10a, n12a), FAR)
+    x6a = swap(t6a, ACROSS)
+    n12b, x10b, t6b = together((n12b, x10b, t6b))
+    n8b = swap(plus(t8b, x10b, n12b), FAR)
+    x6b = swap(t6b, ACROSS)
+    _, t2 = together((x10b, t2))
+    n4a = swap(plus(t4a, x6a), NEAR)
+    n4b = swap(plus(t4b, x6b), NEAR)
+    x2 = swap(t2, ACROSS)
+    parts = (t0, x2, n4a, n4b, n8a, n8b)
     return call(
         functools.partial(final_kernel, len(parts)),
         (block, jax.ShapeDtypeStruct(x_scales.shape, bf16)),
-        (me, after(n8), x_coded, x_scales, sign2) + parts,
+        (me, after(n8b), x_coded, x_scales, sign2) + parts,
         [SMEM, ANY] + [VMEM] * (3 + len(parts)),
     )
 

time: 79.9 us -> 73.5 us (0.920)
  waiting for transfers between devices: 39.2 us -> 23.8 us
  starting transfers between devices: 22.1 us -> 32.2 us
  Pallas kernels: 15.6 us -> 14.5 us
    ppermute x20 -> x26, waiting for transfers between devices: 39.2 us -> 23.8 us  [swap(): return lax.ppermute(value, 'tensor', [(i, i ^ rel) for i in range(count)])]
    ppermute x20 -> x26, starting transfers between devices: 18 us -> 28.7 us  [swap(): return lax.ppermute(value, 'tensor', [(i, i ^ rel) for i in range(count)])]
    pallas_call x14 -> x13, Pallas kernels: 15.6 us -> 14.5 us  [call(): pl.pallas_call(kernel, out_shape=outs, in_specs=specs, out_specs=(VMEM,)...]
  transfers between devices with their start and end apart: 21 -> 27, of which waited for: 13 -> 16; matrix products, arithmetic and copies ran while one was open for 1% -> 2% of each run, Pallas kernels for 15% -> 14%
where the time goes in v1:
time: 73.5 us; the launch traced here: 73.2 us
  starting transfers between devices  32.2 us (44%)
  waiting for transfers between devices  23.8 us (32%)
  Pallas kernels  14.5 us (20%)
  other arithmetic  1.47 us (2%)
  between operations  0.88 us (1%)
    ppermute x26, starting transfers between devices, swap(): return lax.ppermute(value, 'tensor', [(i, i ^ rel) for i in range(count)])  28.7 us
    ppermute x26, waiting for transfers between devices, swap(): return lax.ppermute(value, 'tensor', [(i, i ^ rel) for i in range(count)])  23.8 us
    pallas_call x13, Pallas kernels, call(): pl.pallas_call(kernel, out_shape=outs, in_specs=specs, out_specs=(VMEM,)...  14.5 us
    all_to_all x1, starting transfers between devices, paired(): kv = lax.all_to_all(kv, 'tensor', 0, 0, axis_index_groups=alike, tiled=True)  3.56 us
  transfers between devices with their start and end apart: 27, of which 16 were waited for; matrix products, arithmetic and copies ran while one was open for 2% of the time, Pallas kernels for 14%

profile of v1, /device:TPU:0, one launch (start us, length us, event | category | flops | bytes accessed | tf_op | source)
XLA Modules:
  0.0 73.2 jit_solution(7447712850420918888)
XLA Ops:
  0.6 1.3 %shard_map.104.u_ref.refs_0_ = bf16[128,1024]{1,0:T(8,128)(2,1)S(1)} custom-call(s32[1]{0:T(128)} %bitcast.me, bf16[128,1024]{1,0:T(8,128)(2,1)} %x_ref.1, bf16[8,128]{1,0:T(8,128)(2,1)} %s_ref.1, s32[128,128]{1,0:T(8,128)} %bitcast.17, bf16[128,128]{1,0:T(8,128)(2,1)} %bitcast.19), custom_call_target="tpu_custom_call" | custom-call | flops 1000000000 | bytes 1000000 | tf_op jit(solution)/shard_map/pallas_call | solution.py:159
  1.9 0.0 copy-start.4
  1.9 4.1 %collective-permute-start.5 = (bf16[128,1024]{1,0:T(8,128)(2,1)S(1)}, bf16[128,1024]{1,0:T(8,128)(2,1)S(1)}, u32[]{:S(2)}, u32[]{:S(2)}) collective-permute-start(bf16[128,1024]{1,0:T(8,128)(2,1)S(1)} %shard_map.104.u_ref.refs_0_), channel_id=1, source_target_pairs={{0,8},{1,9},{2,10},{3,11},{4,12},{5,13},{6,14},{7,15},{8,0},{9,1},... | collective-permute-start | bytes 786440 | tf_op jit(solution)/shard_map/ppermute | solution.py:382
  6.0 1.5 %collective-permute-start.3 = (bf16[128,1024]{1,0:T(8,128)(2,1)S(1)}, bf16[128,1024]{1,0:T(8,128)(2,1)S(1)}, u32[]{:S(2)}, u32[]{:S(2)}) collective-permute-start(bf16[128,1024]{1,0:T(8,128)(2,1)S(1)} %shard_map.104.u_ref.refs_0_), channel_id=1, source_target_pairs={{0,2},{1,3},{2,0},{3,1},{4,6},{5,7},{6,4},{7,5},{8,10},{9,11},{10,... | collective-permute-start | bytes 786440 | tf_op jit(solution)/shard_map/ppermute | solution.py:382
  7.5 1.6 %collective-permute-start = (bf16[128,1024]{1,0:T(8,128)(2,1)S(1)}, bf16[128,1024]{1,0:T(8,128)(2,1)S(1)}, u32[]{:S(2)}, u32[]{:S(2)}) collective-permute-start(bf16[128,1024]{1,0:T(8,128)(2,1)S(1)} %shard_map.104.u_ref.refs_0_), channel_id=1, source_target_pairs={{0,4},{1,5},{2,6},{3,7},{4,0},{5,1},{6,2},{7,3},{8,12},{9,13},{10,... | collective-permute-start | bytes 786440 | tf_op jit(solution)/shard_map/ppermute | solution.py:382
  9.1 2.7 %shard_map.105 = bf16[2,2,4,128,128]{4,3,2,1,0:T(8,128)(2,1)S(1)} custom-call(s32[1]{0:T(128)} %bitcast.me, bf16[128,1024]{1,0:T(8,128)(2,1)S(1)} %shard_map.104.u_ref.refs_0_, bf16[1024,1024]{1,0:T(8,128)(2,1)} %wk_hbm.1, bf16[1024,1024]{1,0:T(8,128)(2,1)} %wv_hbm.1), custom_call_target="tpu_custom_call" | custom-call | flops 20000000000 | bytes 1000000 | tf_op jit(solution)/shard_map/pallas_call | solution.py:159
  11.8 0.1 collective-permute-start.1
  11.9 0.5 collective-permute-start.4
  12.4 0.1 iota_add_fusion
  12.5 0.1 convert_element_type.94
  12.6 0.8 %collective-permute-done.1 = bf16[2,4,128,128]{3,2,1,0:T(8,128)(2,1)S(1)} collective-permute-done((bf16[2,4,128,128]{3,2,1,0:T(8,128)(2,1)S(1)}, bf16[2,4,128,128]{3,2,1,0:T(8,128)(2,1)S(1)}, u32[]{:S(2)}, u32[]{:S(2)}) %collective-permute-start.1) | collective-permute-done | bytes 262176 | tf_op jit(solution)/shard_map/ppermute | solution.py:382
  13.4 0.1 fusion
  13.5 0.6 collective-permute-start.2
  14.1 0.0 collective-permute-done.3.refs_0_.refs_1_
  14.1 5.3 %collective-permute-done.refs_1_.refs_2_ = bf16[128,1024]{1,0:T(8,128)(2,1)S(1)} collective-permute-done((bf16[128,1024]{1,0:T(8,128)(2,1)S(1)}, bf16[128,1024]{1,0:T(8,128)(2,1)S(1)}, u32[]{:S(2)}, u32[]{:S(2)}) %collective-permute-start) | collective-permute-done | bytes 262176 | tf_op jit(solution)/shard_map/ppermute | solution.py:382
  19.5 0.0 collective-permute-done.2
  19.5 0.3 collective-permute-done.4.x_hbm
  19.8 0.5 collective-permute-start.7
  20.3 1.0 %collective-permute-start.6 = (bf16[128,1024]{1,0:T(8,128)(2,1)S(1)}, bf16[128,1024]{1,0:T(8,128)(2,1)S(1)}, u32[]{:S(2)}, u32[]{:S(2)}) collective-permute-start(bf16[128,1024]{1,0:T(8,128)(2,1)S(1)} %collective-permute-done.5.refs_1_.refs_0_), channel_id=1, source_target_pairs={{0,4},{1,5},{2,6},{3,7},{4,0},{5,1},{6,2},{7,3},{8,12},{9,13},{10,... | collective-permute-start | bytes 786440 | tf_op jit(solution)/shard_map/ppermute | solution.py:382
  21.3 1.9 %shard_map.109.before_ref = f32[128,384]{1,0:T(8,128)S(1)} custom-call(s32[1]{0:T(128)} %bitcast.me, f32[8,128]{1,0:T(8,128)S(1)} %shard_map.107.token, bf16[128,128]{1,0:T(8,128)(2,1)S(1)} %bitcast.20, bf16[16384,128]{1,0:T(8,128)(2,1)} %w_hbm.5, bf16[16384,128]{1,0:T(8,128)(2,1)} %collective-permute-done.4.x_hbm, ...), custom_call_target="tpu_custom_call" | custom-call | flops 10000000000 | bytes 1000000 | tf_op jit(solution)/shard_map/pallas_call | solution.py:159
  23.2 0.7 fusion.1
  23.9 3.6 %all-to-all-start = ((bf16[4,128,128]{2,1,0:T(8,128)(2,1)}), bf16[4,128,128]{2,1,0:T(8,128)(2,1)S(1)}, u32[]{:S(2)}, u32[]{:S(2)}) async-start(bf16[4,128,128]{2,1,0:T(8,128)(2,1)} %fusion.1), calls=%async_computation | async-start | bytes 262144 | tf_op jit(solution)/shard_map/all_to_all | solution.py:466
  27.5 0.6 collective-permute-done.7.refs_1_
  28.1 0.2 collective-permute-done.6.refs_0_.refs_2_
  28.4 1.2 %collective-permute-start.9 = (bf16[128,1024]{1,0:T(8,128)(2,1)S(1)}, bf16[128,1024]{1,0:T(8,128)(2,1)S(1)}, u32[]{:S(2)}, u32[]{:S(2)}) collective-permute-start(bf16[128,1024]{1,0:T(8,128)(2,1)S(1)} %collective-permute-done.3.refs_0_.refs_1_), channel_id=1, source_target_pairs={{0,4},{1,5},{2,6},{3,7},{4,0},{5,1},{6,2},{7,3},{8,12},{9,13},{10,... | collective-permute-start | bytes 786440 | tf_op jit(solution)/shard_map/ppermute | solution.py:382
  29.6 1.0 %collective-permute-start.8 = (bf16[128,1024]{1,0:T(8,128)(2,1)S(1)}, bf16[128,1024]{1,0:T(8,128)(2,1)S(1)}, u32[]{:S(2)}, u32[]{:S(2)}) collective-permute-start(bf16[128,1024]{1,0:T(8,128)(2,1)S(1)} %collective-permute-done.6.refs_0_.refs_2_), channel_id=1, source_target_pairs={{0,2},{1,3},{2,0},{3,1},{4,6},{5,7},{6,4},{7,5},{8,10},{9,11},{10,... | collective-permute-start | bytes 786440 | tf_op jit(solution)/shard_map/ppermute | solution.py:382
  30.6 1.8 %shard_map.111 = (f32[128,384]{1,0:T(8,128)S(1)}, bf16[2,1024,256]{2,1,0:T(8,128)(2,1)S(1)}) custom-call(s32[1]{0:T(128)} %bitcast.me, f32[8,128]{1,0:T(8,128)S(1)} %shard_map.108.done, bf16[128,128]{1,0:T(8,128)(2,1)S(1)} %bitcast.21, bf16[16384,128]{1,0:T(8,128)(2,1)} %w_hbm.5, bf16[16384,128]{1,0:T(8,128)(2,1)} %collective-permute-done.4.x_hbm, ...), custom_call_target="tpu_custom_call" | custom-call | flops 20000000000 | bytes 1000000 | tf_op jit(solution)/shard_map/pallas_call | solution.py:159
  32.5 5.8 %collective-permute-done.9.refs_1_.refs_0_ = bf16[128,1024]{1,0:T(8,128)(2,1)S(1)} collective-permute-done((bf16[128,1024]{1,0:T(8,128)(2,1)S(1)}, bf16[128,1024]{1,0:T(8,128)(2,1)S(1)}, u32[]{:S(2)}, u32[]{:S(2)}) %collective-permute-start.9) | collective-permute-done | bytes 262176 | tf_op jit(solution)/shard_map/ppermute | solution.py:382
  38.3 0.3 shard_map.112.pay_ref
  38.6 0.1 collective-permute-start.10
  38.7 0.3 fusion.2
  39.0 0.6 collective-permute-start.11
  39.6 0.1 pad_maximum_fusion
  39.7 0.1 add.73.row_ref
  39.8 0.1 add.83.col_ref
  39.9 0.6 collective-permute-done.11.kvx_ref
  40.5 1.8 %shard_map.113 = (bf16[128,256]{1,0:T(8,128)(2,1)S(1)}, bf16[64,1024]{1,0:T(8,128)(2,1)S(1)}, bf16[64,1024]{1,0:T(8,128)(2,1)S(1)}) custom-call(s32[1]{0:T(128)} %bitcast.me, f32[128,384]{1,0:T(8,128)S(1)} %shard_map.112.pay_ref, f32[128,384]{1,0:T(8,128)S(1)} %collective-permute-done.10.got_ref, bf16[128,128]{1,0:T(8,128)(2,1)S(1)} %reduce_sum.12.kv_ref, ...), custom_call_target="tpu_custom_call" | custom-call | flops 1000000000 | bytes 1000000 | tf_op jit(solution)/shard_map/pallas_call | solution.py:159
  42.3 1.1 %collective-permute-start.13 = (bf16[64,1024]{1,0:T(8,128)(2,1)S(1)}, bf16[64,1024]{1,0:T(8,128)(2,1)S(1)}, u32[]{:S(2)}, u32[]{:S(2)}) collective-permute-start(bf16[64,1024]{1,0:T(8,128)(2,1)S(1)} %get-tuple-element.65), channel_id=1, source_target_pairs={{0,2},{1,3},{2,0},{3,1},{4,6},{5,7},{6,4},{7,5},{8,10},{9,11},{10,... | collective-permute-start | bytes 393224 | tf_op jit(solution)/shard_map/ppermute | solution.py:382
  43.3 1.0 %collective-permute-start.18 = (bf16[64,1024]{1,0:T(8,128)(2,1)S(1)}, bf16[64,1024]{1,0:T(8,128)(2,1)S(1)}, u32[]{:S(2)}, u32[]{:S(2)}) collective-permute-start(bf16[64,1024]{1,0:T(8,128)(2,1)S(1)} %get-tuple-element.77), channel_id=1, source_target_pairs={{0,2},{1,3},{2,0},{3,1},{4,6},{5,7},{6,4},{7,5},{8,10},{9,11},{10,... | collective-permute-start | bytes 393224 | tf_op jit(solution)/shard_map/ppermute | solution.py:382
  44.3 3.2 %shard_map.114 = (bf16[64,1024]{1,0:T(8,128)(2,1)S(1)}, bf16[64,1024]{1,0:T(8,128)(2,1)S(1)}, bf16[64,1024]{1,0:T(8,128)(2,1)S(1)}, bf16[64,1024]{1,0:T(8,128)(2...) custom-call(s32[1]{0:T(128)} %bitcast.me, ...), custom_call_target="tpu_custom_call" | custom-call | flops 20000000000 | bytes 1000000 | tf_op jit(solution)/shard_map/pallas_call | solution.py:159
  47.6 1.1 %collective-permute-done.13 = bf16[64,1024]{1,0:T(8,128)(2,1)S(1)} collective-permute-done((bf16[64,1024]{1,0:T(8,128)(2,1)S(1)}, bf16[64,1024]{1,0:T(8,128)(2,1)S(1)}, u32[]{:S(2)}, u32[]{:S(2)}) %collective-permute-start.13) | collective-permute-done | bytes 131104 | tf_op jit(solution)/shard_map/ppermute | solution.py:382
  48.7 0.4 collective-permute-start.14
  49.0 1.0 %collective-permute-start.15 = (bf16[64,1024]{1,0:T(8,128)(2,1)S(1)}, bf16[64,1024]{1,0:T(8,128)(2,1)S(1)}, u32[]{:S(2)}, u32[]{:S(2)}) collective-permute-start(bf16[64,1024]{1,0:T(8,128)(2,1)S(1)} %get-tuple-element.68), channel_id=1, source_target_pairs={{0,2},{1,3},{2,0},{3,1},{4,6},{5,7},{6,4},{7,5},{8,10},{9,11},{10,... | collective-permute-start | bytes 393224 | tf_op jit(solution)/shard_map/ppermute | solution.py:382
  50.0 1.3 %collective-permute-done.18 = bf16[64,1024]{1,0:T(8,128)(2,1)S(1)} collective-permute-done((bf16[64,1024]{1,0:T(8,128)(2,1)S(1)}, bf16[64,1024]{1,0:T(8,128)(2,1)S(1)}, u32[]{:S(2)}, u32[]{:S(2)}) %collective-permute-start.18) | collective-permute-done | bytes 131104 | tf_op jit(solution)/shard_map/ppermute | solution.py:382
  51.3 0.5 collective-permute-start.19
  51.9 1.0 %collective-permute-start.20 = (bf16[64,1024]{1,0:T(8,128)(2,1)S(1)}, bf16[64,1024]{1,0:T(8,128)(2,1)S(1)}, u32[]{:S(2)}, u32[]{:S(2)}) collective-permute-start(bf16[64,1024]{1,0:T(8,128)(2,1)S(1)} %get-tuple-element.80), channel_id=1, source_target_pairs={{0,2},{1,3},{2,0},{3,1},{4,6},{5,7},{6,4},{7,5},{8,10},{9,11},{10,... | collective-permute-start | bytes 393224 | tf_op jit(solution)/shard_map/ppermute | solution.py:382
  52.9 1.4 %collective-permute-done.14 = bf16[64,1024]{1,0:T(8,128)(2,1)S(1)} collective-permute-done((bf16[64,1024]{1,0:T(8,128)(2,1)S(1)}, bf16[64,1024]{1,0:T(8,128)(2,1)S(1)}, u32[]{:S(2)}, u32[]{:S(2)}) %collective-permute-start.14) | collective-permute-done | bytes 131104 | tf_op jit(solution)/shard_map/ppermute | solution.py:382
  54.3 0.5 collective-permute-done.15
  54.9 2.8 %collective-permute-start.16 = (bf16[64,1024]{1,0:T(8,128)(2,1)S(1)}, bf16[64,1024]{1,0:T(8,128)(2,1)S(1)}, u32[]{:S(2)}, u32[]{:S(2)}) collective-permute-start(bf16[64,1024]{1,0:T(8,128)(2,1)S(1)} %add_convert_fusion.4), channel_id=1, source_target_pairs={{0,8},{1,9},{2,10},{3,11},{4,12},{5,13},{6,14},{7,15},{8,0},{9,1},... | collective-permute-start | bytes 393224 | tf_op jit(solution)/shard_map/ppermute | solution.py:382
  57.6 1.0 %collective-permute-start.23 = (bf16[64,1024]{1,0:T(8,128)(2,1)S(1)}, bf16[64,1024]{1,0:T(8,128)(2,1)S(1)}, u32[]{:S(2)}, u32[]{:S(2)}) collective-permute-start(bf16[64,1024]{1,0:T(8,128)(2,1)S(1)} %get-tuple-element.84), channel_id=1, source_target_pairs={{0,2},{1,3},{2,0},{3,1},{4,6},{5,7},{6,4},{7,5},{8,10},{9,11},{10,... | collective-permute-start | bytes 393224 | tf_op jit(solution)/shard_map/ppermute | solution.py:382
  58.7 1.0 %collective-permute-start.21 = (bf16[64,1024]{1,0:T(8,128)(2,1)S(1)}, bf16[64,1024]{1,0:T(8,128)(2,1)S(1)}, u32[]{:S(2)}, u32[]{:S(2)}) collective-permute-start(bf16[64,1024]{1,0:T(8,128)(2,1)S(1)} %get-tuple-element.82), channel_id=1, source_target_pairs={{0,2},{1,3},{2,0},{3,1},{4,6},{5,7},{6,4},{7,5},{8,10},{9,11},{10,... | collective-permute-start | bytes 393224 | tf_op jit(solution)/shard_map/ppermute | solution.py:382
  59.7 2.1 %collective-permute-start.25 = (bf16[64,1024]{1,0:T(8,128)(2,1)S(1)}, bf16[64,1024]{1,0:T(8,128)(2,1)S(1)}, u32[]{:S(2)}, u32[]{:S(2)}) collective-permute-start(bf16[64,1024]{1,0:T(8,128)(2,1)S(1)} %add_convert_fusion), channel_id=1, source_target_pairs={{0,8},{1,9},{2,10},{3,11},{4,12},{5,13},{6,14},{7,15},{8,0},{9,1},... | collective-permute-start | bytes 393224 | tf_op jit(solution)/shard_map/ppermute | solution.py:382
  61.8 1.0 %collective-permute-start.17 = (bf16[128,1024]{1,0:T(8,128)(2,1)S(1)}, bf16[128,1024]{1,0:T(8,128)(2,1)S(1)}, u32[]{:S(2)}, u32[]{:S(2)}) collective-permute-start(bf16[128,1024]{1,0:T(8,128)(2,1)S(1)} %get-tuple-element.74), channel_id=1, source_target_pairs={{0,2},{1,3},{2,0},{3,1},{4,6},{5,7},{6,4},{7,5},{8,10},{9,11},{10,... | collective-permute-start | bytes 786440 | tf_op jit(solution)/shard_map/ppermute | solution.py:382
  62.8 0.9 %collective-permute-done.23 = bf16[64,1024]{1,0:T(8,128)(2,1)S(1)} collective-permute-done((bf16[64,1024]{1,0:T(8,128)(2,1)S(1)}, bf16[64,1024]{1,0:T(8,128)(2,1)S(1)}, u32[]{:S(2)}, u32[]{:S(2)}) %collective-permute-start.23) | collective-permute-done | bytes 131104 | tf_op jit(solution)/shard_map/ppermute | solution.py:382
  63.8 1.5 %collective-permute-start.24 = (bf16[64,1024]{1,0:T(8,128)(2,1)S(1)}, bf16[64,1024]{1,0:T(8,128)(2,1)S(1)}, u32[]{:S(2)}, u32[]{:S(2)}) collective-permute-start(bf16[64,1024]{1,0:T(8,128)(2,1)S(1)} %add_convert_fusion.1), channel_id=1, source_target_pairs={{0,4},{1,5},{2,6},{3,7},{4,0},{5,1},{6,2},{7,3},{8,12},{9,13},{10,... | collective-permute-start | bytes 393224 | tf_op jit(solution)/shard_map/ppermute | solution.py:382
  65.3 1.2 %collective-permute-done.21 = bf16[64,1024]{1,0:T(8,128)(2,1)S(1)} collective-permute-done((bf16[64,1024]{1,0:T(8,128)(2,1)S(1)}, bf16[64,1024]{1,0:T(8,128)(2,1)S(1)}, u32[]{:S(2)}, u32[]{:S(2)}) %collective-permute-start.21) | collective-permute-done | bytes 131104 | tf_op jit(solution)/shard_map/ppermute | solution.py:382
  66.6 0.0 copy-start
  66.6 0.0 copy-start.1
  66.6 0.0 copy-start.3
  66.6 1.5 %collective-permute-start.22 = (bf16[64,1024]{1,0:T(8,128)(2,1)S(1)}, bf16[64,1024]{1,0:T(8,128)(2,1)S(1)}, u32[]{:S(2)}, u32[]{:S(2)}) collective-permute-start(bf16[64,1024]{1,0:T(8,128)(2,1)S(1)} %add_convert_fusion.2), channel_id=1, source_target_pairs={{0,4},{1,5},{2,6},{3,7},{4,0},{5,1},{6,2},{7,3},{8,12},{9,13},{10,... | collective-permute-start | bytes 393224 | tf_op jit(solution)/shard_map/ppermute | solution.py:382
  68.2 0.1 collective-permute-done.25.refs_4_
  68.2 1.4 %collective-permute-done.24.refs_3_ = bf16[64,1024]{1,0:T(8,128)(2,1)S(1)} collective-permute-done((bf16[64,1024]{1,0:T(8,128)(2,1)S(1)}, bf16[64,1024]{1,0:T(8,128)(2,1)S(1)}, u32[]{:S(2)}, u32[]{:S(2)}) %collective-permute-start.24) | collective-permute-done | bytes 131104 | tf_op jit(solution)/shard_map/ppermute | solution.py:382
  69.7 2.0 %collective-permute-done.22.refs_2_ = bf16[64,1024]{1,0:T(8,128)(2,1)S(1)} collective-permute-done((bf16[64,1024]{1,0:T(8,128)(2,1)S(1)}, bf16[64,1024]{1,0:T(8,128)(2,1)S(1)}, u32[]{:S(2)}, u32[]{:S(2)}) %collective-permute-start.22) | collective-permute-done | bytes 131104 | tf_op jit(solution)/shard_map/ppermute | solution.py:382
  71.7 1.5 %shard_map.116 = (bf16[128,1024]{1,0:T(8,128)(2,1)}, bf16[8,128]{1,0:T(8,128)(2,1)}) custom-call(s32[1]{0:T(128)} %bitcast.me, f32[8,128]{1,0:T(8,128)S(1)} %shard_map.115.done, bf16[128,1024]{1,0:T(8,128)(2,1)S(1)} %copy-done, bf16[8,128]{1,0:T(8,128)(2,1)S(1)} %copy-done.3, s32[128,128]{1,0:T(8,128)S(1)} %bitcast.18, ...), custom_call_target="tpu_custom_call" | custom-call | flops 1000000000 | bytes 1000000 | tf_op jit(solution)/shard_map/pallas_call | solution.py:159
  (32 shorter events, 0.3 us)
Async XLA Ops:
  1.9 10.5 %copy-start.4 = (s32[16]{0:T(128)S(1)}, s32[16]{0:T(128)}, u32[]{:S(2)}) copy-start(s32[16]{0:T(128)} %param.12) | copy-start | bytes 196
  1.9 17.5 %collective-permute-start.5 = (bf16[128,1024]{1,0:T(8,128)(2,1)S(1)}, bf16[128,1024]{1,0:T(8,128)(2,1)S(1)}, u32[]{:S(2)}, u32[]{:S(2)}) collective-permute-start(bf16[128,1024]{1,0:T(8,128)(2,1)S(1)} %shard_map.104.u_ref.refs_0_), channel_id=1, source_target_pairs={{0,8},{1,9},{2,10},{3,11},{4,12},{5,13},{6,14},{7,15},{8,0},{9,1},... | collective-permute-start | bytes 786440 | tf_op jit(solution)/shard_map/ppermute | solution.py:382
  6.0 8.1 %collective-permute-start.3 = (bf16[128,1024]{1,0:T(8,128)(2,1)S(1)}, bf16[128,1024]{1,0:T(8,128)(2,1)S(1)}, u32[]{:S(2)}, u32[]{:S(2)}) collective-permute-start(bf16[128,1024]{1,0:T(8,128)(2,1)S(1)} %shard_map.104.u_ref.refs_0_), channel_id=1, source_target_pairs={{0,2},{1,3},{2,0},{3,1},{4,6},{5,7},{6,4},{7,5},{8,10},{9,11},{10,... | collective-permute-start | bytes 786440 | tf_op jit(solution)/shard_map/ppermute | solution.py:382
  7.5 11.9 %collective-permute-start = (bf16[128,1024]{1,0:T(8,128)(2,1)S(1)}, bf16[128,1024]{1,0:T(8,128)(2,1)S(1)}, u32[]{:S(2)}, u32[]{:S(2)}) collective-permute-start(bf16[128,1024]{1,0:T(8,128)(2,1)S(1)} %shard_map.104.u_ref.refs_0_), channel_id=1, source_target_pairs={{0,4},{1,5},{2,6},{3,7},{4,0},{5,1},{6,2},{7,3},{8,12},{9,13},{10,... | collective-permute-start | bytes 786440 | tf_op jit(solution)/shard_map/ppermute | solution.py:382
  11.8 1.6 %collective-permute-start.1 = (bf16[2,4,128,128]{3,2,1,0:T(8,128)(2,1)S(1)}, bf16[2,4,128,128]{3,2,1,0:T(8,128)(2,1)S(1)}, u32[]{:S(2)}, u32[]{:S(2)}) collective-permute-start(bf16[2,4,128,128]{3,2,1,0:T(8,128)(2,1)S(1)} %slice_bitcast_fusion), channel_id=1, source_target_pairs={{0,1},{1,0},{2,3},{3,2},{4,5},{5,4},{6,7},{7,6},{8,9},{9,8},{10,11... | collective-permute-start | bytes 786440 | tf_op jit(solution)/shard_map/ppermute | solution.py:382
  11.9 7.9 %collective-permute-start.4 = (bf16[16384,128]{1,0:T(8,128)(2,1)}, bf16[16384,128]{1,0:T(8,128)(2,1)}, u32[]{:S(2)}, u32[]{:S(2)}) collective-permute-start(bf16[16384,128]{1,0:T(8,128)(2,1)} %w_hbm.5), channel_id=1, source_target_pairs={{0,1},{1,0},{2,3},{3,2},{4,5},{5,4},{6,7},{7,6},{8,9},{9,8},{10,11... | collective-permute-start | bytes 12582920 | tf_op jit(solution)/shard_map/ppermute | solution.py:382
  13.5 5.9 %collective-permute-start.2 = (bf16[4,128,128]{2,1,0:T(8,128)(2,1)S(1)}, bf16[4,128,128]{2,1,0:T(8,128)(2,1)S(1)}, u32[]{:S(2)}, u32[]{:S(2)}) collective-permute-start(bf16[4,128,128]{2,1,0:T(8,128)(2,1)S(1)} %slice_bitcast_fusion.3), channel_id=1, source_target_pairs={{0,2},{1,3},{2,0},{3,1},{4,6},{5,7},{6,4},{7,5},{8,10},{9,11},{10,... | collective-permute-start | bytes 393224 | tf_op jit(solution)/shard_map/ppermute | solution.py:382
  19.5 1.9 %copy-start.2 = (bf16[16384]{0:T(1024)(128)(2,1)S(1)}, bf16[16384]{0:T(1024)(128)(2,1)}, u32[]{:S(2)}) copy-start(bf16[16384]{0:T(1024)(128)(2,1)} %param.13) | copy-start | bytes 98308
  19.8 8.3 %collective-permute-start.7 = (bf16[128,1024]{1,0:T(8,128)(2,1)S(1)}, bf16[128,1024]{1,0:T(8,128)(2,1)S(1)}, u32[]{:S(2)}, u32[]{:S(2)}) collective-permute-start(bf16[128,1024]{1,0:T(8,128)(2,1)S(1)} %collective-permute-done.5.refs_1_.refs_0_), channel_id=1, source_target_pairs={{0,2},{1,3},{2,0},{3,1},{4,6},{5,7},{6,4},{7,5},{8,10},{9,11},{10,... | collective-permute-start | bytes 786440 | tf_op jit(solution)/shard_map/ppermute | solution.py:382
  20.3 8.1 %collective-permute-start.6 = (bf16[128,1024]{1,0:T(8,128)(2,1)S(1)}, bf16[128,1024]{1,0:T(8,128)(2,1)S(1)}, u32[]{:S(2)}, u32[]{:S(2)}) collective-permute-start(bf16[128,1024]{1,0:T(8,128)(2,1)S(1)} %collective-permute-done.5.refs_1_.refs_0_), channel_id=1, source_target_pairs={{0,4},{1,5},{2,6},{3,7},{4,0},{5,1},{6,2},{7,3},{8,12},{9,13},{10,... | collective-permute-start | bytes 786440 | tf_op jit(solution)/shard_map/ppermute | solution.py:382
  21.3 19.1 %collective-permute-start.12 = (bf16[128,16384]{1,0:T(8,128)(2,1)}, bf16[128,16384]{1,0:T(8,128)(2,1)}, u32[]{:S(2)}, u32[]{:S(2)}) collective-permute-start(bf16[128,16384]{1,0:T(8,128)(2,1)} %w_hbm.7), channel_id=1, source_target_pairs={{0,1},{1,0},{2,3},{3,2},{4,5},{5,4},{6,7},{7,6},{8,9},{9,8},{10,11... | collective-permute-start | bytes 12582920 | tf_op jit(solution)/shard_map/ppermute | solution.py:382
  23.9 15.1 %all-to-all-start = ((bf16[4,128,128]{2,1,0:T(8,128)(2,1)}), bf16[4,128,128]{2,1,0:T(8,128)(2,1)S(1)}, u32[]{:S(2)}, u32[]{:S(2)}) async-start(bf16[4,128,128]{2,1,0:T(8,128)(2,1)} %fusion.1), calls=%async_computation | async-start | bytes 262144 | tf_op jit(solution)/shard_map/all_to_all | solution.py:466
  28.4 9.9 %collective-permute-start.9 = (bf16[128,1024]{1,0:T(8,128)(2,1)S(1)}, bf16[128,1024]{1,0:T(8,128)(2,1)S(1)}, u32[]{:S(2)}, u32[]{:S(2)}) collective-permute-start(bf16[128,1024]{1,0:T(8,128)(2,1)S(1)} %collective-permute-done.3.refs_0_.refs_1_), channel_id=1, source_target_pairs={{0,4},{1,5},{2,6},{3,7},{4,0},{5,1},{6,2},{7,3},{8,12},{9,13},{10,... | collective-permute-start | bytes 786440 | tf_op jit(solution)/shard_map/ppermute | solution.py:382
  29.6 8.7 %collective-permute-start.8 = (bf16[128,1024]{1,0:T(8,128)(2,1)S(1)}, bf16[128,1024]{1,0:T(8,128)(2,1)S(1)}, u32[]{:S(2)}, u32[]{:S(2)}) collective-permute-start(bf16[128,1024]{1,0:T(8,128)(2,1)S(1)} %collective-permute-done.6.refs_0_.refs_2_), channel_id=1, source_target_pairs={{0,2},{1,3},{2,0},{3,1},{4,6},{5,7},{6,4},{7,5},{8,10},{9,11},{10,... | collective-permute-start | bytes 786440 | tf_op jit(solution)/shard_map/ppermute | solution.py:382
  38.6 1.9 %collective-permute-start.10 = (f32[128,384]{1,0:T(8,128)S(1)}, f32[128,384]{1,0:T(8,128)S(1)}, u32[]{:S(2)}, u32[]{:S(2)}) collective-permute-start(f32[128,384]{1,0:T(8,128)S(1)} %shard_map.112.pay_ref), channel_id=1, source_target_pairs={{0,1},{1,0},{2,3},{3,2},{4,5},{5,4},{6,7},{7,6},{8,9},{9,8},{10,11... | collective-permute-start | bytes 589832 | tf_op jit(solution)/shard_map/ppermute | solution.py:382
  39.0 1.4 %collective-permute-start.11 = (bf16[128,128]{1,0:T(8,128)(2,1)S(1)}, bf16[128,128]{1,0:T(8,128)(2,1)S(1)}, u32[]{:S(2)}, u32[]{:S(2)}) collective-permute-start(bf16[128,128]{1,0:T(8,128)(2,1)S(1)} %reduce_sum.12.kv_ref), channel_id=1, source_target_pairs={{0,1},{1,0},{2,3},{3,2},{4,5},{5,4},{6,7},{7,6},{8,9},{9,8},{10,11... | collective-permute-start | bytes 98312 | tf_op jit(solution)/shard_map/ppermute | solution.py:382
  42.3 6.4 %collective-permute-start.13 = (bf16[64,1024]{1,0:T(8,128)(2,1)S(1)}, bf16[64,1024]{1,0:T(8,128)(2,1)S(1)}, u32[]{:S(2)}, u32[]{:S(2)}) collective-permute-start(bf16[64,1024]{1,0:T(8,128)(2,1)S(1)} %get-tuple-element.65), channel_id=1, source_target_pairs={{0,2},{1,3},{2,0},{3,1},{4,6},{5,7},{6,4},{7,5},{8,10},{9,11},{10,... | collective-permute-start | bytes 393224 | tf_op jit(solution)/shard_map/ppermute | solution.py:382
  43.3 8.0 %collective-permute-start.18 = (bf16[64,1024]{1,0:T(8,128)(2,1)S(1)}, bf16[64,1024]{1,0:T(8,128)(2,1)S(1)}, u32[]{:S(2)}, u32[]{:S(2)}) collective-permute-start(bf16[64,1024]{1,0:T(8,128)(2,1)S(1)} %get-tuple-element.77), channel_id=1, source_target_pairs={{0,2},{1,3},{2,0},{3,1},{4,6},{5,7},{6,4},{7,5},{8,10},{9,11},{10,... | collective-permute-start | bytes 393224 | tf_op jit(solution)/shard_map/ppermute | solution.py:382
  48.7 5.6 %collective-permute-start.14 = (bf16[64,1024]{1,0:T(8,128)(2,1)S(1)}, bf16[64,1024]{1,0:T(8,128)(2,1)S(1)}, u32[]{:S(2)}, u32[]{:S(2)}) collective-permute-start(bf16[64,1024]{1,0:T(8,128)(2,1)S(1)} %add_convert_fusion.5), channel_id=1, source_target_pairs={{0,4},{1,5},{2,6},{3,7},{4,0},{5,1},{6,2},{7,3},{8,12},{9,13},{10,... | collective-permute-start | bytes 393224 | tf_op jit(solution)/shard_map/ppermute | solution.py:382
  49.0 5.8 %collective-permute-start.15 = (bf16[64,1024]{1,0:T(8,128)(2,1)S(1)}, bf16[64,1024]{1,0:T(8,128)(2,1)S(1)}, u32[]{:S(2)}, u32[]{:S(2)}) collective-permute-start(bf16[64,1024]{1,0:T(8,128)(2,1)S(1)} %get-tuple-element.68), channel_id=1, source_target_pairs={{0,2},{1,3},{2,0},{3,1},{4,6},{5,7},{6,4},{7,5},{8,10},{9,11},{10,... | collective-permute-start | bytes 393224 | tf_op jit(solution)/shard_map/ppermute | solution.py:382
  51.3 7.3 %collective-permute-start.19 = (bf16[64,1024]{1,0:T(8,128)(2,1)S(1)}, bf16[64,1024]{1,0:T(8,128)(2,1)S(1)}, u32[]{:S(2)}, u32[]{:S(2)}) collective-permute-start(bf16[64,1024]{1,0:T(8,128)(2,1)S(1)} %add_convert_fusion.3), channel_id=1, source_target_pairs={{0,4},{1,5},{2,6},{3,7},{4,0},{5,1},{6,2},{7,3},{8,12},{9,13},{10,... | collective-permute-start | bytes 393224 | tf_op jit(solution)/shard_map/ppermute | solution.py:382
  51.9 6.8 %collective-permute-start.20 = (bf16[64,1024]{1,0:T(8,128)(2,1)S(1)}, bf16[64,1024]{1,0:T(8,128)(2,1)S(1)}, u32[]{:S(2)}, u32[]{:S(2)}) collective-permute-start(bf16[64,1024]{1,0:T(8,128)(2,1)S(1)} %get-tuple-element.80), channel_id=1, source_target_pairs={{0,2},{1,3},{2,0},{3,1},{4,6},{5,7},{6,4},{7,5},{8,10},{9,11},{10,... | collective-permute-start | bytes 393224 | tf_op jit(solution)/shard_map/ppermute | solution.py:382
  54.9 13.3 %collective-permute-start.16 = (bf16[64,1024]{1,0:T(8,128)(2,1)S(1)}, bf16[64,1024]{1,0:T(8,128)(2,1)S(1)}, u32[]{:S(2)}, u32[]{:S(2)}) collective-permute-start(bf16[64,1024]{1,0:T(8,128)(2,1)S(1)} %add_convert_fusion.4), channel_id=1, source_target_pairs={{0,8},{1,9},{2,10},{3,11},{4,12},{5,13},{6,14},{7,15},{8,0},{9,1},... | collective-permute-start | bytes 393224 | tf_op jit(solution)/shard_map/ppermute | solution.py:382
  57.6 6.1 %collective-permute-start.23 = (bf16[64,1024]{1,0:T(8,128)(2,1)S(1)}, bf16[64,1024]{1,0:T(8,128)(2,1)S(1)}, u32[]{:S(2)}, u32[]{:S(2)}) collective-permute-start(bf16[64,1024]{1,0:T(8,128)(2,1)S(1)} %get-tuple-element.84), channel_id=1, source_target_pairs={{0,2},{1,3},{2,0},{3,1},{4,6},{5,7},{6,4},{7,5},{8,10},{9,11},{10,... | collective-permute-start | bytes 393224 | tf_op jit(solution)/shard_map/ppermute | solution.py:382
  58.7 7.9 %collective-permute-start.21 = (bf16[64,1024]{1,0:T(8,128)(2,1)S(1)}, bf16[64,1024]{1,0:T(8,128)(2,1)S(1)}, u32[]{:S(2)}, u32[]{:S(2)}) collective-permute-start(bf16[64,1024]{1,0:T(8,128)(2,1)S(1)} %get-tuple-element.82), channel_id=1, source_target_pairs={{0,2},{1,3},{2,0},{3,1},{4,6},{5,7},{6,4},{7,5},{8,10},{9,11},{10,... | collective-permute-start | bytes 393224 | tf_op jit(solution)/shard_map/ppermute | solution.py:382
  59.7 8.5 %collective-permute-start.25 = (bf16[64,1024]{1,0:T(8,128)(2,1)S(1)}, bf16[64,1024]{1,0:T(8,128)(2,1)S(1)}, u32[]{:S(2)}, u32[]{:S(2)}) collective-permute-start(bf16[64,1024]{1,0:T(8,128)(2,1)S(1)} %add_convert_fusion), channel_id=1, source_target_pairs={{0,8},{1,9},{2,10},{3,11},{4,12},{5,13},{6,14},{7,15},{8,0},{9,1},... | collective-permute-start | bytes 393224 | tf_op jit(solution)/shard_map/ppermute | solution.py:382
  61.8 9.9 %collective-permute-start.17 = (bf16[128,1024]{1,0:T(8,128)(2,1)S(1)}, bf16[128,1024]{1,0:T(8,128)(2,1)S(1)}, u32[]{:S(2)}, u32[]{:S(2)}) collective-permute-start(bf16[128,1024]{1,0:T(8,128)(2,1)S(1)} %get-tuple-element.74), channel_id=1, source_target_pairs={{0,2},{1,3},{2,0},{3,1},{4,6},{5,7},{6,4},{7,5},{8,10},{9,11},{10,... | collective-permute-start | bytes 786440 | tf_op jit(solution)/shard_map/ppermute | solution.py:382
  63.8 5.9 %collective-permute-start.24 = (bf16[64,1024]{1,0:T(8,128)(2,1)S(1)}, bf16[64,1024]{1,0:T(8,128)(2,1)S(1)}, u32[]{:S(2)}, u32[]{:S(2)}) collective-permute-start(bf16[64,1024]{1,0:T(8,128)(2,1)S(1)} %add_convert_fusion.1), channel_id=1, source_target_pairs={{0,4},{1,5},{2,6},{3,7},{4,0},{5,1},{6,2},{7,3},{8,12},{9,13},{10,... | collective-permute-start | bytes 393224 | tf_op jit(solution)/shard_map/ppermute | solution.py:382
  66.6 5.1 %copy-start = (bf16[128,1024]{1,0:T(8,128)(2,1)S(1)}, bf16[128,1024]{1,0:T(8,128)(2,1)}, u32[]{:S(2)}) copy-start(bf16[128,1024]{1,0:T(8,128)(2,1)} %x_ref.1) | copy-start | bytes 786436
  66.6 5.1 %copy-start.1 = (s32[16384]{0:T(1024)S(1)}, s32[16384]{0:T(1024)}, u32[]{:S(2)}) copy-start(s32[16384]{0:T(1024)} %param.11) | copy-start | bytes 196612
  66.6 5.1 %copy-start.3 = (bf16[8,128]{1,0:T(8,128)(2,1)S(1)}, bf16[8,128]{1,0:T(8,128)(2,1)}, u32[]{:S(2)}) copy-start(bf16[8,128]{1,0:T(8,128)(2,1)} %s_ref.1) | copy-start | bytes 6148
  66.6 5.0 %collective-permute-start.22 = (bf16[64,1024]{1,0:T(8,128)(2,1)S(1)}, bf16[64,1024]{1,0:T(8,128)(2,1)S(1)}, u32[]{:S(2)}, u32[]{:S(2)}) collective-permute-start(bf16[64,1024]{1,0:T(8,128)(2,1)S(1)} %add_convert_fusion.2), channel_id=1, source_target_pairs={{0,4},{1,5},{2,6},{3,7},{4,0},{5,1},{6,2},{7,3},{8,12},{9,13},{10,... | collective-permute-start | bytes 393224 | tf_op jit(solution)/shard_map/ppermute | solution.py:382

commit v2 on v1

--- a/solution.py
+++ b/solution.py
@@ -300,7 +300,7 @@
     return outs
 
 
-def attend_kernel(total, rels, me, pay_ref, got_ref, kv_ref, kvx_ref, cos_ref, sin_ref, row_ref, col_ref, w_hbm, x_hbm, *refs):
+def attend_kernel(total, rels, me, done, pay_ref, got_ref, kv_ref, kvx_ref, cos_ref, sin_ref, row_ref, col_ref, w_hbm, x_hbm, *refs):
     att_ref, outs, (ws, xs, sems) = refs[0], refs[1:-3], refs[-3:]
     width = ws.shape[2]
     copies = fetch(
@@ -481,12 +481,13 @@
         ],
         micros=20,
     )
+    kv, pay = together((kv, pay))
     kv = jnp.sum(kv.astype(f32), axis=0).astype(bf16)
     kv_other = swap(kv, CORE)
     pay = call(
         functools.partial(last_kernel, late),
         partial,
-        (me, after(chunk[14], chunk[6], micros=10), gain2, ahead, pay) + tuple(chunk[rel] for rel in late),
+        (me, after(after(chunk[14], chunk[6], micros=10), micros=10), gain2, ahead, pay) + tuple(chunk[rel] for rel in late),
         [SMEM, ANY] + [VMEM] * (3 + len(late)),
         [pltpu.VMEM(gain2.shape, f32)],
     )
@@ -504,12 +505,12 @@
     def buffers(n):
         return [pltpu.VMEM((n, HD, width), bf16), pltpu.VMEM((n, HD, width), bf16), dma((2 * n,))]
 
-    args = (me, pay, got, kv, kv_other, cosine, sine, positions[None, :], positions[:, None], w_out, wo_other)
+    args = (me, after(kv_other, micros=10), pay, got, kv, kv_other, cosine, sine, positions[None, :], positions[:, None], w_out, wo_other)
     att, t14a, t14b = call(
         functools.partial(attend_kernel, count * width, (14,)),
         (jax.ShapeDtypeStruct((tokens, 2 * HD), bf16), half_block, half_block),
         args,
-        [SMEM] + [VMEM] * 8 + [HBM] * 2,
+        [SMEM, ANY] + [VMEM] * 8 + [HBM] * 2,
         buffers(1),
     )
 
@@ -527,19 +528,18 @@
     x14a, t10a = together((x14a, t10a))
     n12a = swap(plus(t12a, x14a), NEAR)
     x10a = swap(t10a, ACROSS)
-    x14b, t10b = together((x14b, t10b))
+    x14b, t10b, t6a, t6b = together((x14b, t10b, t6a, t6b))
     n12b = swap(plus(t12b, x14b), NEAR)
     x10b = swap(t10b, ACROSS)
-    n12a, x10a, t6a = together((n12a, x10a, t6a))
+    x6a = swap(t6a, ACROSS)
     n8a = swap(plus(t8a, x10a, n12a), FAR)
-    x6a = swap(t6a, ACROSS)
     n12b, x10b, t6b = together((n12b, x10b, t6b))
+    x6b = swap(t6b, ACROSS)
     n8b = swap(plus(t8b, x10b, n12b), FAR)
-    x6b = swap(t6b, ACROSS)
-    _, t2 = together((x10b, t2))
+    _, t2 = together((x6a, t2))
+    x2 = swap(t2, ACROSS)
     n4a = swap(plus(t4a, x6a), NEAR)
     n4b = swap(plus(t4b, x6b), NEAR)
-    x2 = swap(t2, ACROSS)
     parts = (t0, x2, n4a, n4b, n8a, n8b)
     return call(
         functools.partial(final_kernel, len(parts)),

time: 73.5 us -> 71.4 us (0.971)
  waiting for transfers between devices: 23.8 us -> 21 us
    ppermute x26, waiting for transfers between devices: 23.8 us -> 19.7 us  [swap(): return lax.ppermute(value, 'tensor', [(i, i ^ rel) for i in range(count)])]
    all_to_all x1, waiting for transfers between devices: 0.01 us -> 1.3 us  [paired(): kv = lax.all_to_all(kv, 'tensor', 0, 0, axis_index_groups=alike, tiled=True)]
    pallas_call x13 -> x15, Pallas kernels: 14.5 us -> 14.5 us  [call(): pl.pallas_call(kernel, out_shape=outs, in_specs=specs, out_specs=(VMEM,)...]
  transfers between devices with their start and end apart: 27 -> 27, of which waited for: 16 -> 15; matrix products, arithmetic and copies ran while one was open for 2% -> 3% of each run, Pallas kernels for 14% -> 14%
where the time goes in v2:
time: 71.4 us; the launch traced here: 71.1 us
  starting transfers between devices  32.8 us (46%)
  waiting for transfers between devices  21 us (29%)
  Pallas kernels  14.5 us (20%)
  other arithmetic  1.51 us (2%)
  between operations  0.9 us (1%)
    ppermute x26, starting transfers between devices, swap(): return lax.ppermute(value, 'tensor', [(i, i ^ rel) for i in range(count)])  29.3 us
    ppermute x26, waiting for transfers between devices, swap(): return lax.ppermute(value, 'tensor', [(i, i ^ rel) for i in range(count)])  19.7 us
    pallas_call x15, Pallas kernels, call(): pl.pallas_call(kernel, out_shape=outs, in_specs=specs, out_specs=(VMEM,)...  14.5 us
    all_to_all x1, starting transfers between devices, paired(): kv = lax.all_to_all(kv, 'tensor', 0, 0, axis_index_groups=alike, tiled=True)  3.56 us
  transfers between devices with their start and end apart: 27, of which 15 were waited for; matrix products, arithmetic and copies ran while one was open for 3% of the time, Pallas kernels for 14%

profile of v2, /device:TPU:0, one launch (start us, length us, event | category | flops | bytes accessed | tf_op | source)
XLA Modules:
  0.0 71.1 jit_solution(12387652539428260775)
XLA Ops:
  0.6 1.3 %shard_map.104.u_ref.refs_0_ = bf16[128,1024]{1,0:T(8,128)(2,1)S(1)} custom-call(s32[1]{0:T(128)} %bitcast.me, bf16[128,1024]{1,0:T(8,128)(2,1)} %x_ref.1, bf16[8,128]{1,0:T(8,128)(2,1)} %s_ref.1, s32[128,128]{1,0:T(8,128)} %bitcast.17, bf16[128,128]{1,0:T(8,128)(2,1)} %bitcast.19), custom_call_target="tpu_custom_call" | custom-call | flops 1000000000 | bytes 1000000 | tf_op jit(solution)/shard_map/pallas_call | solution.py:159
  1.9 0.0 copy-start.4
  1.9 4.1 %collective-permute-start.5 = (bf16[128,1024]{1,0:T(8,128)(2,1)S(1)}, bf16[128,1024]{1,0:T(8,128)(2,1)S(1)}, u32[]{:S(2)}, u32[]{:S(2)}) collective-permute-start(bf16[128,1024]{1,0:T(8,128)(2,1)S(1)} %shard_map.104.u_ref.refs_0_), channel_id=1, source_target_pairs={{0,8},{1,9},{2,10},{3,11},{4,12},{5,13},{6,14},{7,15},{8,0},{9,1},... | collective-permute-start | bytes 786440 | tf_op jit(solution)/shard_map/ppermute | solution.py:382
  6.0 1.5 %collective-permute-start.3 = (bf16[128,1024]{1,0:T(8,128)(2,1)S(1)}, bf16[128,1024]{1,0:T(8,128)(2,1)S(1)}, u32[]{:S(2)}, u32[]{:S(2)}) collective-permute-start(bf16[128,1024]{1,0:T(8,128)(2,1)S(1)} %shard_map.104.u_ref.refs_0_), channel_id=1, source_target_pairs={{0,2},{1,3},{2,0},{3,1},{4,6},{5,7},{6,4},{7,5},{8,10},{9,11},{10,... | collective-permute-start | bytes 786440 | tf_op jit(solution)/shard_map/ppermute | solution.py:382
  7.5 1.6 %collective-permute-start = (bf16[128,1024]{1,0:T(8,128)(2,1)S(1)}, bf16[128,1024]{1,0:T(8,128)(2,1)S(1)}, u32[]{:S(2)}, u32[]{:S(2)}) collective-permute-start(bf16[128,1024]{1,0:T(8,128)(2,1)S(1)} %shard_map.104.u_ref.refs_0_), channel_id=1, source_target_pairs={{0,4},{1,5},{2,6},{3,7},{4,0},{5,1},{6,2},{7,3},{8,12},{9,13},{10,... | collective-permute-start | bytes 786440 | tf_op jit(solution)/shard_map/ppermute | solution.py:382
  9.1 2.7 %shard_map.105 = bf16[2,2,4,128,128]{4,3,2,1,0:T(8,128)(2,1)S(1)} custom-call(s32[1]{0:T(128)} %bitcast.me, bf16[128,1024]{1,0:T(8,128)(2,1)S(1)} %shard_map.104.u_ref.refs_0_, bf16[1024,1024]{1,0:T(8,128)(2,1)} %wk_hbm.1, bf16[1024,1024]{1,0:T(8,128)(2,1)} %wv_hbm.1), custom_call_target="tpu_custom_call" | custom-call | flops 20000000000 | bytes 1000000 | tf_op jit(solution)/shard_map/pallas_call | solution.py:159
  11.8 0.1 collective-permute-start.1
  11.9 0.5 collective-permute-start.4
  12.4 0.1 iota_add_fusion
  12.5 0.1 add.73.row_ref
  12.6 0.1 add.83.col_ref
  12.7 0.1 convert_element_type.94
  12.8 0.3 fusion.2
  13.1 0.1 pad_maximum_fusion
  13.2 0.2 collective-permute-done.1
  13.4 0.1 fusion
  13.5 0.6 collective-permute-start.2
  14.1 5.3 %collective-permute-done.refs_1_.refs_2_ = bf16[128,1024]{1,0:T(8,128)(2,1)S(1)} collective-permute-done((bf16[128,1024]{1,0:T(8,128)(2,1)S(1)}, bf16[128,1024]{1,0:T(8,128)(2,1)S(1)}, u32[]{:S(2)}, u32[]{:S(2)}) %collective-permute-start) | collective-permute-done | bytes 262176 | tf_op jit(solution)/shard_map/ppermute | solution.py:382
  19.5 0.3 collective-permute-done.4.x_hbm
  19.8 0.5 collective-permute-start.7
  20.3 1.0 %collective-permute-start.6 = (bf16[128,1024]{1,0:T(8,128)(2,1)S(1)}, bf16[128,1024]{1,0:T(8,128)(2,1)S(1)}, u32[]{:S(2)}, u32[]{:S(2)}) collective-permute-start(bf16[128,1024]{1,0:T(8,128)(2,1)S(1)} %collective-permute-done.5.refs_1_.refs_0_), channel_id=1, source_target_pairs={{0,4},{1,5},{2,6},{3,7},{4,0},{5,1},{6,2},{7,3},{8,12},{9,13},{10,... | collective-permute-start | bytes 786440 | tf_op jit(solution)/shard_map/ppermute | solution.py:382
  21.3 1.9 %shard_map.108.before_ref = f32[128,384]{1,0:T(8,128)S(1)} custom-call(s32[1]{0:T(128)} %bitcast.me, f32[8,128]{1,0:T(8,128)S(1)} %shard_map.107.token, bf16[128,128]{1,0:T(8,128)(2,1)S(1)} %bitcast.20, bf16[16384,128]{1,0:T(8,128)(2,1)} %w_hbm.5, bf16[16384,128]{1,0:T(8,128)(2,1)} %collective-permute-done.4.x_hbm, ...), custom_call_target="tpu_custom_call" | custom-call | flops 10000000000 | bytes 1000000 | tf_op jit(solution)/shard_map/pallas_call | solution.py:159
  23.2 0.7 fusion.1
  23.9 3.6 %all-to-all-start = ((bf16[4,128,128]{2,1,0:T(8,128)(2,1)}), bf16[4,128,128]{2,1,0:T(8,128)(2,1)S(1)}, u32[]{:S(2)}, u32[]{:S(2)}) async-start(bf16[4,128,128]{2,1,0:T(8,128)(2,1)} %fusion.1), calls=%async_computation | async-start | bytes 262144 | tf_op jit(solution)/shard_map/all_to_all | solution.py:466
  27.5 0.6 collective-permute-done.7.refs_1_
  28.1 0.2 collective-permute-done.6.refs_0_.refs_2_
  28.4 1.2 %collective-permute-start.10 = (bf16[128,1024]{1,0:T(8,128)(2,1)S(1)}, bf16[128,1024]{1,0:T(8,128)(2,1)S(1)}, u32[]{:S(2)}, u32[]{:S(2)}) collective-permute-start(bf16[128,1024]{1,0:T(8,128)(2,1)S(1)} %collective-permute-done.3.refs_0_.refs_1_), channel_id=1, source_target_pairs={{0,4},{1,5},{2,6},{3,7},{4,0},{5,1},{6,2},{7,3},{8,12},{9,13},{10,... | collective-permute-start | bytes 786440 | tf_op jit(solution)/shard_map/ppermute | solution.py:382
  29.6 1.0 %collective-permute-start.9 = (bf16[128,1024]{1,0:T(8,128)(2,1)S(1)}, bf16[128,1024]{1,0:T(8,128)(2,1)S(1)}, u32[]{:S(2)}, u32[]{:S(2)}) collective-permute-start(bf16[128,1024]{1,0:T(8,128)(2,1)S(1)} %collective-permute-done.6.refs_0_.refs_2_), channel_id=1, source_target_pairs={{0,2},{1,3},{2,0},{3,1},{4,6},{5,7},{6,4},{7,5},{8,10},{9,11},{10,... | collective-permute-start | bytes 786440 | tf_op jit(solution)/shard_map/ppermute | solution.py:382
  30.6 1.8 %shard_map.110 = (f32[128,384]{1,0:T(8,128)S(1)}, bf16[2,1024,256]{2,1,0:T(8,128)(2,1)S(1)}) custom-call(s32[1]{0:T(128)} %bitcast.me, f32[8,128]{1,0:T(8,128)S(1)} %shard_map.109.done, bf16[128,128]{1,0:T(8,128)(2,1)S(1)} %bitcast.21, bf16[16384,128]{1,0:T(8,128)(2,1)} %w_hbm.5, bf16[16384,128]{1,0:T(8,128)(2,1)} %collective-permute-done.4.x_hbm, ...), custom_call_target="tpu_custom_call" | custom-call | flops 20000000000 | bytes 1000000 | tf_op jit(solution)/shard_map/pallas_call | solution.py:159
  32.5 1.3 %all-to-all-done = bf16[4,128,128]{2,1,0:T(8,128)(2,1)S(1)} async-done(((bf16[4,128,128]{2,1,0:T(8,128)(2,1)}), bf16[4,128,128]{2,1,0:T(8,128)(2,1)S(1)}, u32[]{:S(2)}, u32[]{:S(2)}) %all-to-all-start) | async-done | bytes 131104 | tf_op jit(solution)/shard_map/all_to_all | solution.py:466
  33.8 0.1 collective-permute-start.8
  33.9 4.2 %collective-permute-done.10.refs_1_.refs_0_ = bf16[128,1024]{1,0:T(8,128)(2,1)S(1)} collective-permute-done((bf16[128,1024]{1,0:T(8,128)(2,1)S(1)}, bf16[128,1024]{1,0:T(8,128)(2,1)S(1)}, u32[]{:S(2)}, u32[]{:S(2)}) %collective-permute-start.10) | collective-permute-done | bytes 262176 | tf_op jit(solution)/shard_map/ppermute | solution.py:382
  38.1 0.3 shard_map.114.pay_ref
  38.4 0.1 collective-permute-start.11
  38.5 1.4 %collective-permute-done.11.got_ref = f32[128,384]{1,0:T(8,128)S(1)} collective-permute-done((f32[128,384]{1,0:T(8,128)S(1)}, f32[128,384]{1,0:T(8,128)S(1)}, u32[]{:S(2)}, u32[]{:S(2)}) %collective-permute-start.11) | collective-permute-done | bytes 196640 | tf_op jit(solution)/shard_map/ppermute | solution.py:382
  39.9 1.8 %shard_map.115 = (bf16[128,256]{1,0:T(8,128)(2,1)S(1)}, bf16[64,1024]{1,0:T(8,128)(2,1)S(1)}, bf16[64,1024]{1,0:T(8,128)(2,1)S(1)}) custom-call(s32[1]{0:T(128)} %bitcast.me, f32[8,128]{1,0:T(8,128)S(1)} %shard_map.111.done, f32[128,384]{1,0:T(8,128)S(1)} %shard_map.114.pay_ref, f32[128,384]{1,0:T(8,128)S(1)} %collective-permute-done.11.got_ref, ...), custom_call_target="tpu_custom_call" | custom-call | flops 1000000000 | bytes 1000000 | tf_op jit(solution)/shard_map/pallas_call | solution.py:159
  41.8 1.1 %collective-permute-start.13 = (bf16[64,1024]{1,0:T(8,128)(2,1)S(1)}, bf16[64,1024]{1,0:T(8,128)(2,1)S(1)}, u32[]{:S(2)}, u32[]{:S(2)}) collective-permute-start(bf16[64,1024]{1,0:T(8,128)(2,1)S(1)} %get-tuple-element.68), channel_id=1, source_target_pairs={{0,2},{1,3},{2,0},{3,1},{4,6},{5,7},{6,4},{7,5},{8,10},{9,11},{10,... | collective-permute-start | bytes 393224 | tf_op jit(solution)/shard_map/ppermute | solution.py:382
  42.9 1.0 %collective-permute-start.22 = (bf16[64,1024]{1,0:T(8,128)(2,1)S(1)}, bf16[64,1024]{1,0:T(8,128)(2,1)S(1)}, u32[]{:S(2)}, u32[]{:S(2)}) collective-permute-start(bf16[64,1024]{1,0:T(8,128)(2,1)S(1)} %get-tuple-element.85), channel_id=1, source_target_pairs={{0,2},{1,3},{2,0},{3,1},{4,6},{5,7},{6,4},{7,5},{8,10},{9,11},{10,... | collective-permute-start | bytes 393224 | tf_op jit(solution)/shard_map/ppermute | solution.py:382
  43.9 3.2 %shard_map.116 = (bf16[64,1024]{1,0:T(8,128)(2,1)S(1)}, bf16[64,1024]{1,0:T(8,128)(2,1)S(1)}, bf16[64,1024]{1,0:T(8,128)(2,1)S(1)}, bf16[64,1024]{1,0:T(8,128)(2...) custom-call(s32[1]{0:T(128)} %bitcast.me, ...), custom_call_target="tpu_custom_call" | custom-call | flops 20000000000 | bytes 1000000 | tf_op jit(solution)/shard_map/pallas_call | solution.py:159
  47.0 1.2 %collective-permute-done.13 = bf16[64,1024]{1,0:T(8,128)(2,1)S(1)} collective-permute-done((bf16[64,1024]{1,0:T(8,128)(2,1)S(1)}, bf16[64,1024]{1,0:T(8,128)(2,1)S(1)}, u32[]{:S(2)}, u32[]{:S(2)}) %collective-permute-start.13) | collective-permute-done | bytes 131104 | tf_op jit(solution)/shard_map/ppermute | solution.py:382
  48.2 0.3 collective-permute-start.14
  48.6 1.0 %collective-permute-start.15 = (bf16[64,1024]{1,0:T(8,128)(2,1)S(1)}, bf16[64,1024]{1,0:T(8,128)(2,1)S(1)}, u32[]{:S(2)}, u32[]{:S(2)}) collective-permute-start(bf16[64,1024]{1,0:T(8,128)(2,1)S(1)} %get-tuple-element.73), channel_id=1, source_target_pairs={{0,2},{1,3},{2,0},{3,1},{4,6},{5,7},{6,4},{7,5},{8,10},{9,11},{10,... | collective-permute-start | bytes 393224 | tf_op jit(solution)/shard_map/ppermute | solution.py:382
  49.6 1.0 %collective-permute-start.17 = (bf16[64,1024]{1,0:T(8,128)(2,1)S(1)}, bf16[64,1024]{1,0:T(8,128)(2,1)S(1)}, u32[]{:S(2)}, u32[]{:S(2)}) collective-permute-start(bf16[64,1024]{1,0:T(8,128)(2,1)S(1)} %get-tuple-element.78), channel_id=1, source_target_pairs={{0,2},{1,3},{2,0},{3,1},{4,6},{5,7},{6,4},{7,5},{8,10},{9,11},{10,... | collective-permute-start | bytes 393224 | tf_op jit(solution)/shard_map/ppermute | solution.py:382
  50.6 0.3 collective-permute-done.22
  50.8 1.0 %collective-permute-start.23 = (bf16[64,1024]{1,0:T(8,128)(2,1)S(1)}, bf16[64,1024]{1,0:T(8,128)(2,1)S(1)}, u32[]{:S(2)}, u32[]{:S(2)}) collective-permute-start(bf16[64,1024]{1,0:T(8,128)(2,1)S(1)} %get-tuple-element.87), channel_id=1, source_target_pairs={{0,2},{1,3},{2,0},{3,1},{4,6},{5,7},{6,4},{7,5},{8,10},{9,11},{10,... | collective-permute-start | bytes 393224 | tf_op jit(solution)/shard_map/ppermute | solution.py:382
  51.9 1.6 %collective-permute-start.24 = (bf16[64,1024]{1,0:T(8,128)(2,1)S(1)}, bf16[64,1024]{1,0:T(8,128)(2,1)S(1)}, u32[]{:S(2)}, u32[]{:S(2)}) collective-permute-start(bf16[64,1024]{1,0:T(8,128)(2,1)S(1)} %add_convert_fusion.1), channel_id=1, source_target_pairs={{0,4},{1,5},{2,6},{3,7},{4,0},{5,1},{6,2},{7,3},{8,12},{9,13},{10,... | collective-permute-start | bytes 393224 | tf_op jit(solution)/shard_map/ppermute | solution.py:382
  53.5 0.0 collective-permute-done.14
  53.5 1.5 %collective-permute-done.15 = bf16[64,1024]{1,0:T(8,128)(2,1)S(1)} collective-permute-done((bf16[64,1024]{1,0:T(8,128)(2,1)S(1)}, bf16[64,1024]{1,0:T(8,128)(2,1)S(1)}, u32[]{:S(2)}, u32[]{:S(2)}) %collective-permute-start.15) | collective-permute-done | bytes 131104 | tf_op jit(solution)/shard_map/ppermute | solution.py:382
  55.0 0.1 add_convert_fusion.4
  55.0 2.7 %collective-permute-start.16 = (bf16[64,1024]{1,0:T(8,128)(2,1)S(1)}, bf16[64,1024]{1,0:T(8,128)(2,1)S(1)}, u32[]{:S(2)}, u32[]{:S(2)}) collective-permute-start(bf16[64,1024]{1,0:T(8,128)(2,1)S(1)} %add_convert_fusion.4), channel_id=1, source_target_pairs={{0,8},{1,9},{2,10},{3,11},{4,12},{5,13},{6,14},{7,15},{8,0},{9,1},... | collective-permute-start | bytes 393224 | tf_op jit(solution)/shard_map/ppermute | solution.py:382
  57.7 1.0 %collective-permute-start.20 = (bf16[64,1024]{1,0:T(8,128)(2,1)S(1)}, bf16[64,1024]{1,0:T(8,128)(2,1)S(1)}, u32[]{:S(2)}, u32[]{:S(2)}) collective-permute-start(bf16[64,1024]{1,0:T(8,128)(2,1)S(1)} %get-tuple-element.83), channel_id=1, source_target_pairs={{0,2},{1,3},{2,0},{3,1},{4,6},{5,7},{6,4},{7,5},{8,10},{9,11},{10,... | collective-permute-start | bytes 393224 | tf_op jit(solution)/shard_map/ppermute | solution.py:382
  58.8 1.5 %collective-permute-start.19 = (bf16[64,1024]{1,0:T(8,128)(2,1)S(1)}, bf16[64,1024]{1,0:T(8,128)(2,1)S(1)}, u32[]{:S(2)}, u32[]{:S(2)}) collective-permute-start(bf16[64,1024]{1,0:T(8,128)(2,1)S(1)} %add_convert_fusion.3), channel_id=1, source_target_pairs={{0,4},{1,5},{2,6},{3,7},{4,0},{5,1},{6,2},{7,3},{8,12},{9,13},{10,... | collective-permute-start | bytes 393224 | tf_op jit(solution)/shard_map/ppermute | solution.py:382
  60.3 0.1 add_convert_fusion
  60.3 2.3 %collective-permute-start.25 = (bf16[64,1024]{1,0:T(8,128)(2,1)S(1)}, bf16[64,1024]{1,0:T(8,128)(2,1)S(1)}, u32[]{:S(2)}, u32[]{:S(2)}) collective-permute-start(bf16[64,1024]{1,0:T(8,128)(2,1)S(1)} %add_convert_fusion), channel_id=1, source_target_pairs={{0,8},{1,9},{2,10},{3,11},{4,12},{5,13},{6,14},{7,15},{8,0},{9,1},... | collective-permute-start | bytes 393224 | tf_op jit(solution)/shard_map/ppermute | solution.py:382
  62.6 1.0 %collective-permute-start.18 = (bf16[128,1024]{1,0:T(8,128)(2,1)S(1)}, bf16[128,1024]{1,0:T(8,128)(2,1)S(1)}, u32[]{:S(2)}, u32[]{:S(2)}) collective-permute-start(bf16[128,1024]{1,0:T(8,128)(2,1)S(1)} %get-tuple-element.80), channel_id=1, source_target_pairs={{0,2},{1,3},{2,0},{3,1},{4,6},{5,7},{6,4},{7,5},{8,10},{9,11},{10,... | collective-permute-start | bytes 786440 | tf_op jit(solution)/shard_map/ppermute | solution.py:382
  63.6 0.5 collective-permute-done.20
  64.1 0.0 copy-start
  64.1 0.0 copy-start.1
  64.1 0.0 copy-start.3
  64.2 1.5 %collective-permute-start.21 = (bf16[64,1024]{1,0:T(8,128)(2,1)S(1)}, bf16[64,1024]{1,0:T(8,128)(2,1)S(1)}, u32[]{:S(2)}, u32[]{:S(2)}) collective-permute-start(bf16[64,1024]{1,0:T(8,128)(2,1)S(1)} %add_convert_fusion.2), channel_id=1, source_target_pairs={{0,4},{1,5},{2,6},{3,7},{4,0},{5,1},{6,2},{7,3},{8,12},{9,13},{10,... | collective-permute-start | bytes 393224 | tf_op jit(solution)/shard_map/ppermute | solution.py:382
  65.7 2.3 %collective-permute-done.19.refs_2_ = bf16[64,1024]{1,0:T(8,128)(2,1)S(1)} collective-permute-done((bf16[64,1024]{1,0:T(8,128)(2,1)S(1)}, bf16[64,1024]{1,0:T(8,128)(2,1)S(1)}, u32[]{:S(2)}, u32[]{:S(2)}) %collective-permute-start.19) | collective-permute-done | bytes 131104 | tf_op jit(solution)/shard_map/ppermute | solution.py:382
  67.9 0.2 collective-permute-done.25.refs_4_
  68.1 1.4 %collective-permute-done.21.refs_3_ = bf16[64,1024]{1,0:T(8,128)(2,1)S(1)} collective-permute-done((bf16[64,1024]{1,0:T(8,128)(2,1)S(1)}, bf16[64,1024]{1,0:T(8,128)(2,1)S(1)}, u32[]{:S(2)}, u32[]{:S(2)}) %collective-permute-start.21) | collective-permute-done | bytes 131104 | tf_op jit(solution)/shard_map/ppermute | solution.py:382
  69.6 1.5 %shard_map.118 = (bf16[128,1024]{1,0:T(8,128)(2,1)}, bf16[8,128]{1,0:T(8,128)(2,1)}) custom-call(s32[1]{0:T(128)} %bitcast.me, f32[8,128]{1,0:T(8,128)S(1)} %shard_map.117.done, bf16[128,1024]{1,0:T(8,128)(2,1)S(1)} %copy-done, bf16[8,128]{1,0:T(8,128)(2,1)S(1)} %copy-done.3, s32[128,128]{1,0:T(8,128)S(1)} %bitcast.18, ...), custom_call_target="tpu_custom_call" | custom-call | flops 1000000000 | bytes 1000000 | tf_op jit(solution)/shard_map/pallas_call | solution.py:159
  (34 shorter events, 0.2 us)
Async XLA Ops:
  1.9 10.5 %copy-start.4 = (s32[16]{0:T(128)S(1)}, s32[16]{0:T(128)}, u32[]{:S(2)}) copy-start(s32[16]{0:T(128)} %param.12) | copy-start | bytes 196
  1.9 17.5 %collective-permute-start.5 = (bf16[128,1024]{1,0:T(8,128)(2,1)S(1)}, bf16[128,1024]{1,0:T(8,128)(2,1)S(1)}, u32[]{:S(2)}, u32[]{:S(2)}) collective-permute-start(bf16[128,1024]{1,0:T(8,128)(2,1)S(1)} %shard_map.104.u_ref.refs_0_), channel_id=1, source_target_pairs={{0,8},{1,9},{2,10},{3,11},{4,12},{5,13},{6,14},{7,15},{8,0},{9,1},... | collective-permute-start | bytes 786440 | tf_op jit(solution)/shard_map/ppermute | solution.py:382
  6.0 8.1 %collective-permute-start.3 = (bf16[128,1024]{1,0:T(8,128)(2,1)S(1)}, bf16[128,1024]{1,0:T(8,128)(2,1)S(1)}, u32[]{:S(2)}, u32[]{:S(2)}) collective-permute-start(bf16[128,1024]{1,0:T(8,128)(2,1)S(1)} %shard_map.104.u_ref.refs_0_), channel_id=1, source_target_pairs={{0,2},{1,3},{2,0},{3,1},{4,6},{5,7},{6,4},{7,5},{8,10},{9,11},{10,... | collective-permute-start | bytes 786440 | tf_op jit(solution)/shard_map/ppermute | solution.py:382
  7.5 11.9 %collective-permute-start = (bf16[128,1024]{1,0:T(8,128)(2,1)S(1)}, bf16[128,1024]{1,0:T(8,128)(2,1)S(1)}, u32[]{:S(2)}, u32[]{:S(2)}) collective-permute-start(bf16[128,1024]{1,0:T(8,128)(2,1)S(1)} %shard_map.104.u_ref.refs_0_), channel_id=1, source_target_pairs={{0,4},{1,5},{2,6},{3,7},{4,0},{5,1},{6,2},{7,3},{8,12},{9,13},{10,... | collective-permute-start | bytes 786440 | tf_op jit(solution)/shard_map/ppermute | solution.py:382
  11.8 1.6 %collective-permute-start.1 = (bf16[2,4,128,128]{3,2,1,0:T(8,128)(2,1)S(1)}, bf16[2,4,128,128]{3,2,1,0:T(8,128)(2,1)S(1)}, u32[]{:S(2)}, u32[]{:S(2)}) collective-permute-start(bf16[2,4,128,128]{3,2,1,0:T(8,128)(2,1)S(1)} %slice_bitcast_fusion), channel_id=1, source_target_pairs={{0,1},{1,0},{2,3},{3,2},{4,5},{5,4},{6,7},{7,6},{8,9},{9,8},{10,11... | collective-permute-start | bytes 786440 | tf_op jit(solution)/shard_map/ppermute | solution.py:382
  11.9 7.9 %collective-permute-start.4 = (bf16[16384,128]{1,0:T(8,128)(2,1)}, bf16[16384,128]{1,0:T(8,128)(2,1)}, u32[]{:S(2)}, u32[]{:S(2)}) collective-permute-start(bf16[16384,128]{1,0:T(8,128)(2,1)} %w_hbm.5), channel_id=1, source_target_pairs={{0,1},{1,0},{2,3},{3,2},{4,5},{5,4},{6,7},{7,6},{8,9},{9,8},{10,11... | collective-permute-start | bytes 12582920 | tf_op jit(solution)/shard_map/ppermute | solution.py:382
  13.5 5.9 %collective-permute-start.2 = (bf16[4,128,128]{2,1,0:T(8,128)(2,1)S(1)}, bf16[4,128,128]{2,1,0:T(8,128)(2,1)S(1)}, u32[]{:S(2)}, u32[]{:S(2)}) collective-permute-start(bf16[4,128,128]{2,1,0:T(8,128)(2,1)S(1)} %slice_bitcast_fusion.3), channel_id=1, source_target_pairs={{0,2},{1,3},{2,0},{3,1},{4,6},{5,7},{6,4},{7,5},{8,10},{9,11},{10,... | collective-permute-start | bytes 393224 | tf_op jit(solution)/shard_map/ppermute | solution.py:382
  19.5 1.9 %copy-start.2 = (bf16[16384]{0:T(1024)(128)(2,1)S(1)}, bf16[16384]{0:T(1024)(128)(2,1)}, u32[]{:S(2)}) copy-start(bf16[16384]{0:T(1024)(128)(2,1)} %param.13) | copy-start | bytes 98308
  19.8 8.3 %collective-permute-start.7 = (bf16[128,1024]{1,0:T(8,128)(2,1)S(1)}, bf16[128,1024]{1,0:T(8,128)(2,1)S(1)}, u32[]{:S(2)}, u32[]{:S(2)}) collective-permute-start(bf16[128,1024]{1,0:T(8,128)(2,1)S(1)} %collective-permute-done.5.refs_1_.refs_0_), channel_id=1, source_target_pairs={{0,2},{1,3},{2,0},{3,1},{4,6},{5,7},{6,4},{7,5},{8,10},{9,11},{10,... | collective-permute-start | bytes 786440 | tf_op jit(solution)/shard_map/ppermute | solution.py:382
  20.3 8.1 %collective-permute-start.6 = (bf16[128,1024]{1,0:T(8,128)(2,1)S(1)}, bf16[128,1024]{1,0:T(8,128)(2,1)S(1)}, u32[]{:S(2)}, u32[]{:S(2)}) collective-permute-start(bf16[128,1024]{1,0:T(8,128)(2,1)S(1)} %collective-permute-done.5.refs_1_.refs_0_), channel_id=1, source_target_pairs={{0,4},{1,5},{2,6},{3,7},{4,0},{5,1},{6,2},{7,3},{8,12},{9,13},{10,... | collective-permute-start | bytes 786440 | tf_op jit(solution)/shard_map/ppermute | solution.py:382
  23.9 9.8 %all-to-all-start = ((bf16[4,128,128]{2,1,0:T(8,128)(2,1)}), bf16[4,128,128]{2,1,0:T(8,128)(2,1)S(1)}, u32[]{:S(2)}, u32[]{:S(2)}) async-start(bf16[4,128,128]{2,1,0:T(8,128)(2,1)} %fusion.1), calls=%async_computation | async-start | bytes 262144 | tf_op jit(solution)/shard_map/all_to_all | solution.py:466
  27.5 12.5 %collective-permute-start.12 = (bf16[128,16384]{1,0:T(8,128)(2,1)}, bf16[128,16384]{1,0:T(8,128)(2,1)}, u32[]{:S(2)}, u32[]{:S(2)}) collective-permute-start(bf16[128,16384]{1,0:T(8,128)(2,1)} %w_hbm.7), channel_id=1, source_target_pairs={{0,1},{1,0},{2,3},{3,2},{4,5},{5,4},{6,7},{7,6},{8,9},{9,8},{10,11... | collective-permute-start | bytes 12582920 | tf_op jit(solution)/shard_map/ppermute | solution.py:382
  28.4 9.7 %collective-permute-start.10 = (bf16[128,1024]{1,0:T(8,128)(2,1)S(1)}, bf16[128,1024]{1,0:T(8,128)(2,1)S(1)}, u32[]{:S(2)}, u32[]{:S(2)}) collective-permute-start(bf16[128,1024]{1,0:T(8,128)(2,1)S(1)} %collective-permute-done.3.refs_0_.refs_1_), channel_id=1, source_target_pairs={{0,4},{1,5},{2,6},{3,7},{4,0},{5,1},{6,2},{7,3},{8,12},{9,13},{10,... | collective-permute-start | bytes 786440 | tf_op jit(solution)/shard_map/ppermute | solution.py:382
  29.6 8.5 %collective-permute-start.9 = (bf16[128,1024]{1,0:T(8,128)(2,1)S(1)}, bf16[128,1024]{1,0:T(8,128)(2,1)S(1)}, u32[]{:S(2)}, u32[]{:S(2)}) collective-permute-start(bf16[128,1024]{1,0:T(8,128)(2,1)S(1)} %collective-permute-done.6.refs_0_.refs_2_), channel_id=1, source_target_pairs={{0,2},{1,3},{2,0},{3,1},{4,6},{5,7},{6,4},{7,5},{8,10},{9,11},{10,... | collective-permute-start | bytes 786440 | tf_op jit(solution)/shard_map/ppermute | solution.py:382
  33.8 4.7 %collective-permute-start.8 = (bf16[128,128]{1,0:T(8,128)(2,1)S(1)}, bf16[128,128]{1,0:T(8,128)(2,1)S(1)}, u32[]{:S(2)}, u32[]{:S(2)}) collective-permute-start(bf16[128,128]{1,0:T(8,128)(2,1)S(1)} %reduce_sum.12.kv_ref), channel_id=1, source_target_pairs={{0,1},{1,0},{2,3},{3,2},{4,5},{5,4},{6,7},{7,6},{8,9},{9,8},{10,11... | collective-permute-start | bytes 98312 | tf_op jit(solution)/shard_map/ppermute | solution.py:382
  38.4 1.5 %collective-permute-start.11 = (f32[128,384]{1,0:T(8,128)S(1)}, f32[128,384]{1,0:T(8,128)S(1)}, u32[]{:S(2)}, u32[]{:S(2)}) collective-permute-start(f32[128,384]{1,0:T(8,128)S(1)} %shard_map.114.pay_ref), channel_id=1, source_target_pairs={{0,1},{1,0},{2,3},{3,2},{4,5},{5,4},{6,7},{7,6},{8,9},{9,8},{10,11... | collective-permute-start | bytes 589832 | tf_op jit(solution)/shard_map/ppermute | solution.py:382
  41.8 6.4 %collective-permute-start.13 = (bf16[64,1024]{1,0:T(8,128)(2,1)S(1)}, bf16[64,1024]{1,0:T(8,128)(2,1)S(1)}, u32[]{:S(2)}, u32[]{:S(2)}) collective-permute-start(bf16[64,1024]{1,0:T(8,128)(2,1)S(1)} %get-tuple-element.68), channel_id=1, source_target_pairs={{0,2},{1,3},{2,0},{3,1},{4,6},{5,7},{6,4},{7,5},{8,10},{9,11},{10,... | collective-permute-start | bytes 393224 | tf_op jit(solution)/shard_map/ppermute | solution.py:382
  42.9 8.0 %collective-permute-start.22 = (bf16[64,1024]{1,0:T(8,128)(2,1)S(1)}, bf16[64,1024]{1,0:T(8,128)(2,1)S(1)}, u32[]{:S(2)}, u32[]{:S(2)}) collective-permute-start(bf16[64,1024]{1,0:T(8,128)(2,1)S(1)} %get-tuple-element.85), channel_id=1, source_target_pairs={{0,2},{1,3},{2,0},{3,1},{4,6},{5,7},{6,4},{7,5},{8,10},{9,11},{10,... | collective-permute-start | bytes 393224 | tf_op jit(solution)/shard_map/ppermute | solution.py:382
  48.2 5.3 %collective-permute-start.14 = (bf16[64,1024]{1,0:T(8,128)(2,1)S(1)}, bf16[64,1024]{1,0:T(8,128)(2,1)S(1)}, u32[]{:S(2)}, u32[]{:S(2)}) collective-permute-start(bf16[64,1024]{1,0:T(8,128)(2,1)S(1)} %add_convert_fusion.5), channel_id=1, source_target_pairs={{0,4},{1,5},{2,6},{3,7},{4,0},{5,1},{6,2},{7,3},{8,12},{9,13},{10,... | collective-permute-start | bytes 393224 | tf_op jit(solution)/shard_map/ppermute | solution.py:382
  48.6 6.4 %collective-permute-start.15 = (bf16[64,1024]{1,0:T(8,128)(2,1)S(1)}, bf16[64,1024]{1,0:T(8,128)(2,1)S(1)}, u32[]{:S(2)}, u32[]{:S(2)}) collective-permute-start(bf16[64,1024]{1,0:T(8,128)(2,1)S(1)} %get-tuple-element.73), channel_id=1, source_target_pairs={{0,2},{1,3},{2,0},{3,1},{4,6},{5,7},{6,4},{7,5},{8,10},{9,11},{10,... | collective-permute-start | bytes 393224 | tf_op jit(solution)/shard_map/ppermute | solution.py:382
  49.6 9.2 %collective-permute-start.17 = (bf16[64,1024]{1,0:T(8,128)(2,1)S(1)}, bf16[64,1024]{1,0:T(8,128)(2,1)S(1)}, u32[]{:S(2)}, u32[]{:S(2)}) collective-permute-start(bf16[64,1024]{1,0:T(8,128)(2,1)S(1)} %get-tuple-element.78), channel_id=1, source_target_pairs={{0,2},{1,3},{2,0},{3,1},{4,6},{5,7},{6,4},{7,5},{8,10},{9,11},{10,... | collective-permute-start | bytes 393224 | tf_op jit(solution)/shard_map/ppermute | solution.py:382
  50.8 9.4 %collective-permute-start.23 = (bf16[64,1024]{1,0:T(8,128)(2,1)S(1)}, bf16[64,1024]{1,0:T(8,128)(2,1)S(1)}, u32[]{:S(2)}, u32[]{:S(2)}) collective-permute-start(bf16[64,1024]{1,0:T(8,128)(2,1)S(1)} %get-tuple-element.87), channel_id=1, source_target_pairs={{0,2},{1,3},{2,0},{3,1},{4,6},{5,7},{6,4},{7,5},{8,10},{9,11},{10,... | collective-permute-start | bytes 393224 | tf_op jit(solution)/shard_map/ppermute | solution.py:382
  51.9 8.3 %collective-permute-start.24 = (bf16[64,1024]{1,0:T(8,128)(2,1)S(1)}, bf16[64,1024]{1,0:T(8,128)(2,1)S(1)}, u32[]{:S(2)}, u32[]{:S(2)}) collective-permute-start(bf16[64,1024]{1,0:T(8,128)(2,1)S(1)} %add_convert_fusion.1), channel_id=1, source_target_pairs={{0,4},{1,5},{2,6},{3,7},{4,0},{5,1},{6,2},{7,3},{8,12},{9,13},{10,... | collective-permute-start | bytes 393224 | tf_op jit(solution)/shard_map/ppermute | solution.py:382
  55.0 10.6 %collective-permute-start.16 = (bf16[64,1024]{1,0:T(8,128)(2,1)S(1)}, bf16[64,1024]{1,0:T(8,128)(2,1)S(1)}, u32[]{:S(2)}, u32[]{:S(2)}) collective-permute-start(bf16[64,1024]{1,0:T(8,128)(2,1)S(1)} %add_convert_fusion.4), channel_id=1, source_target_pairs={{0,8},{1,9},{2,10},{3,11},{4,12},{5,13},{6,14},{7,15},{8,0},{9,1},... | collective-permute-start | bytes 393224 | tf_op jit(solution)/shard_map/ppermute | solution.py:382
  57.7 6.4 %collective-permute-start.20 = (bf16[64,1024]{1,0:T(8,128)(2,1)S(1)}, bf16[64,1024]{1,0:T(8,128)(2,1)S(1)}, u32[]{:S(2)}, u32[]{:S(2)}) collective-permute-start(bf16[64,1024]{1,0:T(8,128)(2,1)S(1)} %get-tuple-element.83), channel_id=1, source_target_pairs={{0,2},{1,3},{2,0},{3,1},{4,6},{5,7},{6,4},{7,5},{8,10},{9,11},{10,... | collective-permute-start | bytes 393224 | tf_op jit(solution)/shard_map/ppermute | solution.py:382
  58.8 9.1 %collective-permute-start.19 = (bf16[64,1024]{1,0:T(8,128)(2,1)S(1)}, bf16[64,1024]{1,0:T(8,128)(2,1)S(1)}, u32[]{:S(2)}, u32[]{:S(2)}) collective-permute-start(bf16[64,1024]{1,0:T(8,128)(2,1)S(1)} %add_convert_fusion.3), channel_id=1, source_target_pairs={{0,4},{1,5},{2,6},{3,7},{4,0},{5,1},{6,2},{7,3},{8,12},{9,13},{10,... | collective-permute-start | bytes 393224 | tf_op jit(solution)/shard_map/ppermute | solution.py:382
  60.3 7.8 %collective-permute-start.25 = (bf16[64,1024]{1,0:T(8,128)(2,1)S(1)}, bf16[64,1024]{1,0:T(8,128)(2,1)S(1)}, u32[]{:S(2)}, u32[]{:S(2)}) collective-permute-start(bf16[64,1024]{1,0:T(8,128)(2,1)S(1)} %add_convert_fusion), channel_id=1, source_target_pairs={{0,8},{1,9},{2,10},{3,11},{4,12},{5,13},{6,14},{7,15},{8,0},{9,1},... | collective-permute-start | bytes 393224 | tf_op jit(solution)/shard_map/ppermute | solution.py:382
  62.6 7.0 %collective-permute-start.18 = (bf16[128,1024]{1,0:T(8,128)(2,1)S(1)}, bf16[128,1024]{1,0:T(8,128)(2,1)S(1)}, u32[]{:S(2)}, u32[]{:S(2)}) collective-permute-start(bf16[128,1024]{1,0:T(8,128)(2,1)S(1)} %get-tuple-element.80), channel_id=1, source_target_pairs={{0,2},{1,3},{2,0},{3,1},{4,6},{5,7},{6,4},{7,5},{8,10},{9,11},{10,... | collective-permute-start | bytes 786440 | tf_op jit(solution)/shard_map/ppermute | solution.py:382
  64.1 5.4 %copy-start = (bf16[128,1024]{1,0:T(8,128)(2,1)S(1)}, bf16[128,1024]{1,0:T(8,128)(2,1)}, u32[]{:S(2)}) copy-start(bf16[128,1024]{1,0:T(8,128)(2,1)} %x_ref.1) | copy-start | bytes 786436
  64.1 5.4 %copy-start.1 = (s32[16384]{0:T(1024)S(1)}, s32[16384]{0:T(1024)}, u32[]{:S(2)}) copy-start(s32[16384]{0:T(1024)} %param.11) | copy-start | bytes 196612
  64.1 5.4 %copy-start.3 = (bf16[8,128]{1,0:T(8,128)(2,1)S(1)}, bf16[8,128]{1,0:T(8,128)(2,1)}, u32[]{:S(2)}) copy-start(bf16[8,128]{1,0:T(8,128)(2,1)} %s_ref.1) | copy-start | bytes 6148
  64.2 5.4 %collective-permute-start.21 = (bf16[64,1024]{1,0:T(8,128)(2,1)S(1)}, bf16[64,1024]{1,0:T(8,128)(2,1)S(1)}, u32[]{:S(2)}, u32[]{:S(2)}) collective-permute-start(bf16[64,1024]{1,0:T(8,128)(2,1)S(1)} %add_convert_fusion.2), channel_id=1, source_target_pairs={{0,4},{1,5},{2,6},{3,7},{4,0},{5,1},{6,2},{7,3},{8,12},{9,13},{10,... | collective-permute-start | bytes 393224 | tf_op jit(solution)/shard_map/ppermute | solution.py:382

commit v3 on v2

--- a/solution.py
+++ b/solution.py
@@ -175,12 +175,12 @@
 
 
 def unrotate_kernel(
-    me, x_hbm, s_hbm, sign_hbm, gain_hbm, u_ref, x, s, sign, gain, held, sems
+    me, x_hbm, s_ref, sign_hbm, gain_hbm, u_ref, x, sign, gain, held, sems
 ):
     per = sign.shape[0]
     at = pl.multiple_of(me[0] * per, per)
     copies = fetch(
-        ((gain_hbm, gain), (sign_hbm.at[pl.ds(at, per), :], sign), (s_hbm, s), (x_hbm, x)),
+        ((gain_hbm, gain), (sign_hbm.at[pl.ds(at, per), :], sign), (x_hbm, x)),
         sems,
     )
 
@@ -189,9 +189,8 @@
     held[...] = gain[...].astype(jnp.float32)
     copies[1].wait()
     sg = held[pl.ds(at, per), :] * ((2 * sign[...] - 1).astype(jnp.float32) / math.sqrt(BLK))
+    scale = s_ref[...].astype(jnp.float32).T
     copies[2].wait()
-    scale = s[...].astype(jnp.float32).T
-    copies[3].wait()
     tokens = x.shape[0]
     stacked = jnp.concatenate([x[:, b * BLK : (b + 1) * BLK] for b in range(per)], axis=0)
     turned = dot(stacked, had)
@@ -411,14 +410,13 @@
         unrotate_kernel,
         block,
         (me, x_coded, x_scales, sign2, gain2),
-        [SMEM] + [HBM] * 4,
+        [SMEM, HBM, VMEM, HBM, HBM],
         [
             pltpu.VMEM(x_coded.shape, bf16),
-            pltpu.VMEM(x_scales.shape, bf16),
             pltpu.VMEM((width // BLK, BLK), jnp.int32),
             pltpu.VMEM(gain2.shape, bf16),
             pltpu.VMEM(gain2.shape, f32),
-            dma((4,)),
+            dma((3,)),
         ],
     )
 

time: 71.4 us -> 72 us (level)
  transfers between devices with their start and end apart: 27 -> 27, of which waited for: 15 -> 15; matrix products, arithmetic and copies ran while one was open for 3% -> 2% of each run, Pallas kernels for 14% -> 14%
where the time goes in v3:
time: 72 us; the launch traced here: 71.7 us
  starting transfers between devices  32.8 us (46%)
  waiting for transfers between devices  21 us (29%)
  Pallas kernels  14.4 us (20%)
  other arithmetic  1.51 us (2%)
  local copies, waits for them, and re-layouts  0.99 us (1%)
  between operations  0.9 us (1%)
    ppermute x26, starting transfers between devices, swap(): return lax.ppermute(value, 'tensor', [(i, i ^ rel) for i in range(count)])  29.3 us
    ppermute x26, waiting for transfers between devices, swap(): return lax.ppermute(value, 'tensor', [(i, i ^ rel) for i in range(count)])  19.7 us
    pallas_call x15, Pallas kernels, call(): pl.pallas_call(kernel, out_shape=outs, in_specs=specs, out_specs=(VMEM,)...  14.4 us
    all_to_all x1, starting transfers between devices, paired(): kv = lax.all_to_all(kv, 'tensor', 0, 0, axis_index_groups=alike, tiled=True)  3.56 us
  transfers between devices with their start and end apart: 27, of which 15 were waited for; matrix products, arithmetic and copies ran while one was open for 2% of the time, Pallas kernels for 14%

profile of v3, /device:TPU:0, one launch (start us, length us, event | category | flops | bytes accessed | tf_op | source)
XLA Modules:
  0.0 71.7 jit_solution(8759174324804889497)
XLA Ops:
  0.6 0.0 copy-start.3
  0.6 0.7 copy-done.3
  1.3 1.2 %shard_map.104.u_ref.refs_0_ = bf16[128,1024]{1,0:T(8,128)(2,1)S(1)} custom-call(s32[1]{0:T(128)} %bitcast.me, bf16[128,1024]{1,0:T(8,128)(2,1)} %x_ref.1, bf16[8,128]{1,0:T(8,128)(2,1)S(1)} %copy-done.3, s32[128,128]{1,0:T(8,128)} %bitcast.17, bf16[128,128]{1,0:T(8,128)(2,1)} %bitcast.19), custom_call_target="tpu_custom_call" | custom-call | flops 1000000000 | bytes 1000000 | tf_op jit(solution)/shard_map/pallas_call | solution.py:159
  2.6 0.0 copy-start.5
  2.6 4.1 %collective-permute-start.5 = (bf16[128,1024]{1,0:T(8,128)(2,1)S(1)}, bf16[128,1024]{1,0:T(8,128)(2,1)S(1)}, u32[]{:S(2)}, u32[]{:S(2)}) collective-permute-start(bf16[128,1024]{1,0:T(8,128)(2,1)S(1)} %shard_map.104.u_ref.refs_0_), channel_id=1, source_target_pairs={{0,8},{1,9},{2,10},{3,11},{4,12},{5,13},{6,14},{7,15},{8,0},{9,1},... | collective-permute-start | bytes 786440 | tf_op jit(solution)/shard_map/ppermute | solution.py:381
  6.7 1.5 %collective-permute-start.3 = (bf16[128,1024]{1,0:T(8,128)(2,1)S(1)}, bf16[128,1024]{1,0:T(8,128)(2,1)S(1)}, u32[]{:S(2)}, u32[]{:S(2)}) collective-permute-start(bf16[128,1024]{1,0:T(8,128)(2,1)S(1)} %shard_map.104.u_ref.refs_0_), channel_id=1, source_target_pairs={{0,2},{1,3},{2,0},{3,1},{4,6},{5,7},{6,4},{7,5},{8,10},{9,11},{10,... | collective-permute-start | bytes 786440 | tf_op jit(solution)/shard_map/ppermute | solution.py:381
  8.2 1.6 %collective-permute-start = (bf16[128,1024]{1,0:T(8,128)(2,1)S(1)}, bf16[128,1024]{1,0:T(8,128)(2,1)S(1)}, u32[]{:S(2)}, u32[]{:S(2)}) collective-permute-start(bf16[128,1024]{1,0:T(8,128)(2,1)S(1)} %shard_map.104.u_ref.refs_0_), channel_id=1, source_target_pairs={{0,4},{1,5},{2,6},{3,7},{4,0},{5,1},{6,2},{7,3},{8,12},{9,13},{10,... | collective-permute-start | bytes 786440 | tf_op jit(solution)/shard_map/ppermute | solution.py:381
  9.8 2.7 %shard_map.105 = bf16[2,2,4,128,128]{4,3,2,1,0:T(8,128)(2,1)S(1)} custom-call(s32[1]{0:T(128)} %bitcast.me, bf16[128,1024]{1,0:T(8,128)(2,1)S(1)} %shard_map.104.u_ref.refs_0_, bf16[1024,1024]{1,0:T(8,128)(2,1)} %wk_hbm.1, bf16[1024,1024]{1,0:T(8,128)(2,1)} %wv_hbm.1), custom_call_target="tpu_custom_call" | custom-call | flops 20000000000 | bytes 1000000 | tf_op jit(solution)/shard_map/pallas_call | solution.py:159
  12.5 0.1 collective-permute-start.1
  12.6 0.5 collective-permute-start.4
  13.1 0.1 iota_add_fusion
  13.2 0.1 add.73.row_ref
  13.3 0.1 add.83.col_ref
  13.3 0.1 convert_element_type.94
  13.4 0.3 fusion.2
  13.8 0.1 pad_maximum_fusion
  13.9 0.2 collective-permute-done.1
  14.1 0.1 fusion
  14.2 0.6 collective-permute-start.2
  14.8 5.3 %collective-permute-done.refs_1_.refs_2_ = bf16[128,1024]{1,0:T(8,128)(2,1)S(1)} collective-permute-done((bf16[128,1024]{1,0:T(8,128)(2,1)S(1)}, bf16[128,1024]{1,0:T(8,128)(2,1)S(1)}, u32[]{:S(2)}, u32[]{:S(2)}) %collective-permute-start) | collective-permute-done | bytes 262176 | tf_op jit(solution)/shard_map/ppermute | solution.py:381
  20.1 0.3 collective-permute-done.4.x_hbm
  20.4 0.5 collective-permute-start.7
  21.0 1.0 %collective-permute-start.6 = (bf16[128,1024]{1,0:T(8,128)(2,1)S(1)}, bf16[128,1024]{1,0:T(8,128)(2,1)S(1)}, u32[]{:S(2)}, u32[]{:S(2)}) collective-permute-start(bf16[128,1024]{1,0:T(8,128)(2,1)S(1)} %collective-permute-done.5.refs_1_.refs_0_), channel_id=1, source_target_pairs={{0,4},{1,5},{2,6},{3,7},{4,0},{5,1},{6,2},{7,3},{8,12},{9,13},{10,... | collective-permute-start | bytes 786440 | tf_op jit(solution)/shard_map/ppermute | solution.py:381
  22.0 1.9 %shard_map.108.before_ref = f32[128,384]{1,0:T(8,128)S(1)} custom-call(s32[1]{0:T(128)} %bitcast.me, f32[8,128]{1,0:T(8,128)S(1)} %shard_map.107.token, bf16[128,128]{1,0:T(8,128)(2,1)S(1)} %bitcast.20, bf16[16384,128]{1,0:T(8,128)(2,1)} %w_hbm.5, bf16[16384,128]{1,0:T(8,128)(2,1)} %collective-permute-done.4.x_hbm, ...), custom_call_target="tpu_custom_call" | custom-call | flops 10000000000 | bytes 1000000 | tf_op jit(solution)/shard_map/pallas_call | solution.py:159
  23.9 0.7 fusion.1
  24.6 3.6 %all-to-all-start = ((bf16[4,128,128]{2,1,0:T(8,128)(2,1)}), bf16[4,128,128]{2,1,0:T(8,128)(2,1)S(1)}, u32[]{:S(2)}, u32[]{:S(2)}) async-start(bf16[4,128,128]{2,1,0:T(8,128)(2,1)} %fusion.1), calls=%async_computation | async-start | bytes 262144 | tf_op jit(solution)/shard_map/all_to_all | solution.py:464
  28.2 0.6 collective-permute-done.7.refs_1_
  28.8 0.2 collective-permute-done.6.refs_0_.refs_2_
  29.0 1.2 %collective-permute-start.10 = (bf16[128,1024]{1,0:T(8,128)(2,1)S(1)}, bf16[128,1024]{1,0:T(8,128)(2,1)S(1)}, u32[]{:S(2)}, u32[]{:S(2)}) collective-permute-start(bf16[128,1024]{1,0:T(8,128)(2,1)S(1)} %collective-permute-done.3.refs_0_.refs_1_), channel_id=1, source_target_pairs={{0,4},{1,5},{2,6},{3,7},{4,0},{5,1},{6,2},{7,3},{8,12},{9,13},{10,... | collective-permute-start | bytes 786440 | tf_op jit(solution)/shard_map/ppermute | solution.py:381
  30.3 1.0 %collective-permute-start.9 = (bf16[128,1024]{1,0:T(8,128)(2,1)S(1)}, bf16[128,1024]{1,0:T(8,128)(2,1)S(1)}, u32[]{:S(2)}, u32[]{:S(2)}) collective-permute-start(bf16[128,1024]{1,0:T(8,128)(2,1)S(1)} %collective-permute-done.6.refs_0_.refs_2_), channel_id=1, source_target_pairs={{0,2},{1,3},{2,0},{3,1},{4,6},{5,7},{6,4},{7,5},{8,10},{9,11},{10,... | collective-permute-start | bytes 786440 | tf_op jit(solution)/shard_map/ppermute | solution.py:381
  31.3 1.8 %shard_map.110 = (f32[128,384]{1,0:T(8,128)S(1)}, bf16[2,1024,256]{2,1,0:T(8,128)(2,1)S(1)}) custom-call(s32[1]{0:T(128)} %bitcast.me, f32[8,128]{1,0:T(8,128)S(1)} %shard_map.109.done, bf16[128,128]{1,0:T(8,128)(2,1)S(1)} %bitcast.21, bf16[16384,128]{1,0:T(8,128)(2,1)} %w_hbm.5, bf16[16384,128]{1,0:T(8,128)(2,1)} %collective-permute-done.4.x_hbm, ...), custom_call_target="tpu_custom_call" | custom-call | flops 20000000000 | bytes 1000000 | tf_op jit(solution)/shard_map/pallas_call | solution.py:159
  33.1 1.3 %all-to-all-done = bf16[4,128,128]{2,1,0:T(8,128)(2,1)S(1)} async-done(((bf16[4,128,128]{2,1,0:T(8,128)(2,1)}), bf16[4,128,128]{2,1,0:T(8,128)(2,1)S(1)}, u32[]{:S(2)}, u32[]{:S(2)}) %all-to-all-start) | async-done | bytes 131104 | tf_op jit(solution)/shard_map/all_to_all | solution.py:464
  34.4 0.1 collective-permute-start.8
  34.5 4.2 %collective-permute-done.10.refs_1_.refs_0_ = bf16[128,1024]{1,0:T(8,128)(2,1)S(1)} collective-permute-done((bf16[128,1024]{1,0:T(8,128)(2,1)S(1)}, bf16[128,1024]{1,0:T(8,128)(2,1)S(1)}, u32[]{:S(2)}, u32[]{:S(2)}) %collective-permute-start.10) | collective-permute-done | bytes 262176 | tf_op jit(solution)/shard_map/ppermute | solution.py:381
  38.8 0.3 shard_map.114.pay_ref
  39.1 0.1 collective-permute-start.11
  39.2 1.4 %collective-permute-done.11.got_ref = f32[128,384]{1,0:T(8,128)S(1)} collective-permute-done((f32[128,384]{1,0:T(8,128)S(1)}, f32[128,384]{1,0:T(8,128)S(1)}, u32[]{:S(2)}, u32[]{:S(2)}) %collective-permute-start.11) | collective-permute-done | bytes 196640 | tf_op jit(solution)/shard_map/ppermute | solution.py:381
  40.6 1.8 %shard_map.115 = (bf16[128,256]{1,0:T(8,128)(2,1)S(1)}, bf16[64,1024]{1,0:T(8,128)(2,1)S(1)}, bf16[64,1024]{1,0:T(8,128)(2,1)S(1)}) custom-call(s32[1]{0:T(128)} %bitcast.me, f32[8,128]{1,0:T(8,128)S(1)} %shard_map.111.done, f32[128,384]{1,0:T(8,128)S(1)} %shard_map.114.pay_ref, f32[128,384]{1,0:T(8,128)S(1)} %collective-permute-done.11.got_ref, ...), custom_call_target="tpu_custom_call" | custom-call | flops 1000000000 | bytes 1000000 | tf_op jit(solution)/shard_map/pallas_call | solution.py:159
  42.4 1.1 %collective-permute-start.13 = (bf16[64,1024]{1,0:T(8,128)(2,1)S(1)}, bf16[64,1024]{1,0:T(8,128)(2,1)S(1)}, u32[]{:S(2)}, u32[]{:S(2)}) collective-permute-start(bf16[64,1024]{1,0:T(8,128)(2,1)S(1)} %get-tuple-element.68), channel_id=1, source_target_pairs={{0,2},{1,3},{2,0},{3,1},{4,6},{5,7},{6,4},{7,5},{8,10},{9,11},{10,... | collective-permute-start | bytes 393224 | tf_op jit(solution)/shard_map/ppermute | solution.py:381
  43.5 1.0 %collective-permute-start.22 = (bf16[64,1024]{1,0:T(8,128)(2,1)S(1)}, bf16[64,1024]{1,0:T(8,128)(2,1)S(1)}, u32[]{:S(2)}, u32[]{:S(2)}) collective-permute-start(bf16[64,1024]{1,0:T(8,128)(2,1)S(1)} %get-tuple-element.85), channel_id=1, source_target_pairs={{0,2},{1,3},{2,0},{3,1},{4,6},{5,7},{6,4},{7,5},{8,10},{9,11},{10,... | collective-permute-start | bytes 393224 | tf_op jit(solution)/shard_map/ppermute | solution.py:381
  44.5 3.2 %shard_map.116 = (bf16[64,1024]{1,0:T(8,128)(2,1)S(1)}, bf16[64,1024]{1,0:T(8,128)(2,1)S(1)}, bf16[64,1024]{1,0:T(8,128)(2,1)S(1)}, bf16[64,1024]{1,0:T(8,128)(2...) custom-call(s32[1]{0:T(128)} %bitcast.me, ...), custom_call_target="tpu_custom_call" | custom-call | flops 20000000000 | bytes 1000000 | tf_op jit(solution)/shard_map/pallas_call | solution.py:159
  47.7 1.2 %collective-permute-done.13 = bf16[64,1024]{1,0:T(8,128)(2,1)S(1)} collective-permute-done((bf16[64,1024]{1,0:T(8,128)(2,1)S(1)}, bf16[64,1024]{1,0:T(8,128)(2,1)S(1)}, u32[]{:S(2)}, u32[]{:S(2)}) %collective-permute-start.13) | collective-permute-done | bytes 131104 | tf_op jit(solution)/shard_map/ppermute | solution.py:381
  48.9 0.4 collective-permute-start.14
  49.2 1.0 %collective-permute-start.15 = (bf16[64,1024]{1,0:T(8,128)(2,1)S(1)}, bf16[64,1024]{1,0:T(8,128)(2,1)S(1)}, u32[]{:S(2)}, u32[]{:S(2)}) collective-permute-start(bf16[64,1024]{1,0:T(8,128)(2,1)S(1)} %get-tuple-element.73), channel_id=1, source_target_pairs={{0,2},{1,3},{2,0},{3,1},{4,6},{5,7},{6,4},{7,5},{8,10},{9,11},{10,... | collective-permute-start | bytes 393224 | tf_op jit(solution)/shard_map/ppermute | solution.py:381
  50.2 1.0 %collective-permute-start.17 = (bf16[64,1024]{1,0:T(8,128)(2,1)S(1)}, bf16[64,1024]{1,0:T(8,128)(2,1)S(1)}, u32[]{:S(2)}, u32[]{:S(2)}) collective-permute-start(bf16[64,1024]{1,0:T(8,128)(2,1)S(1)} %get-tuple-element.78), channel_id=1, source_target_pairs={{0,2},{1,3},{2,0},{3,1},{4,6},{5,7},{6,4},{7,5},{8,10},{9,11},{10,... | collective-permute-start | bytes 393224 | tf_op jit(solution)/shard_map/ppermute | solution.py:381
  51.2 0.2 collective-permute-done.22
  51.5 1.1 %collective-permute-start.23 = (bf16[64,1024]{1,0:T(8,128)(2,1)S(1)}, bf16[64,1024]{1,0:T(8,128)(2,1)S(1)}, u32[]{:S(2)}, u32[]{:S(2)}) collective-permute-start(bf16[64,1024]{1,0:T(8,128)(2,1)S(1)} %get-tuple-element.87), channel_id=1, source_target_pairs={{0,2},{1,3},{2,0},{3,1},{4,6},{5,7},{6,4},{7,5},{8,10},{9,11},{10,... | collective-permute-start | bytes 393224 | tf_op jit(solution)/shard_map/ppermute | solution.py:381
  52.6 1.6 %collective-permute-start.24 = (bf16[64,1024]{1,0:T(8,128)(2,1)S(1)}, bf16[64,1024]{1,0:T(8,128)(2,1)S(1)}, u32[]{:S(2)}, u32[]{:S(2)}) collective-permute-start(bf16[64,1024]{1,0:T(8,128)(2,1)S(1)} %add_convert_fusion.1), channel_id=1, source_target_pairs={{0,4},{1,5},{2,6},{3,7},{4,0},{5,1},{6,2},{7,3},{8,12},{9,13},{10,... | collective-permute-start | bytes 393224 | tf_op jit(solution)/shard_map/ppermute | solution.py:381
  54.1 0.0 collective-permute-done.14
  54.1 1.5 %collective-permute-done.15 = bf16[64,1024]{1,0:T(8,128)(2,1)S(1)} collective-permute-done((bf16[64,1024]{1,0:T(8,128)(2,1)S(1)}, bf16[64,1024]{1,0:T(8,128)(2,1)S(1)}, u32[]{:S(2)}, u32[]{:S(2)}) %collective-permute-start.15) | collective-permute-done | bytes 131104 | tf_op jit(solution)/shard_map/ppermute | solution.py:381
  55.6 0.1 add_convert_fusion.4
  55.7 2.7 %collective-permute-start.16 = (bf16[64,1024]{1,0:T(8,128)(2,1)S(1)}, bf16[64,1024]{1,0:T(8,128)(2,1)S(1)}, u32[]{:S(2)}, u32[]{:S(2)}) collective-permute-start(bf16[64,1024]{1,0:T(8,128)(2,1)S(1)} %add_convert_fusion.4), channel_id=1, source_target_pairs={{0,8},{1,9},{2,10},{3,11},{4,12},{5,13},{6,14},{7,15},{8,0},{9,1},... | collective-permute-start | bytes 393224 | tf_op jit(solution)/shard_map/ppermute | solution.py:381
  58.4 1.0 %collective-permute-start.20 = (bf16[64,1024]{1,0:T(8,128)(2,1)S(1)}, bf16[64,1024]{1,0:T(8,128)(2,1)S(1)}, u32[]{:S(2)}, u32[]{:S(2)}) collective-permute-start(bf16[64,1024]{1,0:T(8,128)(2,1)S(1)} %get-tuple-element.83), channel_id=1, source_target_pairs={{0,2},{1,3},{2,0},{3,1},{4,6},{5,7},{6,4},{7,5},{8,10},{9,11},{10,... | collective-permute-start | bytes 393224 | tf_op jit(solution)/shard_map/ppermute | solution.py:381
  59.4 1.5 %collective-permute-start.19 = (bf16[64,1024]{1,0:T(8,128)(2,1)S(1)}, bf16[64,1024]{1,0:T(8,128)(2,1)S(1)}, u32[]{:S(2)}, u32[]{:S(2)}) collective-permute-start(bf16[64,1024]{1,0:T(8,128)(2,1)S(1)} %add_convert_fusion.3), channel_id=1, source_target_pairs={{0,4},{1,5},{2,6},{3,7},{4,0},{5,1},{6,2},{7,3},{8,12},{9,13},{10,... | collective-permute-start | bytes 393224 | tf_op jit(solution)/shard_map/ppermute | solution.py:381
  60.9 0.1 add_convert_fusion
  61.0 2.3 %collective-permute-start.25 = (bf16[64,1024]{1,0:T(8,128)(2,1)S(1)}, bf16[64,1024]{1,0:T(8,128)(2,1)S(1)}, u32[]{:S(2)}, u32[]{:S(2)}) collective-permute-start(bf16[64,1024]{1,0:T(8,128)(2,1)S(1)} %add_convert_fusion), channel_id=1, source_target_pairs={{0,8},{1,9},{2,10},{3,11},{4,12},{5,13},{6,14},{7,15},{8,0},{9,1},... | collective-permute-start | bytes 393224 | tf_op jit(solution)/shard_map/ppermute | solution.py:381
  63.3 1.0 %collective-permute-start.18 = (bf16[128,1024]{1,0:T(8,128)(2,1)S(1)}, bf16[128,1024]{1,0:T(8,128)(2,1)S(1)}, u32[]{:S(2)}, u32[]{:S(2)}) collective-permute-start(bf16[128,1024]{1,0:T(8,128)(2,1)S(1)} %get-tuple-element.80), channel_id=1, source_target_pairs={{0,2},{1,3},{2,0},{3,1},{4,6},{5,7},{6,4},{7,5},{8,10},{9,11},{10,... | collective-permute-start | bytes 786440 | tf_op jit(solution)/shard_map/ppermute | solution.py:381
  64.2 0.5 collective-permute-done.20
  64.8 0.0 copy-start.4
  64.8 1.5 %collective-permute-start.21 = (bf16[64,1024]{1,0:T(8,128)(2,1)S(1)}, bf16[64,1024]{1,0:T(8,128)(2,1)S(1)}, u32[]{:S(2)}, u32[]{:S(2)}) collective-permute-start(bf16[64,1024]{1,0:T(8,128)(2,1)S(1)} %add_convert_fusion.2), channel_id=1, source_target_pairs={{0,4},{1,5},{2,6},{3,7},{4,0},{5,1},{6,2},{7,3},{8,12},{9,13},{10,... | collective-permute-start | bytes 393224 | tf_op jit(solution)/shard_map/ppermute | solution.py:381
  66.3 2.3 %collective-permute-done.19.refs_2_ = bf16[64,1024]{1,0:T(8,128)(2,1)S(1)} collective-permute-done((bf16[64,1024]{1,0:T(8,128)(2,1)S(1)}, bf16[64,1024]{1,0:T(8,128)(2,1)S(1)}, u32[]{:S(2)}, u32[]{:S(2)}) %collective-permute-start.19) | collective-permute-done | bytes 131104 | tf_op jit(solution)/shard_map/ppermute | solution.py:381
  68.6 0.2 collective-permute-done.25.refs_4_
  68.8 1.4 %collective-permute-done.21.refs_3_ = bf16[64,1024]{1,0:T(8,128)(2,1)S(1)} collective-permute-done((bf16[64,1024]{1,0:T(8,128)(2,1)S(1)}, bf16[64,1024]{1,0:T(8,128)(2,1)S(1)}, u32[]{:S(2)}, u32[]{:S(2)}) %collective-permute-start.21) | collective-permute-done | bytes 131104 | tf_op jit(solution)/shard_map/ppermute | solution.py:381
  70.2 1.5 %shard_map.118 = (bf16[128,1024]{1,0:T(8,128)(2,1)}, bf16[8,128]{1,0:T(8,128)(2,1)}) custom-call(s32[1]{0:T(128)} %bitcast.me, f32[8,128]{1,0:T(8,128)S(1)} %shard_map.117.done, bf16[128,1024]{1,0:T(8,128)(2,1)S(1)} %copy-done, bf16[8,128]{1,0:T(8,128)(2,1)S(1)} %copy-done.4, s32[128,128]{1,0:T(8,128)S(1)} %bitcast.18, ...), custom_call_target="tpu_custom_call" | custom-call | flops 1000000000 | bytes 1000000 | tf_op jit(solution)/shard_map/pallas_call | solution.py:159
  (36 shorter events, 0.2 us)
Async XLA Ops:
  0.6 0.7 copy-start.3
  2.6 10.5 %copy-start.5 = (s32[16]{0:T(128)S(1)}, s32[16]{0:T(128)}, u32[]{:S(2)}) copy-start(s32[16]{0:T(128)} %param.12) | copy-start | bytes 196
  2.6 17.5 %collective-permute-start.5 = (bf16[128,1024]{1,0:T(8,128)(2,1)S(1)}, bf16[128,1024]{1,0:T(8,128)(2,1)S(1)}, u32[]{:S(2)}, u32[]{:S(2)}) collective-permute-start(bf16[128,1024]{1,0:T(8,128)(2,1)S(1)} %shard_map.104.u_ref.refs_0_), channel_id=1, source_target_pairs={{0,8},{1,9},{2,10},{3,11},{4,12},{5,13},{6,14},{7,15},{8,0},{9,1},... | collective-permute-start | bytes 786440 | tf_op jit(solution)/shard_map/ppermute | solution.py:381
  6.7 8.1 %collective-permute-start.3 = (bf16[128,1024]{1,0:T(8,128)(2,1)S(1)}, bf16[128,1024]{1,0:T(8,128)(2,1)S(1)}, u32[]{:S(2)}, u32[]{:S(2)}) collective-permute-start(bf16[128,1024]{1,0:T(8,128)(2,1)S(1)} %shard_map.104.u_ref.refs_0_), channel_id=1, source_target_pairs={{0,2},{1,3},{2,0},{3,1},{4,6},{5,7},{6,4},{7,5},{8,10},{9,11},{10,... | collective-permute-start | bytes 786440 | tf_op jit(solution)/shard_map/ppermute | solution.py:381
  8.2 11.9 %collective-permute-start = (bf16[128,1024]{1,0:T(8,128)(2,1)S(1)}, bf16[128,1024]{1,0:T(8,128)(2,1)S(1)}, u32[]{:S(2)}, u32[]{:S(2)}) collective-permute-start(bf16[128,1024]{1,0:T(8,128)(2,1)S(1)} %shard_map.104.u_ref.refs_0_), channel_id=1, source_target_pairs={{0,4},{1,5},{2,6},{3,7},{4,0},{5,1},{6,2},{7,3},{8,12},{9,13},{10,... | collective-permute-start | bytes 786440 | tf_op jit(solution)/shard_map/ppermute | solution.py:381
  12.5 1.6 %collective-permute-start.1 = (bf16[2,4,128,128]{3,2,1,0:T(8,128)(2,1)S(1)}, bf16[2,4,128,128]{3,2,1,0:T(8,128)(2,1)S(1)}, u32[]{:S(2)}, u32[]{:S(2)}) collective-permute-start(bf16[2,4,128,128]{3,2,1,0:T(8,128)(2,1)S(1)} %slice_bitcast_fusion), channel_id=1, source_target_pairs={{0,1},{1,0},{2,3},{3,2},{4,5},{5,4},{6,7},{7,6},{8,9},{9,8},{10,11... | collective-permute-start | bytes 786440 | tf_op jit(solution)/shard_map/ppermute | solution.py:381
  12.6 7.9 %collective-permute-start.4 = (bf16[16384,128]{1,0:T(8,128)(2,1)}, bf16[16384,128]{1,0:T(8,128)(2,1)}, u32[]{:S(2)}, u32[]{:S(2)}) collective-permute-start(bf16[16384,128]{1,0:T(8,128)(2,1)} %w_hbm.5), channel_id=1, source_target_pairs={{0,1},{1,0},{2,3},{3,2},{4,5},{5,4},{6,7},{7,6},{8,9},{9,8},{10,11... | collective-permute-start | bytes 12582920 | tf_op jit(solution)/shard_map/ppermute | solution.py:381
  14.2 5.9 %collective-permute-start.2 = (bf16[4,128,128]{2,1,0:T(8,128)(2,1)S(1)}, bf16[4,128,128]{2,1,0:T(8,128)(2,1)S(1)}, u32[]{:S(2)}, u32[]{:S(2)}) collective-permute-start(bf16[4,128,128]{2,1,0:T(8,128)(2,1)S(1)} %slice_bitcast_fusion.3), channel_id=1, source_target_pairs={{0,2},{1,3},{2,0},{3,1},{4,6},{5,7},{6,4},{7,5},{8,10},{9,11},{10,... | collective-permute-start | bytes 393224 | tf_op jit(solution)/shard_map/ppermute | solution.py:381
  20.1 1.9 %copy-start.2 = (bf16[16384]{0:T(1024)(128)(2,1)S(1)}, bf16[16384]{0:T(1024)(128)(2,1)}, u32[]{:S(2)}) copy-start(bf16[16384]{0:T(1024)(128)(2,1)} %param.13) | copy-start | bytes 98308
  20.4 8.3 %collective-permute-start.7 = (bf16[128,1024]{1,0:T(8,128)(2,1)S(1)}, bf16[128,1024]{1,0:T(8,128)(2,1)S(1)}, u32[]{:S(2)}, u32[]{:S(2)}) collective-permute-start(bf16[128,1024]{1,0:T(8,128)(2,1)S(1)} %collective-permute-done.5.refs_1_.refs_0_), channel_id=1, source_target_pairs={{0,2},{1,3},{2,0},{3,1},{4,6},{5,7},{6,4},{7,5},{8,10},{9,11},{10,... | collective-permute-start | bytes 786440 | tf_op jit(solution)/shard_map/ppermute | solution.py:381
  21.0 8.1 %collective-permute-start.6 = (bf16[128,1024]{1,0:T(8,128)(2,1)S(1)}, bf16[128,1024]{1,0:T(8,128)(2,1)S(1)}, u32[]{:S(2)}, u32[]{:S(2)}) collective-permute-start(bf16[128,1024]{1,0:T(8,128)(2,1)S(1)} %collective-permute-done.5.refs_1_.refs_0_), channel_id=1, source_target_pairs={{0,4},{1,5},{2,6},{3,7},{4,0},{5,1},{6,2},{7,3},{8,12},{9,13},{10,... | collective-permute-start | bytes 786440 | tf_op jit(solution)/shard_map/ppermute | solution.py:381
  24.6 9.8 %all-to-all-start = ((bf16[4,128,128]{2,1,0:T(8,128)(2,1)}), bf16[4,128,128]{2,1,0:T(8,128)(2,1)S(1)}, u32[]{:S(2)}, u32[]{:S(2)}) async-start(bf16[4,128,128]{2,1,0:T(8,128)(2,1)} %fusion.1), calls=%async_computation | async-start | bytes 262144 | tf_op jit(solution)/shard_map/all_to_all | solution.py:464
  28.1 12.5 %collective-permute-start.12 = (bf16[128,16384]{1,0:T(8,128)(2,1)}, bf16[128,16384]{1,0:T(8,128)(2,1)}, u32[]{:S(2)}, u32[]{:S(2)}) collective-permute-start(bf16[128,16384]{1,0:T(8,128)(2,1)} %w_hbm.7), channel_id=1, source_target_pairs={{0,1},{1,0},{2,3},{3,2},{4,5},{5,4},{6,7},{7,6},{8,9},{9,8},{10,11... | collective-permute-start | bytes 12582920 | tf_op jit(solution)/shard_map/ppermute | solution.py:381
  29.0 9.7 %collective-permute-start.10 = (bf16[128,1024]{1,0:T(8,128)(2,1)S(1)}, bf16[128,1024]{1,0:T(8,128)(2,1)S(1)}, u32[]{:S(2)}, u32[]{:S(2)}) collective-permute-start(bf16[128,1024]{1,0:T(8,128)(2,1)S(1)} %collective-permute-done.3.refs_0_.refs_1_), channel_id=1, source_target_pairs={{0,4},{1,5},{2,6},{3,7},{4,0},{5,1},{6,2},{7,3},{8,12},{9,13},{10,... | collective-permute-start | bytes 786440 | tf_op jit(solution)/shard_map/ppermute | solution.py:381
  30.3 8.5 %collective-permute-start.9 = (bf16[128,1024]{1,0:T(8,128)(2,1)S(1)}, bf16[128,1024]{1,0:T(8,128)(2,1)S(1)}, u32[]{:S(2)}, u32[]{:S(2)}) collective-permute-start(bf16[128,1024]{1,0:T(8,128)(2,1)S(1)} %collective-permute-done.6.refs_0_.refs_2_), channel_id=1, source_target_pairs={{0,2},{1,3},{2,0},{3,1},{4,6},{5,7},{6,4},{7,5},{8,10},{9,11},{10,... | collective-permute-start | bytes 786440 | tf_op jit(solution)/shard_map/ppermute | solution.py:381
  34.4 4.7 %collective-permute-start.8 = (bf16[128,128]{1,0:T(8,128)(2,1)S(1)}, bf16[128,128]{1,0:T(8,128)(2,1)S(1)}, u32[]{:S(2)}, u32[]{:S(2)}) collective-permute-start(bf16[128,128]{1,0:T(8,128)(2,1)S(1)} %reduce_sum.12.kv_ref), channel_id=1, source_target_pairs={{0,1},{1,0},{2,3},{3,2},{4,5},{5,4},{6,7},{7,6},{8,9},{9,8},{10,11... | collective-permute-start | bytes 98312 | tf_op jit(solution)/shard_map/ppermute | solution.py:381
  39.1 1.5 %collective-permute-start.11 = (f32[128,384]{1,0:T(8,128)S(1)}, f32[128,384]{1,0:T(8,128)S(1)}, u32[]{:S(2)}, u32[]{:S(2)}) collective-permute-start(f32[128,384]{1,0:T(8,128)S(1)} %shard_map.114.pay_ref), channel_id=1, source_target_pairs={{0,1},{1,0},{2,3},{3,2},{4,5},{5,4},{6,7},{7,6},{8,9},{9,8},{10,11... | collective-permute-start | bytes 589832 | tf_op jit(solution)/shard_map/ppermute | solution.py:381
  42.4 6.4 %collective-permute-start.13 = (bf16[64,1024]{1,0:T(8,128)(2,1)S(1)}, bf16[64,1024]{1,0:T(8,128)(2,1)S(1)}, u32[]{:S(2)}, u32[]{:S(2)}) collective-permute-start(bf16[64,1024]{1,0:T(8,128)(2,1)S(1)} %get-tuple-element.68), channel_id=1, source_target_pairs={{0,2},{1,3},{2,0},{3,1},{4,6},{5,7},{6,4},{7,5},{8,10},{9,11},{10,... | collective-permute-start | bytes 393224 | tf_op jit(solution)/shard_map/ppermute | solution.py:381
  43.5 8.0 %collective-permute-start.22 = (bf16[64,1024]{1,0:T(8,128)(2,1)S(1)}, bf16[64,1024]{1,0:T(8,128)(2,1)S(1)}, u32[]{:S(2)}, u32[]{:S(2)}) collective-permute-start(bf16[64,1024]{1,0:T(8,128)(2,1)S(1)} %get-tuple-element.85), channel_id=1, source_target_pairs={{0,2},{1,3},{2,0},{3,1},{4,6},{5,7},{6,4},{7,5},{8,10},{9,11},{10,... | collective-permute-start | bytes 393224 | tf_op jit(solution)/shard_map/ppermute | solution.py:381
  48.9 5.3 %collective-permute-start.14 = (bf16[64,1024]{1,0:T(8,128)(2,1)S(1)}, bf16[64,1024]{1,0:T(8,128)(2,1)S(1)}, u32[]{:S(2)}, u32[]{:S(2)}) collective-permute-start(bf16[64,1024]{1,0:T(8,128)(2,1)S(1)} %add_convert_fusion.5), channel_id=1, source_target_pairs={{0,4},{1,5},{2,6},{3,7},{4,0},{5,1},{6,2},{7,3},{8,12},{9,13},{10,... | collective-permute-start | bytes 393224 | tf_op jit(solution)/shard_map/ppermute | solution.py:381
  49.2 6.4 %collective-permute-start.15 = (bf16[64,1024]{1,0:T(8,128)(2,1)S(1)}, bf16[64,1024]{1,0:T(8,128)(2,1)S(1)}, u32[]{:S(2)}, u32[]{:S(2)}) collective-permute-start(bf16[64,1024]{1,0:T(8,128)(2,1)S(1)} %get-tuple-element.73), channel_id=1, source_target_pairs={{0,2},{1,3},{2,0},{3,1},{4,6},{5,7},{6,4},{7,5},{8,10},{9,11},{10,... | collective-permute-start | bytes 393224 | tf_op jit(solution)/shard_map/ppermute | solution.py:381
  50.2 9.2 %collective-permute-start.17 = (bf16[64,1024]{1,0:T(8,128)(2,1)S(1)}, bf16[64,1024]{1,0:T(8,128)(2,1)S(1)}, u32[]{:S(2)}, u32[]{:S(2)}) collective-permute-start(bf16[64,1024]{1,0:T(8,128)(2,1)S(1)} %get-tuple-element.78), channel_id=1, source_target_pairs={{0,2},{1,3},{2,0},{3,1},{4,6},{5,7},{6,4},{7,5},{8,10},{9,11},{10,... | collective-permute-start | bytes 393224 | tf_op jit(solution)/shard_map/ppermute | solution.py:381
  51.5 9.5 %collective-permute-start.23 = (bf16[64,1024]{1,0:T(8,128)(2,1)S(1)}, bf16[64,1024]{1,0:T(8,128)(2,1)S(1)}, u32[]{:S(2)}, u32[]{:S(2)}) collective-permute-start(bf16[64,1024]{1,0:T(8,128)(2,1)S(1)} %get-tuple-element.87), channel_id=1, source_target_pairs={{0,2},{1,3},{2,0},{3,1},{4,6},{5,7},{6,4},{7,5},{8,10},{9,11},{10,... | collective-permute-start | bytes 393224 | tf_op jit(solution)/shard_map/ppermute | solution.py:381
  52.6 8.4 %collective-permute-start.24 = (bf16[64,1024]{1,0:T(8,128)(2,1)S(1)}, bf16[64,1024]{1,0:T(8,128)(2,1)S(1)}, u32[]{:S(2)}, u32[]{:S(2)}) collective-permute-start(bf16[64,1024]{1,0:T(8,128)(2,1)S(1)} %add_convert_fusion.1), channel_id=1, source_target_pairs={{0,4},{1,5},{2,6},{3,7},{4,0},{5,1},{6,2},{7,3},{8,12},{9,13},{10,... | collective-permute-start | bytes 393224 | tf_op jit(solution)/shard_map/ppermute | solution.py:381
  55.7 10.6 %collective-permute-start.16 = (bf16[64,1024]{1,0:T(8,128)(2,1)S(1)}, bf16[64,1024]{1,0:T(8,128)(2,1)S(1)}, u32[]{:S(2)}, u32[]{:S(2)}) collective-permute-start(bf16[64,1024]{1,0:T(8,128)(2,1)S(1)} %add_convert_fusion.4), channel_id=1, source_target_pairs={{0,8},{1,9},{2,10},{3,11},{4,12},{5,13},{6,14},{7,15},{8,0},{9,1},... | collective-permute-start | bytes 393224 | tf_op jit(solution)/shard_map/ppermute | solution.py:381
  58.4 6.4 %collective-permute-start.20 = (bf16[64,1024]{1,0:T(8,128)(2,1)S(1)}, bf16[64,1024]{1,0:T(8,128)(2,1)S(1)}, u32[]{:S(2)}, u32[]{:S(2)}) collective-permute-start(bf16[64,1024]{1,0:T(8,128)(2,1)S(1)} %get-tuple-element.83), channel_id=1, source_target_pairs={{0,2},{1,3},{2,0},{3,1},{4,6},{5,7},{6,4},{7,5},{8,10},{9,11},{10,... | collective-permute-start | bytes 393224 | tf_op jit(solution)/shard_map/ppermute | solution.py:381
  59.4 9.1 %collective-permute-start.19 = (bf16[64,1024]{1,0:T(8,128)(2,1)S(1)}, bf16[64,1024]{1,0:T(8,128)(2,1)S(1)}, u32[]{:S(2)}, u32[]{:S(2)}) collective-permute-start(bf16[64,1024]{1,0:T(8,128)(2,1)S(1)} %add_convert_fusion.3), channel_id=1, source_target_pairs={{0,4},{1,5},{2,6},{3,7},{4,0},{5,1},{6,2},{7,3},{8,12},{9,13},{10,... | collective-permute-start | bytes 393224 | tf_op jit(solution)/shard_map/ppermute | solution.py:381
  61.0 7.8 %collective-permute-start.25 = (bf16[64,1024]{1,0:T(8,128)(2,1)S(1)}, bf16[64,1024]{1,0:T(8,128)(2,1)S(1)}, u32[]{:S(2)}, u32[]{:S(2)}) collective-permute-start(bf16[64,1024]{1,0:T(8,128)(2,1)S(1)} %add_convert_fusion), channel_id=1, source_target_pairs={{0,8},{1,9},{2,10},{3,11},{4,12},{5,13},{6,14},{7,15},{8,0},{9,1},... | collective-permute-start | bytes 393224 | tf_op jit(solution)/shard_map/ppermute | solution.py:381
  63.3 6.9 %collective-permute-start.18 = (bf16[128,1024]{1,0:T(8,128)(2,1)S(1)}, bf16[128,1024]{1,0:T(8,128)(2,1)S(1)}, u32[]{:S(2)}, u32[]{:S(2)}) collective-permute-start(bf16[128,1024]{1,0:T(8,128)(2,1)S(1)} %get-tuple-element.80), channel_id=1, source_target_pairs={{0,2},{1,3},{2,0},{3,1},{4,6},{5,7},{6,4},{7,5},{8,10},{9,11},{10,... | collective-permute-start | bytes 786440 | tf_op jit(solution)/shard_map/ppermute | solution.py:381
  64.8 5.4 %copy-start = (bf16[128,1024]{1,0:T(8,128)(2,1)S(1)}, bf16[128,1024]{1,0:T(8,128)(2,1)}, u32[]{:S(2)}) copy-start(bf16[128,1024]{1,0:T(8,128)(2,1)} %x_ref.1) | copy-start | bytes 786436
  64.8 5.4 %copy-start.1 = (s32[16384]{0:T(1024)S(1)}, s32[16384]{0:T(1024)}, u32[]{:S(2)}) copy-start(s32[16384]{0:T(1024)} %param.11) | copy-start | bytes 196612
  64.8 5.4 %copy-start.4 = (bf16[8,128]{1,0:T(8,128)(2,1)S(1)}, bf16[8,128]{1,0:T(8,128)(2,1)}, u32[]{:S(2)}) copy-start(bf16[8,128]{1,0:T(8,128)(2,1)} %s_ref.3) | copy-start | bytes 6148
  64.8 5.4 %collective-permute-start.21 = (bf16[64,1024]{1,0:T(8,128)(2,1)S(1)}, bf16[64,1024]{1,0:T(8,128)(2,1)S(1)}, u32[]{:S(2)}, u32[]{:S(2)}) collective-permute-start(bf16[64,1024]{1,0:T(8,128)(2,1)S(1)} %add_convert_fusion.2), channel_id=1, source_target_pairs={{0,4},{1,5},{2,6},{3,7},{4,0},{5,1},{6,2},{7,3},{8,12},{9,13},{10,... | collective-permute-start | bytes 393224 | tf_op jit(solution)/shard_map/ppermute | solution.py:381

commit v4 on v2

--- a/solution.py
+++ b/solution.py
@@ -424,6 +424,7 @@
 
     _, w_query_now = together((u, w_query))
     wq_other = swap(w_query_now, CORE)
+    far = swap(u, FAR)
     kv = call(
         keyval_kernel,
         jax.ShapeDtypeStruct((2, 2, KVH // 2, tokens, HD), bf16),
@@ -434,13 +435,12 @@
     )
     kv = plus(kv[1], swap(kv[0], CORE))
     kv_across = swap(kv[1], ACROSS)
-    far = swap(u, FAR)
     across = swap(u, ACROSS)
     near = swap(u, NEAR)
     w_out_now = w_out
-    done = after(after(across, near, micros=10), far, micros=30)
-    near, kv_across, across, wq_other, far, w_out_now, done = together(
-        (near, kv_across, across, wq_other, far, w_out_now, done)
+    done = after(after(far, across, near, micros=30), micros=10)
+    across, wq_other, near, done, far, w_out_now, kv_across = together(
+        (across, wq_other, near, done, far, w_out_now, kv_across)
     )
     chunk = {0: u, 2: across, 4: near, 8: far}
     kv = plus(kv[0], kv_across)
@@ -456,15 +456,15 @@
             pltpu.VMEM(gain2.shape, f32),
             dma((2 * len(early),)),
         ],
-        micros=10,
+        micros=20,
     )
     wo_other = swap(w_out_now, CORE)
     chunk[12] = swap(chunk[8], NEAR)
     chunk[10] = swap(chunk[8], ACROSS)
-    pay, kv = together((pay, kv))
+    kv, pay = together((kv, pay))
     alike = [[4 * z + low for z in range(count // 4)] for low in range(4)]
     kv = lax.all_to_all(kv, "tensor", 0, 0, axis_index_groups=alike, tiled=True)
-    done = after(chunk[12], chunk[10])
+    done = after(after(chunk[12]), chunk[10])
     done, chunk[2], chunk[12], chunk[10], pay, _ = together((done, chunk[2], chunk[12], chunk[10], pay, w_out_now))
 
     chunk[14] = swap(chunk[12], ACROSS)

time: 71.4 us -> 71.3 us (level)
  starting transfers between devices: 32.8 us -> 31.8 us
  waiting for transfers between devices: 21 us -> 21.9 us
    ppermute x26, starting transfers between devices: 29.3 us -> 28.2 us  [swap(): return lax.ppermute(value, 'tensor', [(i, i ^ rel) for i in range(count)])]
    pallas_call x15 -> x16, Pallas kernels: 14.5 us -> 14.5 us  [call(): pl.pallas_call(kernel, out_shape=outs, in_specs=specs, out_specs=(VMEM,)...]
  transfers between devices with their start and end apart: 27 -> 27, of which waited for: 15 -> 18; matrix products, arithmetic and copies ran while one was open for 3% -> 3% of each run, Pallas kernels for 14% -> 14%
where the time goes in v4:
time: 71.3 us; the launch traced here: 71 us
  starting transfers between devices  31.8 us (45%)
  waiting for transfers between devices  21.9 us (31%)
  Pallas kernels  14.5 us (20%)
  other arithmetic  1.51 us (2%)
  between operations  0.89 us (1%)
    ppermute x26, starting transfers between devices, swap(): return lax.ppermute(value, 'tensor', [(i, i ^ rel) for i in range(count)])  28.2 us
    ppermute x26, waiting for transfers between devices, swap(): return lax.ppermute(value, 'tensor', [(i, i ^ rel) for i in range(count)])  20.4 us
    pallas_call x16, Pallas kernels, call(): pl.pallas_call(kernel, out_shape=outs, in_specs=specs, out_specs=(VMEM,)...  14.5 us
    all_to_all x1, starting transfers between devices, paired(): kv = lax.all_to_all(kv, 'tensor', 0, 0, axis_index_groups=alike, tiled=True)  3.61 us
    all_to_all x1, waiting for transfers between devices, paired(): kv = lax.all_to_all(kv, 'tensor', 0, 0, axis_index_groups=alike, tiled=True)  1.56 us
  transfers between devices with their start and end apart: 27, of which 18 were waited for; matrix products, arithmetic and copies ran while one was open for 3% of the time, Pallas kernels for 14%

profile of v4, /device:TPU:0, one launch (start us, length us, event | category | flops | bytes accessed | tf_op | source)
XLA Modules:
  0.0 71.0 jit_solution(3986724903892294316)
XLA Ops:
  0.6 1.3 %shard_map.104.u_ref.refs_0_ = bf16[128,1024]{1,0:T(8,128)(2,1)S(1)} custom-call(s32[1]{0:T(128)} %bitcast.me, bf16[128,1024]{1,0:T(8,128)(2,1)} %x_ref.1, bf16[8,128]{1,0:T(8,128)(2,1)} %s_ref.1, s32[128,128]{1,0:T(8,128)} %bitcast.17, bf16[128,128]{1,0:T(8,128)(2,1)} %bitcast.19), custom_call_target="tpu_custom_call" | custom-call | flops 1000000000 | bytes 1000000 | tf_op jit(solution)/shard_map/pallas_call | solution.py:159
  1.9 0.0 copy-start.4
  1.9 4.1 %collective-permute-start.4 = (bf16[128,1024]{1,0:T(8,128)(2,1)S(1)}, bf16[128,1024]{1,0:T(8,128)(2,1)S(1)}, u32[]{:S(2)}, u32[]{:S(2)}) collective-permute-start(bf16[128,1024]{1,0:T(8,128)(2,1)S(1)} %shard_map.104.u_ref.refs_0_), channel_id=1, source_target_pairs={{0,8},{1,9},{2,10},{3,11},{4,12},{5,13},{6,14},{7,15},{8,0},{9,1},... | collective-permute-start | bytes 786440 | tf_op jit(solution)/shard_map/ppermute | solution.py:382
  6.0 1.6 %collective-permute-start.3 = (bf16[128,1024]{1,0:T(8,128)(2,1)S(1)}, bf16[128,1024]{1,0:T(8,128)(2,1)S(1)}, u32[]{:S(2)}, u32[]{:S(2)}) collective-permute-start(bf16[128,1024]{1,0:T(8,128)(2,1)S(1)} %shard_map.104.u_ref.refs_0_), channel_id=1, source_target_pairs={{0,4},{1,5},{2,6},{3,7},{4,0},{5,1},{6,2},{7,3},{8,12},{9,13},{10,... | collective-permute-start | bytes 786440 | tf_op jit(solution)/shard_map/ppermute | solution.py:382
  7.6 1.5 %collective-permute-start.1 = (bf16[128,1024]{1,0:T(8,128)(2,1)S(1)}, bf16[128,1024]{1,0:T(8,128)(2,1)S(1)}, u32[]{:S(2)}, u32[]{:S(2)}) collective-permute-start(bf16[128,1024]{1,0:T(8,128)(2,1)S(1)} %shard_map.104.u_ref.refs_0_), channel_id=1, source_target_pairs={{0,2},{1,3},{2,0},{3,1},{4,6},{5,7},{6,4},{7,5},{8,10},{9,11},{10,... | collective-permute-start | bytes 786440 | tf_op jit(solution)/shard_map/ppermute | solution.py:382
  9.1 2.7 %shard_map.105 = bf16[2,2,4,128,128]{4,3,2,1,0:T(8,128)(2,1)S(1)} custom-call(s32[1]{0:T(128)} %bitcast.me, bf16[128,1024]{1,0:T(8,128)(2,1)S(1)} %shard_map.104.u_ref.refs_0_, bf16[1024,1024]{1,0:T(8,128)(2,1)} %wk_hbm.1, bf16[1024,1024]{1,0:T(8,128)(2,1)} %wv_hbm.1), custom_call_target="tpu_custom_call" | custom-call | flops 20000000000 | bytes 1000000 | tf_op jit(solution)/shard_map/pallas_call | solution.py:159
  11.8 0.1 collective-permute-start
  11.9 0.5 collective-permute-start.2
  12.4 0.1 iota_add_fusion
  12.5 0.1 add.73.row_ref
  12.6 0.1 add.83.col_ref
  12.7 0.1 convert_element_type.94
  12.8 0.3 fusion.2
  13.1 0.1 pad_maximum_fusion
  13.2 0.2 collective-permute-done
  13.4 0.1 fusion
  13.5 0.6 collective-permute-start.5
  14.1 3.9 %collective-permute-done.4.refs_0_ = bf16[128,1024]{1,0:T(8,128)(2,1)S(1)} collective-permute-done((bf16[128,1024]{1,0:T(8,128)(2,1)S(1)}, bf16[128,1024]{1,0:T(8,128)(2,1)S(1)}, u32[]{:S(2)}, u32[]{:S(2)}) %collective-permute-start.4) | collective-permute-done | bytes 262176 | tf_op jit(solution)/shard_map/ppermute | solution.py:382
  18.1 0.2 collective-permute-done.3.refs_2_
  18.3 0.9 %collective-permute-done.5 = bf16[4,128,128]{2,1,0:T(8,128)(2,1)S(1)} collective-permute-done((bf16[4,128,128]{2,1,0:T(8,128)(2,1)S(1)}, bf16[4,128,128]{2,1,0:T(8,128)(2,1)S(1)}, u32[]{:S(2)}, u32[]{:S(2)}) %collective-permute-start.5) | collective-permute-done | bytes 131104 | tf_op jit(solution)/shard_map/ppermute | solution.py:382
  19.1 0.6 collective-permute-done.2.x_hbm
  19.8 0.5 collective-permute-start.7
  20.3 1.0 %collective-permute-start.6 = (bf16[128,1024]{1,0:T(8,128)(2,1)S(1)}, bf16[128,1024]{1,0:T(8,128)(2,1)S(1)}, u32[]{:S(2)}, u32[]{:S(2)}) collective-permute-start(bf16[128,1024]{1,0:T(8,128)(2,1)S(1)} %collective-permute-done.4.refs_0_), channel_id=1, source_target_pairs={{0,4},{1,5},{2,6},{3,7},{4,0},{5,1},{6,2},{7,3},{8,12},{9,13},{10,... | collective-permute-start | bytes 786440 | tf_op jit(solution)/shard_map/ppermute | solution.py:382
  21.3 1.9 %shard_map.108.before_ref = f32[128,384]{1,0:T(8,128)S(1)} custom-call(s32[1]{0:T(128)} %bitcast.me, f32[8,128]{1,0:T(8,128)S(1)} %shard_map.107.token, bf16[128,128]{1,0:T(8,128)(2,1)S(1)} %bitcast.20, bf16[16384,128]{1,0:T(8,128)(2,1)} %w_hbm.5, bf16[16384,128]{1,0:T(8,128)(2,1)} %collective-permute-done.2.x_hbm, ...), custom_call_target="tpu_custom_call" | custom-call | flops 20000000000 | bytes 1000000 | tf_op jit(solution)/shard_map/pallas_call | solution.py:159
  23.2 0.7 fusion.1
  23.9 3.6 %all-to-all-start = ((bf16[4,128,128]{2,1,0:T(8,128)(2,1)}), bf16[4,128,128]{2,1,0:T(8,128)(2,1)S(1)}, u32[]{:S(2)}, u32[]{:S(2)}) async-start(bf16[4,128,128]{2,1,0:T(8,128)(2,1)} %fusion.1), calls=%async_computation | async-start | bytes 262144 | tf_op jit(solution)/shard_map/all_to_all | solution.py:466
  27.5 0.8 %collective-permute-done.6.refs_0_.refs_2_ = bf16[128,1024]{1,0:T(8,128)(2,1)S(1)} collective-permute-done((bf16[128,1024]{1,0:T(8,128)(2,1)S(1)}, bf16[128,1024]{1,0:T(8,128)(2,1)S(1)}, u32[]{:S(2)}, u32[]{:S(2)}) %collective-permute-start.6) | collective-permute-done | bytes 262176 | tf_op jit(solution)/shard_map/ppermute | solution.py:382
  28.4 1.3 %collective-permute-start.10 = (bf16[128,1024]{1,0:T(8,128)(2,1)S(1)}, bf16[128,1024]{1,0:T(8,128)(2,1)S(1)}, u32[]{:S(2)}, u32[]{:S(2)}) collective-permute-start(bf16[128,1024]{1,0:T(8,128)(2,1)S(1)} %collective-permute-done.1.refs_1_), channel_id=1, source_target_pairs={{0,4},{1,5},{2,6},{3,7},{4,0},{5,1},{6,2},{7,3},{8,12},{9,13},{10,... | collective-permute-start | bytes 786440 | tf_op jit(solution)/shard_map/ppermute | solution.py:382
  29.7 0.8 %collective-permute-start.9 = (bf16[128,1024]{1,0:T(8,128)(2,1)S(1)}, bf16[128,1024]{1,0:T(8,128)(2,1)S(1)}, u32[]{:S(2)}, u32[]{:S(2)}) collective-permute-start(bf16[128,1024]{1,0:T(8,128)(2,1)S(1)} %collective-permute-done.6.refs_0_.refs_2_), channel_id=1, source_target_pairs={{0,2},{1,3},{2,0},{3,1},{4,6},{5,7},{6,4},{7,5},{8,10},{9,11},{10,... | collective-permute-start | bytes 786440 | tf_op jit(solution)/shard_map/ppermute | solution.py:382
  30.4 1.8 %shard_map.111 = (f32[128,384]{1,0:T(8,128)S(1)}, bf16[2,1024,256]{2,1,0:T(8,128)(2,1)S(1)}) custom-call(s32[1]{0:T(128)} %bitcast.me, f32[8,128]{1,0:T(8,128)S(1)} %shard_map.110.done, bf16[128,128]{1,0:T(8,128)(2,1)S(1)} %bitcast.21, bf16[16384,128]{1,0:T(8,128)(2,1)} %w_hbm.5, bf16[16384,128]{1,0:T(8,128)(2,1)} %collective-permute-done.2.x_hbm, ...), custom_call_target="tpu_custom_call" | custom-call | flops 20000000000 | bytes 1000000 | tf_op jit(solution)/shard_map/pallas_call | solution.py:159
  32.2 1.6 %all-to-all-done = bf16[4,128,128]{2,1,0:T(8,128)(2,1)S(1)} async-done(((bf16[4,128,128]{2,1,0:T(8,128)(2,1)}), bf16[4,128,128]{2,1,0:T(8,128)(2,1)S(1)}, u32[]{:S(2)}, u32[]{:S(2)}) %all-to-all-start) | async-done | bytes 131104 | tf_op jit(solution)/shard_map/all_to_all | solution.py:466
  33.8 0.1 collective-permute-start.8
  33.9 4.2 %collective-permute-done.10.refs_1_.refs_0_ = bf16[128,1024]{1,0:T(8,128)(2,1)S(1)} collective-permute-done((bf16[128,1024]{1,0:T(8,128)(2,1)S(1)}, bf16[128,1024]{1,0:T(8,128)(2,1)S(1)}, u32[]{:S(2)}, u32[]{:S(2)}) %collective-permute-start.10) | collective-permute-done | bytes 262176 | tf_op jit(solution)/shard_map/ppermute | solution.py:382
  38.1 0.3 shard_map.115.pay_ref
  38.5 0.1 collective-permute-start.11
  38.6 1.4 %collective-permute-done.11.got_ref = f32[128,384]{1,0:T(8,128)S(1)} collective-permute-done((f32[128,384]{1,0:T(8,128)S(1)}, f32[128,384]{1,0:T(8,128)S(1)}, u32[]{:S(2)}, u32[]{:S(2)}) %collective-permute-start.11) | collective-permute-done | bytes 196640 | tf_op jit(solution)/shard_map/ppermute | solution.py:382
  40.0 1.8 %shard_map.116 = (bf16[128,256]{1,0:T(8,128)(2,1)S(1)}, bf16[64,1024]{1,0:T(8,128)(2,1)S(1)}, bf16[64,1024]{1,0:T(8,128)(2,1)S(1)}) custom-call(s32[1]{0:T(128)} %bitcast.me, f32[8,128]{1,0:T(8,128)S(1)} %shard_map.112.done, f32[128,384]{1,0:T(8,128)S(1)} %shard_map.115.pay_ref, f32[128,384]{1,0:T(8,128)S(1)} %collective-permute-done.11.got_ref, ...), custom_call_target="tpu_custom_call" | custom-call | flops 1000000000 | bytes 1000000 | tf_op jit(solution)/shard_map/pallas_call | solution.py:159
  41.8 0.9 %collective-permute-start.13 = (bf16[64,1024]{1,0:T(8,128)(2,1)S(1)}, bf16[64,1024]{1,0:T(8,128)(2,1)S(1)}, u32[]{:S(2)}, u32[]{:S(2)}) collective-permute-start(bf16[64,1024]{1,0:T(8,128)(2,1)S(1)} %get-tuple-element.68), channel_id=1, source_target_pairs={{0,2},{1,3},{2,0},{3,1},{4,6},{5,7},{6,4},{7,5},{8,10},{9,11},{10,... | collective-permute-start | bytes 393224 | tf_op jit(solution)/shard_map/ppermute | solution.py:382
  42.7 1.2 %collective-permute-start.22 = (bf16[64,1024]{1,0:T(8,128)(2,1)S(1)}, bf16[64,1024]{1,0:T(8,128)(2,1)S(1)}, u32[]{:S(2)}, u32[]{:S(2)}) collective-permute-start(bf16[64,1024]{1,0:T(8,128)(2,1)S(1)} %get-tuple-element.85), channel_id=1, source_target_pairs={{0,2},{1,3},{2,0},{3,1},{4,6},{5,7},{6,4},{7,5},{8,10},{9,11},{10,... | collective-permute-start | bytes 393224 | tf_op jit(solution)/shard_map/ppermute | solution.py:382
  43.9 3.2 %shard_map.117 = (bf16[64,1024]{1,0:T(8,128)(2,1)S(1)}, bf16[64,1024]{1,0:T(8,128)(2,1)S(1)}, bf16[64,1024]{1,0:T(8,128)(2,1)S(1)}, bf16[64,1024]{1,0:T(8,128)(2...) custom-call(s32[1]{0:T(128)} %bitcast.me, ...), custom_call_target="tpu_custom_call" | custom-call | flops 20000000000 | bytes 1000000 | tf_op jit(solution)/shard_map/pallas_call | solution.py:159
  47.1 1.1 %collective-permute-done.13 = bf16[64,1024]{1,0:T(8,128)(2,1)S(1)} collective-permute-done((bf16[64,1024]{1,0:T(8,128)(2,1)S(1)}, bf16[64,1024]{1,0:T(8,128)(2,1)S(1)}, u32[]{:S(2)}, u32[]{:S(2)}) %collective-permute-start.13) | collective-permute-done | bytes 131104 | tf_op jit(solution)/shard_map/ppermute | solution.py:382
  48.2 0.4 collective-permute-start.14
  48.6 0.6 collective-permute-start.15
  49.2 1.4 %collective-permute-start.17 = (bf16[64,1024]{1,0:T(8,128)(2,1)S(1)}, bf16[64,1024]{1,0:T(8,128)(2,1)S(1)}, u32[]{:S(2)}, u32[]{:S(2)}) collective-permute-start(bf16[64,1024]{1,0:T(8,128)(2,1)S(1)} %get-tuple-element.78), channel_id=1, source_target_pairs={{0,2},{1,3},{2,0},{3,1},{4,6},{5,7},{6,4},{7,5},{8,10},{9,11},{10,... | collective-permute-start | bytes 393224 | tf_op jit(solution)/shard_map/ppermute | solution.py:382
  50.6 0.2 collective-permute-done.22
  50.9 0.9 %collective-permute-start.23 = (bf16[64,1024]{1,0:T(8,128)(2,1)S(1)}, bf16[64,1024]{1,0:T(8,128)(2,1)S(1)}, u32[]{:S(2)}, u32[]{:S(2)}) collective-permute-start(bf16[64,1024]{1,0:T(8,128)(2,1)S(1)} %get-tuple-element.87), channel_id=1, source_target_pairs={{0,2},{1,3},{2,0},{3,1},{4,6},{5,7},{6,4},{7,5},{8,10},{9,11},{10,... | collective-permute-start | bytes 393224 | tf_op jit(solution)/shard_map/ppermute | solution.py:382
  51.8 1.6 %collective-permute-start.24 = (bf16[64,1024]{1,0:T(8,128)(2,1)S(1)}, bf16[64,1024]{1,0:T(8,128)(2,1)S(1)}, u32[]{:S(2)}, u32[]{:S(2)}) collective-permute-start(bf16[64,1024]{1,0:T(8,128)(2,1)S(1)} %add_convert_fusion.1), channel_id=1, source_target_pairs={{0,4},{1,5},{2,6},{3,7},{4,0},{5,1},{6,2},{7,3},{8,12},{9,13},{10,... | collective-permute-start | bytes 393224 | tf_op jit(solution)/shard_map/ppermute | solution.py:382
  53.3 0.4 collective-permute-done.14
  53.7 1.3 %collective-permute-done.15 = bf16[64,1024]{1,0:T(8,128)(2,1)S(1)} collective-permute-done((bf16[64,1024]{1,0:T(8,128)(2,1)S(1)}, bf16[64,1024]{1,0:T(8,128)(2,1)S(1)}, u32[]{:S(2)}, u32[]{:S(2)}) %collective-permute-start.15) | collective-permute-done | bytes 131104 | tf_op jit(solution)/shard_map/ppermute | solution.py:382
  55.0 0.1 add_convert_fusion.4
  55.1 2.7 %collective-permute-start.16 = (bf16[64,1024]{1,0:T(8,128)(2,1)S(1)}, bf16[64,1024]{1,0:T(8,128)(2,1)S(1)}, u32[]{:S(2)}, u32[]{:S(2)}) collective-permute-start(bf16[64,1024]{1,0:T(8,128)(2,1)S(1)} %add_convert_fusion.4), channel_id=1, source_target_pairs={{0,8},{1,9},{2,10},{3,11},{4,12},{5,13},{6,14},{7,15},{8,0},{9,1},... | collective-permute-start | bytes 393224 | tf_op jit(solution)/shard_map/ppermute | solution.py:382
  57.8 0.7 collective-permute-start.20
  58.5 1.5 %collective-permute-start.19 = (bf16[64,1024]{1,0:T(8,128)(2,1)S(1)}, bf16[64,1024]{1,0:T(8,128)(2,1)S(1)}, u32[]{:S(2)}, u32[]{:S(2)}) collective-permute-start(bf16[64,1024]{1,0:T(8,128)(2,1)S(1)} %add_convert_fusion.3), channel_id=1, source_target_pairs={{0,4},{1,5},{2,6},{3,7},{4,0},{5,1},{6,2},{7,3},{8,12},{9,13},{10,... | collective-permute-start | bytes 393224 | tf_op jit(solution)/shard_map/ppermute | solution.py:382
  59.9 0.1 collective-permute-done.23
  60.0 0.1 add_convert_fusion
  60.1 2.6 %collective-permute-start.25 = (bf16[64,1024]{1,0:T(8,128)(2,1)S(1)}, bf16[64,1024]{1,0:T(8,128)(2,1)S(1)}, u32[]{:S(2)}, u32[]{:S(2)}) collective-permute-start(bf16[64,1024]{1,0:T(8,128)(2,1)S(1)} %add_convert_fusion), channel_id=1, source_target_pairs={{0,8},{1,9},{2,10},{3,11},{4,12},{5,13},{6,14},{7,15},{8,0},{9,1},... | collective-permute-start | bytes 393224 | tf_op jit(solution)/shard_map/ppermute | solution.py:382
  62.7 0.4 collective-permute-start.18
  63.1 1.0 %collective-permute-done.20 = bf16[64,1024]{1,0:T(8,128)(2,1)S(1)} collective-permute-done((bf16[64,1024]{1,0:T(8,128)(2,1)S(1)}, bf16[64,1024]{1,0:T(8,128)(2,1)S(1)}, u32[]{:S(2)}, u32[]{:S(2)}) %collective-permute-start.20) | collective-permute-done | bytes 131104 | tf_op jit(solution)/shard_map/ppermute | solution.py:382
  64.2 0.0 copy-start.3
  64.2 1.5 %collective-permute-start.21 = (bf16[64,1024]{1,0:T(8,128)(2,1)S(1)}, bf16[64,1024]{1,0:T(8,128)(2,1)S(1)}, u32[]{:S(2)}, u32[]{:S(2)}) collective-permute-start(bf16[64,1024]{1,0:T(8,128)(2,1)S(1)} %add_convert_fusion.2), channel_id=1, source_target_pairs={{0,4},{1,5},{2,6},{3,7},{4,0},{5,1},{6,2},{7,3},{8,12},{9,13},{10,... | collective-permute-start | bytes 393224 | tf_op jit(solution)/shard_map/ppermute | solution.py:382
  65.7 1.9 %collective-permute-done.19.refs_2_ = bf16[64,1024]{1,0:T(8,128)(2,1)S(1)} collective-permute-done((bf16[64,1024]{1,0:T(8,128)(2,1)S(1)}, bf16[64,1024]{1,0:T(8,128)(2,1)S(1)}, u32[]{:S(2)}, u32[]{:S(2)}) %collective-permute-start.19) | collective-permute-done | bytes 131104 | tf_op jit(solution)/shard_map/ppermute | solution.py:382
  67.6 0.6 collective-permute-done.25.refs_4_
  68.2 1.3 %collective-permute-done.21.refs_3_ = bf16[64,1024]{1,0:T(8,128)(2,1)S(1)} collective-permute-done((bf16[64,1024]{1,0:T(8,128)(2,1)S(1)}, bf16[64,1024]{1,0:T(8,128)(2,1)S(1)}, u32[]{:S(2)}, u32[]{:S(2)}) %collective-permute-start.21) | collective-permute-done | bytes 131104 | tf_op jit(solution)/shard_map/ppermute | solution.py:382
  69.5 1.5 %shard_map.119 = (bf16[128,1024]{1,0:T(8,128)(2,1)}, bf16[8,128]{1,0:T(8,128)(2,1)}) custom-call(s32[1]{0:T(128)} %bitcast.me, f32[8,128]{1,0:T(8,128)S(1)} %shard_map.118.done, bf16[128,1024]{1,0:T(8,128)(2,1)S(1)} %copy-done, bf16[8,128]{1,0:T(8,128)(2,1)S(1)} %copy-done.3, s32[128,128]{1,0:T(8,128)S(1)} %bitcast.18, ...), custom_call_target="tpu_custom_call" | custom-call | flops 1000000000 | bytes 1000000 | tf_op jit(solution)/shard_map/pallas_call | solution.py:159
  (35 shorter events, 0.2 us)
Async XLA Ops:
  1.9 10.5 %copy-start.4 = (s32[16]{0:T(128)S(1)}, s32[16]{0:T(128)}, u32[]{:S(2)}) copy-start(s32[16]{0:T(128)} %param.12) | copy-start | bytes 196
  1.9 16.1 %collective-permute-start.4 = (bf16[128,1024]{1,0:T(8,128)(2,1)S(1)}, bf16[128,1024]{1,0:T(8,128)(2,1)S(1)}, u32[]{:S(2)}, u32[]{:S(2)}) collective-permute-start(bf16[128,1024]{1,0:T(8,128)(2,1)S(1)} %shard_map.104.u_ref.refs_0_), channel_id=1, source_target_pairs={{0,8},{1,9},{2,10},{3,11},{4,12},{5,13},{6,14},{7,15},{8,0},{9,1},... | collective-permute-start | bytes 786440 | tf_op jit(solution)/shard_map/ppermute | solution.py:382
  6.0 12.2 %collective-permute-start.3 = (bf16[128,1024]{1,0:T(8,128)(2,1)S(1)}, bf16[128,1024]{1,0:T(8,128)(2,1)S(1)}, u32[]{:S(2)}, u32[]{:S(2)}) collective-permute-start(bf16[128,1024]{1,0:T(8,128)(2,1)S(1)} %shard_map.104.u_ref.refs_0_), channel_id=1, source_target_pairs={{0,4},{1,5},{2,6},{3,7},{4,0},{5,1},{6,2},{7,3},{8,12},{9,13},{10,... | collective-permute-start | bytes 786440 | tf_op jit(solution)/shard_map/ppermute | solution.py:382
  7.6 10.7 %collective-permute-start.1 = (bf16[128,1024]{1,0:T(8,128)(2,1)S(1)}, bf16[128,1024]{1,0:T(8,128)(2,1)S(1)}, u32[]{:S(2)}, u32[]{:S(2)}) collective-permute-start(bf16[128,1024]{1,0:T(8,128)(2,1)S(1)} %shard_map.104.u_ref.refs_0_), channel_id=1, source_target_pairs={{0,2},{1,3},{2,0},{3,1},{4,6},{5,7},{6,4},{7,5},{8,10},{9,11},{10,... | collective-permute-start | bytes 786440 | tf_op jit(solution)/shard_map/ppermute | solution.py:382
  11.8 1.6 %collective-permute-start = (bf16[2,4,128,128]{3,2,1,0:T(8,128)(2,1)S(1)}, bf16[2,4,128,128]{3,2,1,0:T(8,128)(2,1)S(1)}, u32[]{:S(2)}, u32[]{:S(2)}) collective-permute-start(bf16[2,4,128,128]{3,2,1,0:T(8,128)(2,1)S(1)} %slice_bitcast_fusion), channel_id=1, source_target_pairs={{0,1},{1,0},{2,3},{3,2},{4,5},{5,4},{6,7},{7,6},{8,9},{9,8},{10,11... | collective-permute-start | bytes 786440 | tf_op jit(solution)/shard_map/ppermute | solution.py:382
  11.9 7.9 %collective-permute-start.2 = (bf16[16384,128]{1,0:T(8,128)(2,1)}, bf16[16384,128]{1,0:T(8,128)(2,1)}, u32[]{:S(2)}, u32[]{:S(2)}) collective-permute-start(bf16[16384,128]{1,0:T(8,128)(2,1)} %w_hbm.5), channel_id=1, source_target_pairs={{0,1},{1,0},{2,3},{3,2},{4,5},{5,4},{6,7},{7,6},{8,9},{9,8},{10,11... | collective-permute-start | bytes 12582920 | tf_op jit(solution)/shard_map/ppermute | solution.py:382
  13.5 5.6 %collective-permute-start.5 = (bf16[4,128,128]{2,1,0:T(8,128)(2,1)S(1)}, bf16[4,128,128]{2,1,0:T(8,128)(2,1)S(1)}, u32[]{:S(2)}, u32[]{:S(2)}) collective-permute-start(bf16[4,128,128]{2,1,0:T(8,128)(2,1)S(1)} %slice_bitcast_fusion.2), channel_id=1, source_target_pairs={{0,2},{1,3},{2,0},{3,1},{4,6},{5,7},{6,4},{7,5},{8,10},{9,11},{10,... | collective-permute-start | bytes 393224 | tf_op jit(solution)/shard_map/ppermute | solution.py:382
  18.3 3.1 %copy-start.2 = (bf16[16384]{0:T(1024)(128)(2,1)S(1)}, bf16[16384]{0:T(1024)(128)(2,1)}, u32[]{:S(2)}) copy-start(bf16[16384]{0:T(1024)(128)(2,1)} %param.13) | copy-start | bytes 98308
  19.8 8.6 %collective-permute-start.7 = (bf16[128,1024]{1,0:T(8,128)(2,1)S(1)}, bf16[128,1024]{1,0:T(8,128)(2,1)S(1)}, u32[]{:S(2)}, u32[]{:S(2)}) collective-permute-start(bf16[128,1024]{1,0:T(8,128)(2,1)S(1)} %collective-permute-done.4.refs_0_), channel_id=1, source_target_pairs={{0,2},{1,3},{2,0},{3,1},{4,6},{5,7},{6,4},{7,5},{8,10},{9,11},{10,... | collective-permute-start | bytes 786440 | tf_op jit(solution)/shard_map/ppermute | solution.py:382
  20.3 8.1 %collective-permute-start.6 = (bf16[128,1024]{1,0:T(8,128)(2,1)S(1)}, bf16[128,1024]{1,0:T(8,128)(2,1)S(1)}, u32[]{:S(2)}, u32[]{:S(2)}) collective-permute-start(bf16[128,1024]{1,0:T(8,128)(2,1)S(1)} %collective-permute-done.4.refs_0_), channel_id=1, source_target_pairs={{0,4},{1,5},{2,6},{3,7},{4,0},{5,1},{6,2},{7,3},{8,12},{9,13},{10,... | collective-permute-start | bytes 786440 | tf_op jit(solution)/shard_map/ppermute | solution.py:382
  23.9 9.9 %all-to-all-start = ((bf16[4,128,128]{2,1,0:T(8,128)(2,1)}), bf16[4,128,128]{2,1,0:T(8,128)(2,1)S(1)}, u32[]{:S(2)}, u32[]{:S(2)}) async-start(bf16[4,128,128]{2,1,0:T(8,128)(2,1)} %fusion.1), calls=%async_computation | async-start | bytes 262144 | tf_op jit(solution)/shard_map/all_to_all | solution.py:466
  27.5 12.5 %collective-permute-start.12 = (bf16[128,16384]{1,0:T(8,128)(2,1)}, bf16[128,16384]{1,0:T(8,128)(2,1)}, u32[]{:S(2)}, u32[]{:S(2)}) collective-permute-start(bf16[128,16384]{1,0:T(8,128)(2,1)} %w_hbm.7), channel_id=1, source_target_pairs={{0,1},{1,0},{2,3},{3,2},{4,5},{5,4},{6,7},{7,6},{8,9},{9,8},{10,11... | collective-permute-start | bytes 12582920 | tf_op jit(solution)/shard_map/ppermute | solution.py:382
  28.4 9.7 %collective-permute-start.10 = (bf16[128,1024]{1,0:T(8,128)(2,1)S(1)}, bf16[128,1024]{1,0:T(8,128)(2,1)S(1)}, u32[]{:S(2)}, u32[]{:S(2)}) collective-permute-start(bf16[128,1024]{1,0:T(8,128)(2,1)S(1)} %collective-permute-done.1.refs_1_), channel_id=1, source_target_pairs={{0,4},{1,5},{2,6},{3,7},{4,0},{5,1},{6,2},{7,3},{8,12},{9,13},{10,... | collective-permute-start | bytes 786440 | tf_op jit(solution)/shard_map/ppermute | solution.py:382
  29.7 8.5 %collective-permute-start.9 = (bf16[128,1024]{1,0:T(8,128)(2,1)S(1)}, bf16[128,1024]{1,0:T(8,128)(2,1)S(1)}, u32[]{:S(2)}, u32[]{:S(2)}) collective-permute-start(bf16[128,1024]{1,0:T(8,128)(2,1)S(1)} %collective-permute-done.6.refs_0_.refs_2_), channel_id=1, source_target_pairs={{0,2},{1,3},{2,0},{3,1},{4,6},{5,7},{6,4},{7,5},{8,10},{9,11},{10,... | collective-permute-start | bytes 786440 | tf_op jit(solution)/shard_map/ppermute | solution.py:382
  33.8 4.7 %collective-permute-start.8 = (bf16[128,128]{1,0:T(8,128)(2,1)S(1)}, bf16[128,128]{1,0:T(8,128)(2,1)S(1)}, u32[]{:S(2)}, u32[]{:S(2)}) collective-permute-start(bf16[128,128]{1,0:T(8,128)(2,1)S(1)} %reduce_sum.12.kv_ref), channel_id=1, source_target_pairs={{0,1},{1,0},{2,3},{3,2},{4,5},{5,4},{6,7},{7,6},{8,9},{9,8},{10,11... | collective-permute-start | bytes 98312 | tf_op jit(solution)/shard_map/ppermute | solution.py:382
  38.5 1.5 %collective-permute-start.11 = (f32[128,384]{1,0:T(8,128)S(1)}, f32[128,384]{1,0:T(8,128)S(1)}, u32[]{:S(2)}, u32[]{:S(2)}) collective-permute-start(f32[128,384]{1,0:T(8,128)S(1)} %shard_map.115.pay_ref), channel_id=1, source_target_pairs={{0,1},{1,0},{2,3},{3,2},{4,5},{5,4},{6,7},{7,6},{8,9},{9,8},{10,11... | collective-permute-start | bytes 589832 | tf_op jit(solution)/shard_map/ppermute | solution.py:382
  41.8 6.4 %collective-permute-start.13 = (bf16[64,1024]{1,0:T(8,128)(2,1)S(1)}, bf16[64,1024]{1,0:T(8,128)(2,1)S(1)}, u32[]{:S(2)}, u32[]{:S(2)}) collective-permute-start(bf16[64,1024]{1,0:T(8,128)(2,1)S(1)} %get-tuple-element.68), channel_id=1, source_target_pairs={{0,2},{1,3},{2,0},{3,1},{4,6},{5,7},{6,4},{7,5},{8,10},{9,11},{10,... | collective-permute-start | bytes 393224 | tf_op jit(solution)/shard_map/ppermute | solution.py:382
  42.7 8.1 %collective-permute-start.22 = (bf16[64,1024]{1,0:T(8,128)(2,1)S(1)}, bf16[64,1024]{1,0:T(8,128)(2,1)S(1)}, u32[]{:S(2)}, u32[]{:S(2)}) collective-permute-start(bf16[64,1024]{1,0:T(8,128)(2,1)S(1)} %get-tuple-element.85), channel_id=1, source_target_pairs={{0,2},{1,3},{2,0},{3,1},{4,6},{5,7},{6,4},{7,5},{8,10},{9,11},{10,... | collective-permute-start | bytes 393224 | tf_op jit(solution)/shard_map/ppermute | solution.py:382
  48.2 5.5 %collective-permute-start.14 = (bf16[64,1024]{1,0:T(8,128)(2,1)S(1)}, bf16[64,1024]{1,0:T(8,128)(2,1)S(1)}, u32[]{:S(2)}, u32[]{:S(2)}) collective-permute-start(bf16[64,1024]{1,0:T(8,128)(2,1)S(1)} %add_convert_fusion.5), channel_id=1, source_target_pairs={{0,4},{1,5},{2,6},{3,7},{4,0},{5,1},{6,2},{7,3},{8,12},{9,13},{10,... | collective-permute-start | bytes 393224 | tf_op jit(solution)/shard_map/ppermute | solution.py:382
  48.6 6.4 %collective-permute-start.15 = (bf16[64,1024]{1,0:T(8,128)(2,1)S(1)}, bf16[64,1024]{1,0:T(8,128)(2,1)S(1)}, u32[]{:S(2)}, u32[]{:S(2)}) collective-permute-start(bf16[64,1024]{1,0:T(8,128)(2,1)S(1)} %get-tuple-element.73), channel_id=1, source_target_pairs={{0,2},{1,3},{2,0},{3,1},{4,6},{5,7},{6,4},{7,5},{8,10},{9,11},{10,... | collective-permute-start | bytes 393224 | tf_op jit(solution)/shard_map/ppermute | solution.py:382
  49.2 9.2 %collective-permute-start.17 = (bf16[64,1024]{1,0:T(8,128)(2,1)S(1)}, bf16[64,1024]{1,0:T(8,128)(2,1)S(1)}, u32[]{:S(2)}, u32[]{:S(2)}) collective-permute-start(bf16[64,1024]{1,0:T(8,128)(2,1)S(1)} %get-tuple-element.78), channel_id=1, source_target_pairs={{0,2},{1,3},{2,0},{3,1},{4,6},{5,7},{6,4},{7,5},{8,10},{9,11},{10,... | collective-permute-start | bytes 393224 | tf_op jit(solution)/shard_map/ppermute | solution.py:382
  50.9 9.2 %collective-permute-start.23 = (bf16[64,1024]{1,0:T(8,128)(2,1)S(1)}, bf16[64,1024]{1,0:T(8,128)(2,1)S(1)}, u32[]{:S(2)}, u32[]{:S(2)}) collective-permute-start(bf16[64,1024]{1,0:T(8,128)(2,1)S(1)} %get-tuple-element.87), channel_id=1, source_target_pairs={{0,2},{1,3},{2,0},{3,1},{4,6},{5,7},{6,4},{7,5},{8,10},{9,11},{10,... | collective-permute-start | bytes 393224 | tf_op jit(solution)/shard_map/ppermute | solution.py:382
  51.8 8.3 %collective-permute-start.24 = (bf16[64,1024]{1,0:T(8,128)(2,1)S(1)}, bf16[64,1024]{1,0:T(8,128)(2,1)S(1)}, u32[]{:S(2)}, u32[]{:S(2)}) collective-permute-start(bf16[64,1024]{1,0:T(8,128)(2,1)S(1)} %add_convert_fusion.1), channel_id=1, source_target_pairs={{0,4},{1,5},{2,6},{3,7},{4,0},{5,1},{6,2},{7,3},{8,12},{9,13},{10,... | collective-permute-start | bytes 393224 | tf_op jit(solution)/shard_map/ppermute | solution.py:382
  55.1 10.6 %collective-permute-start.16 = (bf16[64,1024]{1,0:T(8,128)(2,1)S(1)}, bf16[64,1024]{1,0:T(8,128)(2,1)S(1)}, u32[]{:S(2)}, u32[]{:S(2)}) collective-permute-start(bf16[64,1024]{1,0:T(8,128)(2,1)S(1)} %add_convert_fusion.4), channel_id=1, source_target_pairs={{0,8},{1,9},{2,10},{3,11},{4,12},{5,13},{6,14},{7,15},{8,0},{9,1},... | collective-permute-start | bytes 393224 | tf_op jit(solution)/shard_map/ppermute | solution.py:382
  57.8 6.4 %collective-permute-start.20 = (bf16[64,1024]{1,0:T(8,128)(2,1)S(1)}, bf16[64,1024]{1,0:T(8,128)(2,1)S(1)}, u32[]{:S(2)}, u32[]{:S(2)}) collective-permute-start(bf16[64,1024]{1,0:T(8,128)(2,1)S(1)} %get-tuple-element.83), channel_id=1, source_target_pairs={{0,2},{1,3},{2,0},{3,1},{4,6},{5,7},{6,4},{7,5},{8,10},{9,11},{10,... | collective-permute-start | bytes 393224 | tf_op jit(solution)/shard_map/ppermute | solution.py:382
  58.5 9.1 %collective-permute-start.19 = (bf16[64,1024]{1,0:T(8,128)(2,1)S(1)}, bf16[64,1024]{1,0:T(8,128)(2,1)S(1)}, u32[]{:S(2)}, u32[]{:S(2)}) collective-permute-start(bf16[64,1024]{1,0:T(8,128)(2,1)S(1)} %add_convert_fusion.3), channel_id=1, source_target_pairs={{0,4},{1,5},{2,6},{3,7},{4,0},{5,1},{6,2},{7,3},{8,12},{9,13},{10,... | collective-permute-start | bytes 393224 | tf_op jit(solution)/shard_map/ppermute | solution.py:382
  60.1 8.1 %collective-permute-start.25 = (bf16[64,1024]{1,0:T(8,128)(2,1)S(1)}, bf16[64,1024]{1,0:T(8,128)(2,1)S(1)}, u32[]{:S(2)}, u32[]{:S(2)}) collective-permute-start(bf16[64,1024]{1,0:T(8,128)(2,1)S(1)} %add_convert_fusion), channel_id=1, source_target_pairs={{0,8},{1,9},{2,10},{3,11},{4,12},{5,13},{6,14},{7,15},{8,0},{9,1},... | collective-permute-start | bytes 393224 | tf_op jit(solution)/shard_map/ppermute | solution.py:382
  62.7 6.8 %collective-permute-start.18 = (bf16[128,1024]{1,0:T(8,128)(2,1)S(1)}, bf16[128,1024]{1,0:T(8,128)(2,1)S(1)}, u32[]{:S(2)}, u32[]{:S(2)}) collective-permute-start(bf16[128,1024]{1,0:T(8,128)(2,1)S(1)} %get-tuple-element.80), channel_id=1, source_target_pairs={{0,2},{1,3},{2,0},{3,1},{4,6},{5,7},{6,4},{7,5},{8,10},{9,11},{10,... | collective-permute-start | bytes 786440 | tf_op jit(solution)/shard_map/ppermute | solution.py:382
  64.2 5.3 %copy-start = (bf16[128,1024]{1,0:T(8,128)(2,1)S(1)}, bf16[128,1024]{1,0:T(8,128)(2,1)}, u32[]{:S(2)}) copy-start(bf16[128,1024]{1,0:T(8,128)(2,1)} %x_ref.1) | copy-start | bytes 786436
  64.2 5.3 %copy-start.1 = (s32[16384]{0:T(1024)S(1)}, s32[16384]{0:T(1024)}, u32[]{:S(2)}) copy-start(s32[16384]{0:T(1024)} %param.11) | copy-start | bytes 196612
  64.2 5.3 %copy-start.3 = (bf16[8,128]{1,0:T(8,128)(2,1)S(1)}, bf16[8,128]{1,0:T(8,128)(2,1)}, u32[]{:S(2)}) copy-start(bf16[8,128]{1,0:T(8,128)(2,1)} %s_ref.1) | copy-start | bytes 6148
  64.2 5.3 %collective-permute-start.21 = (bf16[64,1024]{1,0:T(8,128)(2,1)S(1)}, bf16[64,1024]{1,0:T(8,128)(2,1)S(1)}, u32[]{:S(2)}, u32[]{:S(2)}) collective-permute-start(bf16[64,1024]{1,0:T(8,128)(2,1)S(1)} %add_convert_fusion.2), channel_id=1, source_target_pairs={{0,4},{1,5},{2,6},{3,7},{4,0},{5,1},{6,2},{7,3},{8,12},{9,13},{10,... | collective-permute-start | bytes 393224 | tf_op jit(solution)/shard_map/ppermute | solution.py:382
